TPU v7x, 256 devices: a whole 4x4x8 slice. The times are simulated.
256 devices in a mesh: tm: 16 (over z_hi, y, core), dp: 16 (over z_lo, x).
Axes of the slice: x: 4, y: 4, z: 8 (z_hi: 2, z_lo: 4; z = z_hi * 4 + z_lo), core: 2. Of those that a mesh axis runs over, the one named last changes fastest.
Arguments:
- tokens: bfloat16 [16, 32, 64, 1152], P('dp', 'tm'), may hold values from -6 to 6
- clip_frames: int32 [16, 4], P('dp'), may hold values from 1 to 16, 32 in all within a row
- teacher_scores: float32 [16, 4, 8], P('dp'), may hold values from -4 to 4
- ln_gain: float32 [1152], replicated, may hold values from 0.25 to 1.75
- w_qkv: bfloat16 [1152, 3456], replicated, may hold values from -1 to 1
- w_out: bfloat16 [1152, 1152], replicated, may hold values from -0.1875 to 0.1875
- out_gain: float32 [1152], replicated, may hold values from 0.25 to 1.75
- reward_head: float32 [1152, 8], replicated, may hold values from -1.8856181 to 1.8856181
Outputs:
- scores: float32 [16, 4, 8], P('dp')
- grad_qkv: float32 [1152, 3456], P('dp')
- grad_out: float32 [1152, 1152], P('dp')
Inputs may be any that keep to these rules, and one draw needn't show every extreme that they name: `clip_frames`: each row lists the lengths of 4 clips laid end to end over its 32 frames; the longest clip of every row has exactly 16 frames.
All inputs are finite; a program needn't handle non-finite values.
Results may differ from a plain program's by a relative error of at most 0.033.
Values may be sent and summed in bfloat16 or wider, within the bound.
No kernel may reach another device: no remote copies, remote signals or barrier semaphores. Data moves between devices by JAX's collectives and lax.ppermute only.
A program may use at most 128 MiB of HBM per device.

v0:
```python
import math

import jax
import jax.numpy as jnp
from jax import lax
from jax.experimental import pallas as pl
from jax.experimental.pallas import tpu as pltpu
from jax.sharding import PartitionSpec as P

HEADS = 16
HEAD_DIM = 72
WINDOW = 8
D = 1152
TOK = 128
CLIPS = 4
REWARDS = 8
ROWS = 16
CHUNK = 384
PIECE = 18
GROUP = 4
EPS = 1e-06
SCALE = 1.0 / math.sqrt(HEAD_DIM)

f32 = jnp.float32
bf16 = jnp.bfloat16
HI = lax.Precision.HIGHEST
VMEM = pl.BlockSpec(memory_space=pltpu.VMEM)
ANY = pl.BlockSpec(memory_space=pl.ANY)


def dot(a, b, ca, cb, precision=None):
    return lax.dot_general(
        a, b, (((ca,), (cb,)), ((), ())), preferred_element_type=f32, precision=precision
    )


def clip_of(small, frame):
    end, clip = small[10:11, 0:1], jnp.zeros_like(frame)
    for c in range(CLIPS):
        clip += (frame >= end).astype(f32)
        if c + 1 < CLIPS:
            end = end + small[10:11, c + 1 : c + 2]
    return clip


def frames(dims, axis):
    return (lax.broadcasted_iota(jnp.int32, dims, axis) >> 2).astype(f32)


def span(h):
    low = HEAD_DIM * h
    return low // 128 * 128, -(-(low + HEAD_DIM) // 128) * 128


def lane_mask(h):
    start, end = span(h)
    lane = lax.broadcasted_iota(jnp.int32, (1, end - start), 1) + (start - HEAD_DIM * h)
    return ((lane >= 0) & (lane < HEAD_DIM)).astype(f32).astype(bf16)


def standard(values):
    centre = values - jnp.mean(values, axis=-1, keepdims=True)
    inv_std = lax.rsqrt(jnp.mean(centre * centre, axis=-1, keepdims=True) + EPS)
    return centre * inv_std, inv_std


def position():
    tm, dp = lax.axis_index("tm"), lax.axis_index("dp")
    return dp & 3, (tm >> 1) & 3, dp >> 2, tm & 1


def shape(dims, kind):
    return jax.ShapeDtypeStruct(dims, kind)


def call(kernel, out_shape, in_specs, scratch, mib, name, flops=0, moved=0):
    return pl.pallas_call(
        kernel,
        out_shape=out_shape,
        in_specs=in_specs,
        out_specs=jax.tree.map(lambda _: VMEM, out_shape),
        scratch_shapes=scratch,
        compiler_params=pltpu.CompilerParams(vmem_limit_bytes=mib << 20),
        cost_estimate=pl.CostEstimate(flops=flops, bytes_accessed=moved, transcendentals=0),
        name=name,
    )


def halves_kernel(x_ref, keep_ref, send_ref):
    z = lax.axis_index("tm") >> 3
    for a in range(2):
        keep_ref[a] = x_ref[a, z]
        send_ref[a] = x_ref[a, 1 - z]


def halves(tokens):
    return call(
        halves_kernel,
        (shape((2, 4, 8, D), bf16),) * 2,
        [VMEM],
        [],
        4,
        "halves",
        moved=600_000,
    )(tokens.reshape(2, 2, 4, 8, D))


def deal_kernel(keep_ref, far_ref, small, loaded, *outs):
    _, y, _, _ = position()
    for k in range(4):
        for a in range(2):
            outs[k][a] = keep_ref[a, (y + k) & 3]
            outs[k][2 + a] = far_ref[a, (y + k) & 3]


def deal(keep, far, small, loaded):
    return call(
        deal_kernel,
        (shape((4, 8, D), bf16),) * 4,
        [VMEM] * 4,
        [],
        4,
        "deal",
        moved=600_000,
    )(keep, far, small, loaded)


def pack_kernel(lens_ref, teacher_ref, ln_ref, og_ref, rh_ref, small):
    small[...] = jnp.zeros_like(small)
    small[0:REWARDS] = rh_ref[...]
    small[8] = og_ref[...]
    small[9] = ln_ref[...]
    small[10:11, 0:CLIPS] = lens_ref[...].astype(f32)
    for c in range(CLIPS):
        small[16 : 16 + REWARDS, c : c + 1] = upright(teacher_ref[c : c + 1])


def upright(row):
    return jnp.sum(jnp.where(eye(), row, 0.0), axis=1, keepdims=True)


def eye():
    side = (REWARDS, REWARDS)
    return lax.broadcasted_iota(jnp.int32, side, 0) == lax.broadcasted_iota(jnp.int32, side, 1)


def pack(clip_frames, teacher, ln_gain, out_gain, reward):
    return call(
        pack_kernel, shape((24, D), f32), [VMEM] * 5, [], 2, "pack", moved=200_000
    )(clip_frames, teacher, ln_gain, out_gain, reward)


def split_kernel(loaded, *refs):
    core = position()[3]
    for k in range(4):
        for z in range(2):
            rows = [refs[k][2 * z + a].astype(f32) for a in range(2)]
            low = jnp.concatenate([r[0:4] for r in rows], axis=0)
            high = jnp.concatenate([r[4:8] for r in rows], axis=0)
            refs[4][2 * k + z] = jnp.where(core == 0, low, high).astype(bf16)
            refs[5][2 * k + z] = jnp.where(core == 0, high, low).astype(bf16)


def split(parts, loaded):
    return call(
        split_kernel,
        (shape((8, 8, D), bf16),) * 2,
        [VMEM] * 5,
        [],
        4,
        "split",
        moved=600_000,
    )(loaded, *parts)


def load(sources, after, mib):
    def kernel(*refs):
        count = len(sources)
        ins, outs, sems = refs[:count], refs[count + 1 : -1], refs[-1]
        copies = []
        for k, (_, column) in enumerate(sources):
            source = ins[k] if column is None else ins[k].at[:, pl.ds(column, D)]
            copies.append(pltpu.make_async_copy(source, outs[k], sems.at[k]))
        for copy in copies:
            copy.start()
        outs[count][...] = jnp.zeros_like(outs[count])
        for copy in copies:
            copy.wait()

    return call(
        kernel,
        (shape((D, D), bf16),) * len(sources) + (shape((8, 128), f32),),
        [ANY] * (len(sources) + 1),
        [pltpu.SemaphoreType.DMA((len(sources),))],
        mib,
        "load",
        moved=10_000_000,
    )(*[array for array, _ in sources], after)


def forward_kernel(
    x0, x1, wq_ref, wk_ref, wv_ref, wo_ref, small,
    normed_ref, attended_ref, proj_ref, p_ref, cen_ref, inv_ref, tot_ref,
    acc, xs,
):
    tm = lax.axis_index("tm")
    for core, part in enumerate((x0, x1)):
        for k in range(4):
            y = ((tm >> 1) - k) & 3
            for z in range(2):
                xs[((tm & 9) ^ (8 * z + core)) | (2 * y)] = part[2 * k + z].astype(f32)
    x = xs[...].reshape(TOK, D)
    norm, _ = standard(x)
    normed = (norm * small[9:10, :]).astype(bf16)
    normed_ref[...] = normed
    for i, w_ref in enumerate((wq_ref, wk_ref, wv_ref)):
        for j in range(0, D, CHUNK):
            part = dot(normed, w_ref[:, j : j + CHUNK], 1, 0)
            proj_ref[:, i * D + j : i * D + j + CHUNK] = part.astype(bf16)
    row = lax.broadcasted_iota(jnp.int32, (TOK, TOK), 0)
    col = lax.broadcasted_iota(jnp.int32, (TOK, TOK), 1)
    lag = (col >> 2) - (row >> 2)
    allowed = (
        ((row & 3) == (col & 3))
        & (lag >= -(WINDOW // 2))
        & (lag < WINDOW - WINDOW // 2)
        & (clip_of(small, frames((TOK, TOK), 0)) == clip_of(small, frames((TOK, TOK), 1)))
    )
    acc[...] = jnp.zeros_like(acc)
    for h in range(HEADS):
        a, b = span(h)
        mask = lane_mask(h)
        p_ref[h] = dot(proj_ref[:, a:b] * mask, proj_ref[:, D + a : D + b], 1, 1) * SCALE
    for h in range(0, HEADS, GROUP):
        masked = jnp.where(allowed[None], p_ref[h : h + GROUP], -1e30)
        terms = jnp.exp(masked - jnp.max(masked, axis=2, keepdims=True))
        weights = terms / jnp.sum(terms, axis=2, keepdims=True)
        p_ref[h : h + GROUP] = weights
    for h in range(HEADS):
        a, b = span(h)
        acc[:, a:b] += dot(
            p_ref[h].astype(bf16), proj_ref[:, 2 * D + a : 2 * D + b] * lane_mask(h), 1, 0
        )
    attended = acc[...].astype(bf16)
    attended_ref[...] = attended
    mixed = xs[...].reshape(TOK, D) + dot(attended, wo_ref[...], 1, 0)
    centred, inv_std = standard(mixed)
    cen_ref[...] = centred
    inv_ref[...] = jnp.broadcast_to(inv_std, (TOK, 128))
    final = centred * small[8:9, :]
    clip = clip_of(small, frames((TOK, 1), 0))
    tot_ref[...] = jnp.zeros_like(tot_ref)
    for c in range(CLIPS):
        sums = jnp.sum(jnp.where(clip == c, final, 0.0), axis=0, keepdims=True)
        tot_ref[:, c : c + 1] = jnp.sum(small[0:REWARDS, :] * sums, axis=1, keepdims=True)


def forward(x, weights, small):
    return call(
        forward_kernel,
        (
            shape((TOK, D), bf16),
            shape((TOK, D), bf16),
            shape((TOK, 3 * D), bf16),
            shape((HEADS, TOK, TOK), f32),
            shape((TOK, D), f32),
            shape((TOK, 128), f32),
            shape((REWARDS, 8), f32),
        ),
        [VMEM] * 7,
        [pltpu.VMEM((TOK, D), f32), pltpu.VMEM((16, 8, D), f32)],
        24,
        "forward",
        flops=2_000_000_000,
        moved=14_000_000,
    )(*x, *weights, small)


def place_rows(src, dst, where, x_first):
    x, y, z, _ = where
    for k in range(64):
        first, second, kz = k // 16, k // 4 % 4, k % 4
        kx, ky = (first, second) if x_first else (second, first)
        dp = ((z + kz) & 3) * 4 + ((x + kx) & 3)
        start = dp * 72 + ((y + ky) & 3) * PIECE
        dst[PIECE * k : PIECE * (k + 1), :] = src[pl.ds(start, PIECE), :]


def turn_kernel(normed_ref, attended_ref, keep_ref, send_ref, turned, placed):
    where = position()
    core = where[3]
    turned[0] = normed_ref[...].astype(f32).T
    turned[1] = attended_ref[...].astype(f32).T
    place_rows(turned.at[0], placed, where, True)
    keep_ref[0] = placed[...].astype(bf16)
    send_ref[0] = keep_ref[0]
    place_rows(turned.at[core], placed, where, False)
    keep_ref[1] = placed[...].astype(bf16)
    place_rows(turned.at[1 - core], placed, where, False)
    send_ref[1] = placed[...].astype(bf16)


def turn(normed, attended):
    return call(
        turn_kernel,
        (shape((2, D, TOK), bf16), shape((2, D, TOK), bf16)),
        [VMEM] * 2,
        [pltpu.VMEM((2, D, TOK), f32), pltpu.VMEM((D, TOK), f32)],
        8,
        "turn",
        moved=4_000_000,
    )(normed, attended)


def backward_kernel(
    t0, t1, t2, t3, small, proj_ref, p_ref, cen_ref, inv_ref, wo_ref,
    scores_ref, keep_ref, send_ref,
    dq, dk, dv, wg, da_ref,
):
    clip_col = lax.broadcasted_iota(jnp.int32, (REWARDS, 8), 1)
    count = jnp.ones((REWARDS, 8), f32)
    for c in range(CLIPS):
        count = jnp.where(clip_col == c, small[10:11, c : c + 1] * 64.0, count)
    scores = ((t0[...] + t2[...]) + (t1[...] + t3[...])) / count
    scores = scores[:, 0:CLIPS]
    for c in range(CLIPS):
        column = jnp.where(eye(), scores[:, c : c + 1], 0.0)
        scores_ref[c : c + 1, :] = jnp.sum(column, axis=0, keepdims=True)
    residue = (scores - small[16:24, 0:CLIPS]) / ROWS
    clip = clip_of(small, frames((TOK, 1), 0))
    scaled = jnp.zeros((TOK, D), f32)
    for c in range(CLIPS):
        row = jnp.sum(small[0:REWARDS, :] * residue[:, c : c + 1], axis=0, keepdims=True)
        scaled = jnp.where(clip == c, row * small[8:9, :], scaled)
    centred = cen_ref[...]
    mixed_grad = (
        scaled
        - jnp.mean(scaled, axis=-1, keepdims=True)
        - centred * jnp.mean(scaled * centred, axis=-1, keepdims=True)
    ) * inv_ref[:, 0:1]
    mixed_grad = mixed_grad.astype(bf16)
    da_ref[...] = dot(mixed_grad, wo_ref[...], 1, 1).astype(bf16)
    dq[...] = jnp.zeros_like(dq)
    dk[...] = jnp.zeros_like(dk)
    dv[...] = jnp.zeros_like(dv)
    for h in range(HEADS):
        a, b = span(h)
        mask = lane_mask(h)
        wg[h] = dot(da_ref[:, a:b] * mask, proj_ref[:, 2 * D + a : 2 * D + b], 1, 1)
    for h in range(0, HEADS, GROUP):
        weights = p_ref[h : h + GROUP]
        weight_grad = wg[h : h + GROUP]
        inner = jnp.sum(weights * weight_grad, axis=2, keepdims=True)
        wg[h : h + GROUP] = weights * (weight_grad - inner)
    for h in range(HEADS):
        a, b = span(h)
        mask = lane_mask(h)
        logit_grad = wg[h].astype(bf16)
        dq[:, a:b] += dot(logit_grad, proj_ref[:, D + a : D + b] * mask, 1, 0)
        dk[:, a:b] += dot(logit_grad, proj_ref[:, a:b] * mask, 0, 0)
        dv[:, a:b] += dot(p_ref[h].astype(bf16), da_ref[:, a:b] * mask, 0, 0)

    def store(ref_qk, ref_vo):
        ref_qk[0] = (dq[...] * SCALE).astype(bf16)
        ref_qk[1] = (dk[...] * SCALE).astype(bf16)
        ref_vo[0] = dv[...].astype(bf16)
        ref_vo[1] = mixed_grad

    core = position()[3]

    @pl.when(core == 0)
    def _():
        store(keep_ref, send_ref)

    @pl.when(core != 0)
    def _():
        store(send_ref, keep_ref)


def backward(totals, small, proj, p, centred, inv, w_out):
    return call(
        backward_kernel,
        (
            shape((CLIPS, REWARDS), f32),
            shape((2, TOK, D), bf16),
            shape((2, TOK, D), bf16),
        ),
        [VMEM] * 10,
        [pltpu.VMEM((TOK, D), f32)] * 3
        + [
            pltpu.VMEM((HEADS, TOK, TOK), f32),
            pltpu.VMEM((TOK, D), bf16),
        ],
        16,
        "backward",
        flops=1_500_000_000,
        moved=8_000_000,
    )(*totals, small, proj, p, centred, inv, w_out)


PARTS = ((2, 0), (2, 1), (1, 1), (3, 0), (1, 0), (3, 1))


def gradient_kernel(lk, lr, rk, rr, *outs):
    for i in range(2):
        right = jnp.concatenate([rk[i], rr[i]], axis=0)
        for k in (2, 1, 3, 0):
            rows = slice(288 * k, 288 * (k + 1))
            left = jnp.concatenate([lk[i, rows], lr[i, rows]], axis=1)
            part = dot(left, right, 1, 0).astype(bf16)
            if k == 0:
                outs[7 * i + 6][...] = part
            else:
                for j, (distance, piece) in enumerate(PARTS):
                    if distance == k:
                        outs[7 * i + j][...] = part[144 * piece : 144 * (piece + 1)]


def gradient(left_keep, left_recv, right_keep, right_recv):
    parts = call(
        gradient_kernel,
        ((shape((144, D), bf16),) * 6 + (shape((288, D), bf16),)) * 2,
        [VMEM] * 4,
        [],
        16,
        "gradient",
        flops=1_400_000_000,
        moved=8_000_000,
    )(left_keep, left_recv, right_keep, right_recv)
    return parts[:7], parts[7:]


def relay_kernel(*refs):
    for k in range(4):
        refs[8 + k][...] = (refs[k][...].astype(f32) + refs[4 + k][...].astype(f32)).astype(bf16)


def relay(arrived, own):
    return call(
        relay_kernel,
        (shape((144, D), bf16),) * 4,
        [VMEM] * 8,
        [],
        8,
        "relay",
        moved=4_000_000,
    )(*arrived, *own)


def total(refs):
    result = refs[0][...].astype(f32)
    for ref in refs[1:]:
        result += ref[...].astype(f32)
    return result


SLOT = ((0, 3, 6, 5), (1, 2, 7, 4))


def first_sum_kernel(*refs):
    for i in range(2):
        plain_on, plain_back, relayed_on, relayed_back, own = (refs[2 * j + i] for j in range(5))
        result = own[...].astype(f32) + jnp.concatenate(
            [
                plain_back[...].astype(f32) + relayed_on[...].astype(f32),
                plain_on[...].astype(f32) + relayed_back[...].astype(f32),
            ],
            axis=0,
        )
        for k in range(4):
            refs[10 + SLOT[1 - i][k]][...] = result[72 * k : 72 * (k + 1)].astype(bf16)


def first_sum(parts):
    return call(
        first_sum_kernel,
        (shape((72, D), bf16),) * 8,
        [VMEM] * 10,
        [],
        12,
        "first_sum",
        moved=6_000_000,
    )(*parts)


def second_sum_kernel(*refs):
    sums = [total([refs[SLOT[i][k]] for k in range(4)]) for i in (1, 0)]
    rest = jnp.zeros((4, D), f32)
    for k in range(4):
        rows = slice(PIECE * k, PIECE * (k + 1))
        refs[8 + k][...] = jnp.concatenate([sums[0][rows], sums[1][rows], rest], axis=0).astype(
            bf16
        )


def second_sum(parts):
    return call(
        second_sum_kernel,
        (shape((40, D), bf16),) * 4,
        [VMEM] * 8,
        [],
        6,
        "second_sum",
        moved=1_700_000,
    )(*parts)


def sum_kernel(*refs):
    refs[-1][...] = total(refs[:-1]).astype(bf16)


def pair_sum_kernel(a, b, *rest):
    out = rest[-1]
    out[...] = a[...] + b[...]


def pair_sum(a, b, *after):
    specs = [VMEM] * 2 + [ANY] * len(after)
    return call(
        pair_sum_kernel, shape((REWARDS, 8), f32), specs, [], 1, "pair_sum", moved=20_000
    )(a, b, *after)


def plain_sum(parts):
    return call(
        sum_kernel,
        shape(parts[0].shape, bf16),
        [VMEM] * len(parts),
        [],
        3,
        "plain_sum",
        moved=500_000,
    )(*parts)


def stack_kernel(*refs):
    for k in range(4):
        refs[4][k] = refs[k][...]


def stack(parts):
    return call(
        stack_kernel, shape((4, 40, D), bf16), [VMEM] * 4, [], 3, "stack", moved=800_000
    )(*parts)


def last_kernel(mine, other, qkv_ref, out_ref, held):
    _, y_here, _, core = position()
    for k in range(4):
        y = (y_here - k) & 3
        held[core, y] = mine[k].astype(f32)
        held[1 - core, y] = other[k].astype(f32)
    for y in range(4):
        rows = slice(PIECE * y, PIECE * (y + 1))
        qkv_ref[rows, 0:D] = held[0, y, 0:PIECE]
        qkv_ref[rows, D : 2 * D] = held[0, y, PIECE : 2 * PIECE]
        qkv_ref[rows, 2 * D : 3 * D] = held[1, y, 0:PIECE]
        out_ref[rows, :] = held[1, y, PIECE : 2 * PIECE]


def last(mine, other):
    return call(
        last_kernel,
        (shape((72, 3 * D), f32), shape((72, D), f32)),
        [VMEM] * 2,
        [pltpu.VMEM((2, 4, 40, D), f32)],
        10,
        "last",
        moved=2_000_000,
    )(mine, other)


def to_core(block):
    return lax.ppermute(block, "tm", [(i, i ^ 1) for i in range(16)])


def to_far(block):
    return lax.ppermute(block, "tm", [(i, i ^ 8) for i in range(16)])


def along_y(block, k):
    return lax.ppermute(block, "tm", [(i, i & 9 | (i + 2 * k) & 6) for i in range(16)])


def along_x(block, k):
    return lax.ppermute(block, "dp", [(i, i & 12 | (i + k) & 3) for i in range(16)])


def around_z(block, k):
    route = []
    for tm in range(16):
        for dp in range(16):
            step = {1: 1, 3: -1, 2: -2 if tm & 1 else 2}[k]
            z = ((tm >> 3) * 4 + (dp >> 2) + step) & 7
            there = (tm & 7 | (z >> 2) << 3) * 16 + ((z & 3) << 2 | dp & 3)
            route.append((tm * 16 + dp, there))
    return lax.ppermute(block, ("tm", "dp"), route)


def exchange(slots):
    moved = list(slots)
    for k in (1, 3, 2):
        moved[SLOT[1][k]] = along_y(slots[SLOT[1][k]], k)
        moved[SLOT[0][k]] = along_x(slots[SLOT[0][k]], k)
    return moved


def around(x_half, y_half):
    on, back = (along_x, along_y), 3
    halves = (x_half, y_half)
    arrived = [on[i](halves[i][j], 1 if j == 0 else back) for j in range(2) for i in range(2)]
    plain = []
    for j in range(2):
        for i in range(2):
            block, _ = lax.optimization_barrier((halves[i][2 + j], arrived[2 * j + i]))
            plain.append(on[i](block, 1 if j == 0 else back))
    own = [halves[i][4 + j] for j in range(2) for i in range(2)]
    sums = relay(arrived, own)
    relayed = [on[i](sums[2 * j + i], 1 if j == 0 else back) for j in range(2) for i in range(2)]
    return first_sum(plain + relayed + [x_half[6], y_half[6]])


def on_device(tokens, clip_frames, teacher_scores, ln_gain, w_qkv, w_out, out_gain, reward_head):
    keep, send = halves(tokens[0])
    small = pack(clip_frames, teacher_scores[0], ln_gain, out_gain, reward_head.T)
    wq, wk, loaded = load([(w_qkv, 0), (w_qkv, D)], keep, 44)
    parts = deal(keep, to_far(send), small, loaded)
    wv, wo, loaded = load([(w_qkv, 2 * D), (w_out, None)], parts[0], 42)
    weights = wq, wk, wv, wo
    keep, send = split([parts[0]] + [along_y(parts[k], k) for k in (1, 2, 3)], loaded)
    x = [keep, to_core(send)]
    normed, attended, proj, p, centred, inv, partial = forward(x, weights, small)
    partial = pair_sum(partial, to_core(partial))
    normed, attended, _ = lax.optimization_barrier((normed, attended, partial))
    left_keep, left_send = turn(normed, attended)
    left_recv = to_core(left_send)
    partial = pair_sum(partial, to_far(partial), left_keep)
    totals = [partial] + [along_y(partial, k) for k in (1, 2, 3)]
    scores, right_keep, right_send = backward(totals, small, proj, p, centred, inv, weights[3])
    parts = gradient(left_keep, left_recv, right_keep, to_core(right_send))
    parts = second_sum(exchange(around(*parts)))
    part = plain_sum([parts[0]] + [around_z(parts[k], k) for k in (1, 2, 3)])
    part = plain_sum([part, to_far(part)])
    mine = stack([part] + [along_y(part, k) for k in (1, 2, 3)])
    qkv_total, out_total = last(mine, to_core(mine))
    return (scores[None], qkv_total, out_total)


def solution(mesh):
    return jax.shard_map(
        on_device,
        mesh=mesh,
        in_specs=(
            P("dp", "tm", None, None),
            P("dp", None),
            P("dp", None, None),
            P(),
            P(),
            P(),
            P(),
            P(),
        ),
        out_specs=(P("dp", None, None), P("dp", None), P("dp", None)),
        check_vma=False,
    )
```

profile of v0, /device:TPU:1, one launch (start us, length us, event | category | flops | bytes accessed | tf_op | source)
XLA Modules:
  0.0 134.4 jit_solution(8163342435573231648)
XLA Ops:
  0.6 1.0 copy-done.1
  1.6 7.8 %collective-permute-start = (bf16[2,4,8,1152]{3,2,1,0:T(8,128)(2,1)S(1)}, bf16[2,4,8,1152]{3,2,1,0:T(8,128)(2,1)S(1)}, u32[]{:S(2)}, u32[]{:S(2)}) collective-permute-start(bf16[2,4,8,1152]{3,2,1,0:T(8,128)(2,1)S(1)} %get-tuple-element.68), channel_id=1, source_target_pairs={{0,128},{16,144},{32,160},{48,176},{64,192},{80,208},{96,224},{112... | collective-permute-start | bytes 442376 | tf_op jit(solution)/shard_map/ppermute | solution.py:578
  9.5 2.7 %load.2 = (bf16[1152,1152]{1,0:T(8,128)(2,1)S(1)}, bf16[1152,1152]{1,0:T(8,128)(2,1)S(1)}, f32[8,128]{1,0:T(8,128)S(1)}) custom-call(bf16[1152,3456]{1,0:T(8,128)(2,1)} %refs_0_.3, bf16[1152,3456]{1,0:T(8,128)(2,1)} %refs_0_.3, bf16[2,4,8,1152]{3,2,1,0:T(8,128)(2,1)S(1)} %get-tuple-element.67.refs_2_.keep_ref), custom_call_target="tpu_custom_call" | custom-call | bytes 10000000 | tf_op jit(solution)/shard_map/load/pallas_call | solution.py:190
  12.4 0.1 collective-permute-done.far_ref
  12.5 1.9 %collective-permute-start.1 = (bf16[4,8,1152]{2,1,0:T(8,128)(2,1)S(1)}, bf16[4,8,1152]{2,1,0:T(8,128)(2,1)S(1)}, u32[]{:S(2)}, u32[]{:S(2)}) collective-permute-start(bf16[4,8,1152]{2,1,0:T(8,128)(2,1)S(1)} %get-tuple-element.72), channel_id=1, source_target_pairs={{0,32},{16,48},{32,64},{48,80},{64,96},{80,112},{96,0},{112,16},{1... | collective-permute-start | bytes 221192 | tf_op jit(solution)/shard_map/ppermute | solution.py:582
  14.4 2.6 %collective-permute-start.2 = (bf16[4,8,1152]{2,1,0:T(8,128)(2,1)S(1)}, bf16[4,8,1152]{2,1,0:T(8,128)(2,1)S(1)}, u32[]{:S(2)}, u32[]{:S(2)}) collective-permute-start(bf16[4,8,1152]{2,1,0:T(8,128)(2,1)S(1)} %get-tuple-element.73), channel_id=1, source_target_pairs={{0,64},{16,80},{32,96},{48,112},{64,0},{80,16},{96,32},{112,48},{1... | collective-permute-start | bytes 221192 | tf_op jit(solution)/shard_map/ppermute | solution.py:582
  17.0 1.1 collective-permute-start.3
  18.1 1.8 %load.3 = (bf16[1152,1152]{1,0:T(8,128)(2,1)S(1)}, bf16[1152,1152]{1,0:T(8,128)(2,1)S(1)}, f32[8,128]{1,0:T(8,128)S(1)}) custom-call(bf16[1152,3456]{1,0:T(8,128)(2,1)} %refs_0_.3, bf16[1152,1152]{1,0:T(8,128)(2,1)S(1)} %copy-done, bf16[4,8,1152]{2,1,0:T(8,128)(2,1)S(1)} %get-tuple-element.70.refs_2_.refs_0_), custom_call_target="tpu_custom_call" | custom-call | bytes 10000000 | tf_op jit(solution)/shard_map/load/pallas_call | solution.py:190
  19.9 1.4 %collective-permute-done.3.refs_3_ = bf16[4,8,1152]{2,1,0:T(8,128)(2,1)S(1)} collective-permute-done((bf16[4,8,1152]{2,1,0:T(8,128)(2,1)S(1)}, bf16[4,8,1152]{2,1,0:T(8,128)(2,1)S(1)}, u32[]{:S(2)}, u32[]{:S(2)}) %collective-permute-start.3) | collective-permute-done | bytes 73760 | tf_op jit(solution)/shard_map/ppermute | solution.py:582
  21.4 2.1 %collective-permute-start.4 = (bf16[8,8,1152]{2,1,0:T(8,128)(2,1)S(1)}, bf16[8,8,1152]{2,1,0:T(8,128)(2,1)S(1)}, u32[]{:S(2)}, u32[]{:S(2)}) collective-permute-start(bf16[8,8,1152]{2,1,0:T(8,128)(2,1)S(1)} %get-tuple-element.76), channel_id=1, source_target_pairs={{0,16},{16,0},{32,48},{48,32},{64,80},{80,64},{96,112},{112,96},{1... | collective-permute-start | bytes 442376 | tf_op jit(solution)/shard_map/ppermute | solution.py:574
  23.5 1.0 collective-permute-done.4.x1
  24.5 3.8 %forward.1 = (bf16[128,1152]{1,0:T(8,128)(2,1)S(1)}, bf16[128,1152]{1,0:T(8,128)(2,1)S(1)}, bf16[128,3456]{1,0:T(8,128)(2,1)S(1)}, f32[16,128,128]{2,1,0:T(8,128...) custom-call(bf16[8,8,1152]{2,1,0:T(8,128)(2,1)S(1)} %get-tuple-element.75.x0, ...), custom_call_target="tpu_custom_call" | custom-call | flops 2000000000 | bytes 14000000 | tf_op jit(solution)/shard_map/forward/pallas_call | solution.py:259
  28.3 0.4 collective-permute-start.5
  28.6 0.8 collective-permute-done.5.b
  29.5 7.7 %collective-permute-start.6 = (f32[8,8]{1,0:T(8,128)S(1)}, f32[8,8]{1,0:T(8,128)S(1)}, u32[]{:S(2)}, u32[]{:S(2)}) collective-permute-start(f32[8,8]{1,0:T(8,128)S(1)} %pair_sum.2.a), channel_id=1, source_target_pairs={{0,128},{16,144},{32,160},{48,176},{64,192},{80,208},{96,224},{112... | collective-permute-start | bytes 776 | tf_op jit(solution)/shard_map/ppermute | solution.py:578
  37.2 0.5 turn.1
  37.7 0.5 collective-permute-done.6.b
  38.2 2.3 %collective-permute-start.9 = (f32[8,8]{1,0:T(8,128)S(1)}, f32[8,8]{1,0:T(8,128)S(1)}, u32[]{:S(2)}, u32[]{:S(2)}) collective-permute-start(f32[8,8]{1,0:T(8,128)S(1)} %pair_sum.3.t0), channel_id=1, source_target_pairs={{0,96},{16,112},{32,0},{48,16},{64,32},{80,48},{96,64},{112,80},{1... | collective-permute-start | bytes 776 | tf_op jit(solution)/shard_map/ppermute | solution.py:582
  40.5 0.6 collective-permute-start.7
  41.1 1.8 %collective-permute-start.10 = (bf16[2,1152,128]{2,1,0:T(8,128)(2,1)S(1)}, bf16[2,1152,128]{2,1,0:T(8,128)(2,1)S(1)}, u32[]{:S(2)}, u32[]{:S(2)}) collective-permute-start(bf16[2,1152,128]{2,1,0:T(8,128)(2,1)S(1)} %get-tuple-element.92), channel_id=1, source_target_pairs={{0,16},{16,0},{32,48},{48,32},{64,80},{80,64},{96,112},{112,96},{1... | collective-permute-start | bytes 1769480 | tf_op jit(solution)/shard_map/ppermute | solution.py:574
  42.8 1.6 %collective-permute-done.8.t2 = f32[8,8]{1,0:T(8,128)S(1)} collective-permute-done((f32[8,8]{1,0:T(8,128)S(1)}, f32[8,8]{1,0:T(8,128)S(1)}, u32[]{:S(2)}, u32[]{:S(2)}) %collective-permute-start.8) | collective-permute-done | bytes 288 | tf_op jit(solution)/shard_map/ppermute | solution.py:582
  44.4 3.3 %backward.1 = (f32[4,8]{1,0:T(4,128)}, bf16[2,128,1152]{2,1,0:T(8,128)(2,1)S(1)}, bf16[2,128,1152]{2,1,0:T(8,128)(2,1)S(1)}) custom-call(f32[8,8]{1,0:T(8,128)S(1)} %pair_sum.3.t0, f32[8,8]{1,0:T(8,128)S(1)} %collective-permute-done.7.t1, f32[8,8]{1,0:T(8,128)S(1)} %collective-permute-done.8.t2, f32[8,8]{1,0:T(8,128)S(1)} %collective-permute-done.9.t3, ...), custom_call_target="tpu_custom_call" | custom-call | flops 1500000000 | bytes 8000000 | tf_op jit(solution)/shard_map/backward/pallas_call | solution.py:381
  47.7 2.6 %collective-permute-start.11 = (bf16[2,128,1152]{2,1,0:T(8,128)(2,1)S(1)}, bf16[2,128,1152]{2,1,0:T(8,128)(2,1)S(1)}, u32[]{:S(2)}, u32[]{:S(2)}) collective-permute-start(bf16[2,128,1152]{2,1,0:T(8,128)(2,1)S(1)} %get-tuple-element.94), channel_id=1, source_target_pairs={{0,16},{16,0},{32,48},{48,32},{64,80},{80,64},{96,112},{112,96},{1... | collective-permute-start | bytes 1769480 | tf_op jit(solution)/shard_map/ppermute | solution.py:574
  50.4 1.6 %collective-permute-done.11.rr = bf16[2,128,1152]{2,1,0:T(8,128)(2,1)S(1)} collective-permute-done((bf16[2,128,1152]{2,1,0:T(8,128)(2,1)S(1)}, bf16[2,128,1152]{2,1,0:T(8,128)(2,1)S(1)}, u32[]{:S(2)}, u32[]{:S(2)}) %collective-permute-start.11) | collective-permute-done | bytes 589856 | tf_op jit(solution)/shard_map/ppermute | solution.py:574
  52.0 1.7 %gradient.1 = (bf16[144,1152]{1,0:T(8,128)(2,1)S(1)}, bf16[144,1152]{1,0:T(8,128)(2,1)S(1)}, bf16[144,1152]{1,0:T(8,128)(2,1)S(1)}, bf16[144,1152]{1,0:T(8,128)(...) custom-call(bf16[2,1152,128]{2,1,0:T(8,128)(2,1)S(1)} %get-tuple-ele, ...), custom_call_target="tpu_custom_call" | custom-call | flops 1400000000 | bytes 8000000 | tf_op jit(solution)/shard_map/gradient/pallas_call | solution.py:420
  53.7 1.3 collective-permute-start.12
  55.0 1.5 %collective-permute-start.16 = (bf16[144,1152]{1,0:T(8,128)(2,1)S(1)}, bf16[144,1152]{1,0:T(8,128)(2,1)S(1)}, u32[]{:S(2)}, u32[]{:S(2)}) collective-permute-start(bf16[144,1152]{1,0:T(8,128)(2,1)S(1)} %get-tuple-element.102), channel_id=1, source_target_pairs={{0,3},{1,0},{2,1},{3,2},{4,7},{5,4},{6,5},{7,6},{8,11},{9,8},{10,9... | collective-permute-start | bytes 995336 | tf_op jit(solution)/shard_map/ppermute | solution.py:586
  56.5 2.7 %collective-permute-start.18 = (bf16[144,1152]{1,0:T(8,128)(2,1)S(1)}, bf16[144,1152]{1,0:T(8,128)(2,1)S(1)}, u32[]{:S(2)}, u32[]{:S(2)}) collective-permute-start(bf16[144,1152]{1,0:T(8,128)(2,1)S(1)} %get-tuple-element.105), channel_id=1, source_target_pairs={{0,96},{16,112},{32,0},{48,16},{64,32},{80,48},{96,64},{112,80},{1... | collective-permute-start | bytes 995336 | tf_op jit(solution)/shard_map/ppermute | solution.py:582
  59.1 4.9 %collective-permute-done.12.refs_0_ = bf16[144,1152]{1,0:T(8,128)(2,1)S(1)} collective-permute-done((bf16[144,1152]{1,0:T(8,128)(2,1)S(1)}, bf16[144,1152]{1,0:T(8,128)(2,1)S(1)}, u32[]{:S(2)}, u32[]{:S(2)}) %collective-permute-start.12) | collective-permute-done | bytes 331808 | tf_op jit(solution)/shard_map/ppermute | solution.py:586
  64.0 0.9 collective-permute-done.14.refs_1_
  64.9 1.9 %collective-permute-start.17 = (bf16[144,1152]{1,0:T(8,128)(2,1)S(1)}, bf16[144,1152]{1,0:T(8,128)(2,1)S(1)}, u32[]{:S(2)}, u32[]{:S(2)}) collective-permute-start(bf16[144,1152]{1,0:T(8,128)(2,1)S(1)} %get-tuple-element.103), channel_id=1, source_target_pairs={{0,3},{1,0},{2,1},{3,2},{4,7},{5,4},{6,5},{7,6},{8,11},{9,8},{10,9... | collective-permute-start | bytes 995336 | tf_op jit(solution)/shard_map/ppermute | solution.py:586
  66.8 2.6 %collective-permute-start.19 = (bf16[144,1152]{1,0:T(8,128)(2,1)S(1)}, bf16[144,1152]{1,0:T(8,128)(2,1)S(1)}, u32[]{:S(2)}, u32[]{:S(2)}) collective-permute-start(bf16[144,1152]{1,0:T(8,128)(2,1)S(1)} %get-tuple-element.106), channel_id=1, source_target_pairs={{0,96},{16,112},{32,0},{48,16},{64,32},{80,48},{96,64},{112,80},{1... | collective-permute-start | bytes 995336 | tf_op jit(solution)/shard_map/ppermute | solution.py:582
  69.4 0.3 relay.1
  69.8 3.5 %collective-permute-done.13.refs_0_ = bf16[144,1152]{1,0:T(8,128)(2,1)S(1)} collective-permute-done((bf16[144,1152]{1,0:T(8,128)(2,1)S(1)}, bf16[144,1152]{1,0:T(8,128)(2,1)S(1)}, u32[]{:S(2)}, u32[]{:S(2)}) %collective-permute-start.13) | collective-permute-done | bytes 331808 | tf_op jit(solution)/shard_map/ppermute | solution.py:586
  73.3 0.6 collective-permute-done.15.refs_1_
  73.9 1.8 %collective-permute-start.22 = (bf16[144,1152]{1,0:T(8,128)(2,1)S(1)}, bf16[144,1152]{1,0:T(8,128)(2,1)S(1)}, u32[]{:S(2)}, u32[]{:S(2)}) collective-permute-start(bf16[144,1152]{1,0:T(8,128)(2,1)S(1)} %get-tuple-element.113), channel_id=1, source_target_pairs={{0,3},{1,0},{2,1},{3,2},{4,7},{5,4},{6,5},{7,6},{8,11},{9,8},{10,9... | collective-permute-start | bytes 995336 | tf_op jit(solution)/shard_map/ppermute | solution.py:586
  75.7 0.4 collective-permute-start.23
  76.1 4.6 %collective-permute-done.20.refs_4_ = bf16[144,1152]{1,0:T(8,128)(2,1)S(1)} collective-permute-done((bf16[144,1152]{1,0:T(8,128)(2,1)S(1)}, bf16[144,1152]{1,0:T(8,128)(2,1)S(1)}, u32[]{:S(2)}, u32[]{:S(2)}) %collective-permute-start.20) | collective-permute-done | bytes 331808 | tf_op jit(solution)/shard_map/ppermute | solution.py:586
  80.7 0.1 collective-permute-done.21.refs_5_
  80.8 1.2 collective-permute-done.23.refs_7_
  82.0 0.5 first_sum.1
  82.6 0.5 collective-permute-start.25
  83.0 2.3 %collective-permute-start.26 = (bf16[72,1152]{1,0:T(8,128)(2,1)S(1)}, bf16[72,1152]{1,0:T(8,128)(2,1)S(1)}, u32[]{:S(2)}, u32[]{:S(2)}) collective-permute-start(bf16[72,1152]{1,0:T(8,128)(2,1)S(1)} %get-tuple-element.121), channel_id=1, source_target_pairs={{0,96},{16,112},{32,0},{48,16},{64,32},{80,48},{96,64},{112,80},{1... | collective-permute-start | bytes 497672 | tf_op jit(solution)/shard_map/ppermute | solution.py:582
  85.3 2.6 %collective-permute-start.27 = (bf16[72,1152]{1,0:T(8,128)(2,1)S(1)}, bf16[72,1152]{1,0:T(8,128)(2,1)S(1)}, u32[]{:S(2)}, u32[]{:S(2)}) collective-permute-start(bf16[72,1152]{1,0:T(8,128)(2,1)S(1)} %get-tuple-element.122), channel_id=1, source_target_pairs={{0,3},{1,0},{2,1},{3,2},{4,7},{5,4},{6,5},{7,6},{8,11},{9,8},{10,9... | collective-permute-start | bytes 497672 | tf_op jit(solution)/shard_map/ppermute | solution.py:586
  87.9 0.6 collective-permute-start.29
  88.5 3.4 %collective-permute-done.27.refs_5_ = bf16[72,1152]{1,0:T(8,128)(2,1)S(1)} collective-permute-done((bf16[72,1152]{1,0:T(8,128)(2,1)S(1)}, bf16[72,1152]{1,0:T(8,128)(2,1)S(1)}, u32[]{:S(2)}, u32[]{:S(2)}) %collective-permute-start.27) | collective-permute-done | bytes 165920 | tf_op jit(solution)/shard_map/ppermute | solution.py:586
  92.0 2.4 %collective-permute-done.28.refs_6_ = bf16[72,1152]{1,0:T(8,128)(2,1)S(1)} collective-permute-done((bf16[72,1152]{1,0:T(8,128)(2,1)S(1)}, bf16[72,1152]{1,0:T(8,128)(2,1)S(1)}, u32[]{:S(2)}, u32[]{:S(2)}) %collective-permute-start.28) | collective-permute-done | bytes 165920 | tf_op jit(solution)/shard_map/ppermute | solution.py:586
  94.3 1.0 collective-permute-done.29.refs_7_
  95.4 0.2 second_sum.1
  95.6 1.8 %collective-permute-start.30 = (bf16[40,1152]{1,0:T(8,128)(2,1)S(1)}, bf16[40,1152]{1,0:T(8,128)(2,1)S(1)}, u32[]{:S(2)}, u32[]{:S(2)}) collective-permute-start(bf16[40,1152]{1,0:T(8,128)(2,1)S(1)} %get-tuple-element.126), channel_id=1, source_target_pairs={{0,4},{1,5},{2,6},{3,7},{4,8},{5,9},{6,10},{7,11},{8,12},{9,13},{1... | collective-permute-start | bytes 276488 | tf_op jit(solution)/shard_map/ppermute | solution.py:597
  97.4 3.7 %collective-permute-start.31 = (bf16[40,1152]{1,0:T(8,128)(2,1)S(1)}, bf16[40,1152]{1,0:T(8,128)(2,1)S(1)}, u32[]{:S(2)}, u32[]{:S(2)}) collective-permute-start(bf16[40,1152]{1,0:T(8,128)(2,1)S(1)} %get-tuple-element.127), channel_id=1, source_target_pairs={{0,8},{1,9},{2,10},{3,11},{4,12},{5,13},{6,14},{7,15},{8,128},{9,1... | collective-permute-start | bytes 276488 | tf_op jit(solution)/shard_map/ppermute | solution.py:597
  101.2 1.4 %collective-permute-start.32 = (bf16[40,1152]{1,0:T(8,128)(2,1)S(1)}, bf16[40,1152]{1,0:T(8,128)(2,1)S(1)}, u32[]{:S(2)}, u32[]{:S(2)}) collective-permute-start(bf16[40,1152]{1,0:T(8,128)(2,1)S(1)} %get-tuple-element.128), channel_id=1, source_target_pairs={{0,140},{1,141},{2,142},{3,143},{4,0},{5,1},{6,2},{7,3},{8,4},{9,5... | collective-permute-start | bytes 276488 | tf_op jit(solution)/shard_map/ppermute | solution.py:597
  102.5 0.5 collective-permute-done.31.refs_2_
  103.0 1.6 %collective-permute-done.32.refs_3_ = bf16[40,1152]{1,0:T(8,128)(2,1)S(1)} collective-permute-done((bf16[40,1152]{1,0:T(8,128)(2,1)S(1)}, bf16[40,1152]{1,0:T(8,128)(2,1)S(1)}, u32[]{:S(2)}, u32[]{:S(2)}) %collective-permute-start.32) | collective-permute-done | bytes 92192 | tf_op jit(solution)/shard_map/ppermute | solution.py:597
  104.6 4.6 %collective-permute-start.33 = (bf16[40,1152]{1,0:T(8,128)(2,1)S(1)}, bf16[40,1152]{1,0:T(8,128)(2,1)S(1)}, u32[]{:S(2)}, u32[]{:S(2)}) collective-permute-start(bf16[40,1152]{1,0:T(8,128)(2,1)S(1)} %plain_sum.2.refs_0_), channel_id=1, source_target_pairs={{0,128},{16,144},{32,160},{48,176},{64,192},{80,208},{96,224},{112... | collective-permute-start | bytes 276488 | tf_op jit(solution)/shard_map/ppermute | solution.py:578
  109.2 3.4 %collective-permute-done.33.refs_1_ = bf16[40,1152]{1,0:T(8,128)(2,1)S(1)} collective-permute-done((bf16[40,1152]{1,0:T(8,128)(2,1)S(1)}, bf16[40,1152]{1,0:T(8,128)(2,1)S(1)}, u32[]{:S(2)}, u32[]{:S(2)}) %collective-permute-start.33) | collective-permute-done | bytes 92192 | tf_op jit(solution)/shard_map/ppermute | solution.py:578
  112.7 0.8 collective-permute-start.35
  113.5 0.7 collective-permute-start.34
  114.2 1.9 %collective-permute-done.36.refs_3_ = bf16[40,1152]{1,0:T(8,128)(2,1)S(1)} collective-permute-done((bf16[40,1152]{1,0:T(8,128)(2,1)S(1)}, bf16[40,1152]{1,0:T(8,128)(2,1)S(1)}, u32[]{:S(2)}, u32[]{:S(2)}) %collective-permute-start.36) | collective-permute-done | bytes 92192 | tf_op jit(solution)/shard_map/ppermute | solution.py:582
  116.1 1.6 %collective-permute-done.35.refs_2_ = bf16[40,1152]{1,0:T(8,128)(2,1)S(1)} collective-permute-done((bf16[40,1152]{1,0:T(8,128)(2,1)S(1)}, bf16[40,1152]{1,0:T(8,128)(2,1)S(1)}, u32[]{:S(2)}, u32[]{:S(2)}) %collective-permute-start.35) | collective-permute-done | bytes 92192 | tf_op jit(solution)/shard_map/ppermute | solution.py:582
  117.7 1.3 collective-permute-done.34.refs_1_
  119.0 12.8 %collective-permute-start.37 = (bf16[4,40,1152]{2,1,0:T(8,128)(2,1)S(1)}, bf16[4,40,1152]{2,1,0:T(8,128)(2,1)S(1)}, u32[]{:S(2)}, u32[]{:S(2)}) collective-permute-start(bf16[4,40,1152]{2,1,0:T(8,128)(2,1)S(1)} %stack.1.mine), channel_id=1, source_target_pairs={{0,16},{16,0},{32,48},{48,32},{64,80},{80,64},{96,112},{112,96},{1... | collective-permute-start | bytes 1105928 | tf_op jit(solution)/shard_map/ppermute | solution.py:574
  131.8 1.3 collective-permute-done.37.other
  133.1 1.3 last.1
  (45 shorter events, 0.7 us)
Async XLA Ops:
  0.6 1.0 copy-start.1
  1.6 10.9 %collective-permute-start = (bf16[2,4,8,1152]{3,2,1,0:T(8,128)(2,1)S(1)}, bf16[2,4,8,1152]{3,2,1,0:T(8,128)(2,1)S(1)}, u32[]{:S(2)}, u32[]{:S(2)}) collective-permute-start(bf16[2,4,8,1152]{3,2,1,0:T(8,128)(2,1)S(1)} %get-tuple-element.68), channel_id=1, source_target_pairs={{0,128},{16,144},{32,160},{48,176},{64,192},{80,208},{96,224},{112... | collective-permute-start | bytes 442376 | tf_op jit(solution)/shard_map/ppermute | solution.py:578
  9.4 2.8 %copy-start.2 = (f32[1152,8]{0,1:T(8,128)S(1)}, f32[1152,8]{0,1:T(8,128)}, u32[]{:S(2)}) copy-start(f32[1152,8]{0,1:T(8,128)} %param.15) | copy-start | bytes 110596
  9.4 2.8 %copy-start.3 = (f32[1152]{0:T(1024)S(1)}, f32[1152]{0:T(1024)}, u32[]{:S(2)}) copy-start(f32[1152]{0:T(1024)} %ln_ref.1) | copy-start | bytes 13828
  9.4 2.8 %copy-start.4 = (f32[1152]{0:T(1024)S(1)}, f32[1152]{0:T(1024)}, u32[]{:S(2)}) copy-start(f32[1152]{0:T(1024)} %og_ref.1) | copy-start | bytes 13828
  9.4 2.8 %copy-start.5 = (f32[1,4,8]{2,1,0:T(4,128)S(1)}, f32[1,4,8]{2,1,0:T(4,128)}, u32[]{:S(2)}) copy-start(f32[1,4,8]{2,1,0:T(4,128)} %param.10) | copy-start | bytes 388
  9.5 2.8 %copy-start.6 = (s32[1,4]{1,0:T(1,128)S(1)}, s32[1,4]{1,0:T(1,128)}, u32[]{:S(2)}) copy-start(s32[1,4]{1,0:T(1,128)} %lens_ref.1) | copy-start | bytes 52
  9.5 8.6 %copy-start = (bf16[1152,1152]{1,0:T(8,128)(2,1)S(1)}, bf16[1152,1152]{1,0:T(8,128)(2,1)}, u32[]{:S(2)}) copy-start(bf16[1152,1152]{1,0:T(8,128)(2,1)} %refs_1_.3) | copy-start | bytes 7962628
  12.5 7.4 %collective-permute-start.1 = (bf16[4,8,1152]{2,1,0:T(8,128)(2,1)S(1)}, bf16[4,8,1152]{2,1,0:T(8,128)(2,1)S(1)}, u32[]{:S(2)}, u32[]{:S(2)}) collective-permute-start(bf16[4,8,1152]{2,1,0:T(8,128)(2,1)S(1)} %get-tuple-element.72), channel_id=1, source_target_pairs={{0,32},{16,48},{32,64},{48,80},{64,96},{80,112},{96,0},{112,16},{1... | collective-permute-start | bytes 221192 | tf_op jit(solution)/shard_map/ppermute | solution.py:582
  14.4 5.5 %collective-permute-start.2 = (bf16[4,8,1152]{2,1,0:T(8,128)(2,1)S(1)}, bf16[4,8,1152]{2,1,0:T(8,128)(2,1)S(1)}, u32[]{:S(2)}, u32[]{:S(2)}) collective-permute-start(bf16[4,8,1152]{2,1,0:T(8,128)(2,1)S(1)} %get-tuple-element.73), channel_id=1, source_target_pairs={{0,64},{16,80},{32,96},{48,112},{64,0},{80,16},{96,32},{112,48},{1... | collective-permute-start | bytes 221192 | tf_op jit(solution)/shard_map/ppermute | solution.py:582
  17.0 4.2 %collective-permute-start.3 = (bf16[4,8,1152]{2,1,0:T(8,128)(2,1)S(1)}, bf16[4,8,1152]{2,1,0:T(8,128)(2,1)S(1)}, u32[]{:S(2)}, u32[]{:S(2)}) collective-permute-start(bf16[4,8,1152]{2,1,0:T(8,128)(2,1)S(1)} %get-tuple-element.74), channel_id=1, source_target_pairs={{0,96},{16,112},{32,0},{48,16},{64,32},{80,48},{96,64},{112,80},{1... | collective-permute-start | bytes 221192 | tf_op jit(solution)/shard_map/ppermute | solution.py:582
  21.4 3.1 %collective-permute-start.4 = (bf16[8,8,1152]{2,1,0:T(8,128)(2,1)S(1)}, bf16[8,8,1152]{2,1,0:T(8,128)(2,1)S(1)}, u32[]{:S(2)}, u32[]{:S(2)}) collective-permute-start(bf16[8,8,1152]{2,1,0:T(8,128)(2,1)S(1)} %get-tuple-element.76), channel_id=1, source_target_pairs={{0,16},{16,0},{32,48},{48,32},{64,80},{80,64},{96,112},{112,96},{1... | collective-permute-start | bytes 442376 | tf_op jit(solution)/shard_map/ppermute | solution.py:574
  28.3 1.2 collective-permute-start.5
  29.5 8.7 %collective-permute-start.6 = (f32[8,8]{1,0:T(8,128)S(1)}, f32[8,8]{1,0:T(8,128)S(1)}, u32[]{:S(2)}, u32[]{:S(2)}) collective-permute-start(f32[8,8]{1,0:T(8,128)S(1)} %pair_sum.2.a), channel_id=1, source_target_pairs={{0,128},{16,144},{32,160},{48,176},{64,192},{80,208},{96,224},{112... | collective-permute-start | bytes 776 | tf_op jit(solution)/shard_map/ppermute | solution.py:578
  38.2 4.6 %collective-permute-start.9 = (f32[8,8]{1,0:T(8,128)S(1)}, f32[8,8]{1,0:T(8,128)S(1)}, u32[]{:S(2)}, u32[]{:S(2)}) collective-permute-start(f32[8,8]{1,0:T(8,128)S(1)} %pair_sum.3.t0), channel_id=1, source_target_pairs={{0,96},{16,112},{32,0},{48,16},{64,32},{80,48},{96,64},{112,80},{1... | collective-permute-start | bytes 776 | tf_op jit(solution)/shard_map/ppermute | solution.py:582
  40.5 4.0 %collective-permute-start.8 = (f32[8,8]{1,0:T(8,128)S(1)}, f32[8,8]{1,0:T(8,128)S(1)}, u32[]{:S(2)}, u32[]{:S(2)}) collective-permute-start(f32[8,8]{1,0:T(8,128)S(1)} %pair_sum.3.t0), channel_id=1, source_target_pairs={{0,64},{16,80},{32,96},{48,112},{64,0},{80,16},{96,32},{112,48},{1... | collective-permute-start | bytes 776 | tf_op jit(solution)/shard_map/ppermute | solution.py:582
  40.5 4.0 %collective-permute-start.7 = (f32[8,8]{1,0:T(8,128)S(1)}, f32[8,8]{1,0:T(8,128)S(1)}, u32[]{:S(2)}, u32[]{:S(2)}) collective-permute-start(f32[8,8]{1,0:T(8,128)S(1)} %pair_sum.3.t0), channel_id=1, source_target_pairs={{0,32},{16,48},{32,64},{48,80},{64,96},{80,112},{96,0},{112,16},{1... | collective-permute-start | bytes 776 | tf_op jit(solution)/shard_map/ppermute | solution.py:582
  41.1 9.3 %collective-permute-start.10 = (bf16[2,1152,128]{2,1,0:T(8,128)(2,1)S(1)}, bf16[2,1152,128]{2,1,0:T(8,128)(2,1)S(1)}, u32[]{:S(2)}, u32[]{:S(2)}) collective-permute-start(bf16[2,1152,128]{2,1,0:T(8,128)(2,1)S(1)} %get-tuple-element.92), channel_id=1, source_target_pairs={{0,16},{16,0},{32,48},{48,32},{64,80},{80,64},{96,112},{112,96},{1... | collective-permute-start | bytes 1769480 | tf_op jit(solution)/shard_map/ppermute | solution.py:574
  47.7 4.3 %collective-permute-start.11 = (bf16[2,128,1152]{2,1,0:T(8,128)(2,1)S(1)}, bf16[2,128,1152]{2,1,0:T(8,128)(2,1)S(1)}, u32[]{:S(2)}, u32[]{:S(2)}) collective-permute-start(bf16[2,128,1152]{2,1,0:T(8,128)(2,1)S(1)} %get-tuple-element.94), channel_id=1, source_target_pairs={{0,16},{16,0},{32,48},{48,32},{64,80},{80,64},{96,112},{112,96},{1... | collective-permute-start | bytes 1769480 | tf_op jit(solution)/shard_map/ppermute | solution.py:574
  53.7 10.3 %collective-permute-start.12 = (bf16[144,1152]{1,0:T(8,128)(2,1)S(1)}, bf16[144,1152]{1,0:T(8,128)(2,1)S(1)}, u32[]{:S(2)}, u32[]{:S(2)}) collective-permute-start(bf16[144,1152]{1,0:T(8,128)(2,1)S(1)} %get-tuple-element.96), channel_id=1, source_target_pairs={{0,1},{1,2},{2,3},{3,0},{4,5},{5,6},{6,7},{7,4},{8,9},{9,10},{10,1... | collective-permute-start | bytes 995336 | tf_op jit(solution)/shard_map/ppermute | solution.py:586
  55.0 9.9 %collective-permute-start.14 = (bf16[144,1152]{1,0:T(8,128)(2,1)S(1)}, bf16[144,1152]{1,0:T(8,128)(2,1)S(1)}, u32[]{:S(2)}, u32[]{:S(2)}) collective-permute-start(bf16[144,1152]{1,0:T(8,128)(2,1)S(1)} %get-tuple-element.99), channel_id=1, source_target_pairs={{0,32},{16,48},{32,64},{48,80},{64,96},{80,112},{96,0},{112,16},{1... | collective-permute-start | bytes 995336 | tf_op jit(solution)/shard_map/ppermute | solution.py:582
  55.0 9.9 %collective-permute-start.16 = (bf16[144,1152]{1,0:T(8,128)(2,1)S(1)}, bf16[144,1152]{1,0:T(8,128)(2,1)S(1)}, u32[]{:S(2)}, u32[]{:S(2)}) collective-permute-start(bf16[144,1152]{1,0:T(8,128)(2,1)S(1)} %get-tuple-element.102), channel_id=1, source_target_pairs={{0,3},{1,0},{2,1},{3,2},{4,7},{5,4},{6,5},{7,6},{8,11},{9,8},{10,9... | collective-permute-start | bytes 995336 | tf_op jit(solution)/shard_map/ppermute | solution.py:586
  56.5 10.3 %collective-permute-start.18 = (bf16[144,1152]{1,0:T(8,128)(2,1)S(1)}, bf16[144,1152]{1,0:T(8,128)(2,1)S(1)}, u32[]{:S(2)}, u32[]{:S(2)}) collective-permute-start(bf16[144,1152]{1,0:T(8,128)(2,1)S(1)} %get-tuple-element.105), channel_id=1, source_target_pairs={{0,96},{16,112},{32,0},{48,16},{64,32},{80,48},{96,64},{112,80},{1... | collective-permute-start | bytes 995336 | tf_op jit(solution)/shard_map/ppermute | solution.py:582
  64.0 9.3 %collective-permute-start.13 = (bf16[144,1152]{1,0:T(8,128)(2,1)S(1)}, bf16[144,1152]{1,0:T(8,128)(2,1)S(1)}, u32[]{:S(2)}, u32[]{:S(2)}) collective-permute-start(bf16[144,1152]{1,0:T(8,128)(2,1)S(1)} %get-tuple-element.97), channel_id=1, source_target_pairs={{0,1},{1,2},{2,3},{3,0},{4,5},{5,6},{6,7},{7,4},{8,9},{9,10},{10,1... | collective-permute-start | bytes 995336 | tf_op jit(solution)/shard_map/ppermute | solution.py:586
  64.9 9.0 %collective-permute-start.15 = (bf16[144,1152]{1,0:T(8,128)(2,1)S(1)}, bf16[144,1152]{1,0:T(8,128)(2,1)S(1)}, u32[]{:S(2)}, u32[]{:S(2)}) collective-permute-start(bf16[144,1152]{1,0:T(8,128)(2,1)S(1)} %get-tuple-element.100), channel_id=1, source_target_pairs={{0,32},{16,48},{32,64},{48,80},{64,96},{80,112},{96,0},{112,16},{1... | collective-permute-start | bytes 995336 | tf_op jit(solution)/shard_map/ppermute | solution.py:582
  64.9 10.8 %collective-permute-start.17 = (bf16[144,1152]{1,0:T(8,128)(2,1)S(1)}, bf16[144,1152]{1,0:T(8,128)(2,1)S(1)}, u32[]{:S(2)}, u32[]{:S(2)}) collective-permute-start(bf16[144,1152]{1,0:T(8,128)(2,1)S(1)} %get-tuple-element.103), channel_id=1, source_target_pairs={{0,3},{1,0},{2,1},{3,2},{4,7},{5,4},{6,5},{7,6},{8,11},{9,8},{10,9... | collective-permute-start | bytes 995336 | tf_op jit(solution)/shard_map/ppermute | solution.py:586
  66.8 9.3 %collective-permute-start.19 = (bf16[144,1152]{1,0:T(8,128)(2,1)S(1)}, bf16[144,1152]{1,0:T(8,128)(2,1)S(1)}, u32[]{:S(2)}, u32[]{:S(2)}) collective-permute-start(bf16[144,1152]{1,0:T(8,128)(2,1)S(1)} %get-tuple-element.106), channel_id=1, source_target_pairs={{0,96},{16,112},{32,0},{48,16},{64,32},{80,48},{96,64},{112,80},{1... | collective-permute-start | bytes 995336 | tf_op jit(solution)/shard_map/ppermute | solution.py:582
  69.7 11.0 %collective-permute-start.20 = (bf16[144,1152]{1,0:T(8,128)(2,1)S(1)}, bf16[144,1152]{1,0:T(8,128)(2,1)S(1)}, u32[]{:S(2)}, u32[]{:S(2)}) collective-permute-start(bf16[144,1152]{1,0:T(8,128)(2,1)S(1)} %get-tuple-element.111), channel_id=1, source_target_pairs={{0,1},{1,2},{2,3},{3,0},{4,5},{5,6},{6,7},{7,4},{8,9},{9,10},{10,1... | collective-permute-start | bytes 995336 | tf_op jit(solution)/shard_map/ppermute | solution.py:586
  73.3 7.5 %collective-permute-start.21 = (bf16[144,1152]{1,0:T(8,128)(2,1)S(1)}, bf16[144,1152]{1,0:T(8,128)(2,1)S(1)}, u32[]{:S(2)}, u32[]{:S(2)}) collective-permute-start(bf16[144,1152]{1,0:T(8,128)(2,1)S(1)} %get-tuple-element.112), channel_id=1, source_target_pairs={{0,32},{16,48},{32,64},{48,80},{64,96},{80,112},{96,0},{112,16},{1... | collective-permute-start | bytes 995336 | tf_op jit(solution)/shard_map/ppermute | solution.py:582
  73.9 6.9 %collective-permute-start.22 = (bf16[144,1152]{1,0:T(8,128)(2,1)S(1)}, bf16[144,1152]{1,0:T(8,128)(2,1)S(1)}, u32[]{:S(2)}, u32[]{:S(2)}) collective-permute-start(bf16[144,1152]{1,0:T(8,128)(2,1)S(1)} %get-tuple-element.113), channel_id=1, source_target_pairs={{0,3},{1,0},{2,1},{3,2},{4,7},{5,4},{6,5},{7,6},{8,11},{9,8},{10,9... | collective-permute-start | bytes 995336 | tf_op jit(solution)/shard_map/ppermute | solution.py:586
  75.7 6.3 %collective-permute-start.23 = (bf16[144,1152]{1,0:T(8,128)(2,1)S(1)}, bf16[144,1152]{1,0:T(8,128)(2,1)S(1)}, u32[]{:S(2)}, u32[]{:S(2)}) collective-permute-start(bf16[144,1152]{1,0:T(8,128)(2,1)S(1)} %get-tuple-element.114), channel_id=1, source_target_pairs={{0,96},{16,112},{32,0},{48,16},{64,32},{80,48},{96,64},{112,80},{1... | collective-permute-start | bytes 995336 | tf_op jit(solution)/shard_map/ppermute | solution.py:582
  82.5 5.5 %collective-permute-start.24 = (bf16[72,1152]{1,0:T(8,128)(2,1)S(1)}, bf16[72,1152]{1,0:T(8,128)(2,1)S(1)}, u32[]{:S(2)}, u32[]{:S(2)}) collective-permute-start(bf16[72,1152]{1,0:T(8,128)(2,1)S(1)} %get-tuple-element.119), channel_id=1, source_target_pairs={{0,32},{16,48},{32,64},{48,80},{64,96},{80,112},{96,0},{112,16},{1... | collective-permute-start | bytes 497672 | tf_op jit(solution)/shard_map/ppermute | solution.py:582
  82.6 6.0 %collective-permute-start.25 = (bf16[72,1152]{1,0:T(8,128)(2,1)S(1)}, bf16[72,1152]{1,0:T(8,128)(2,1)S(1)}, u32[]{:S(2)}, u32[]{:S(2)}) collective-permute-start(bf16[72,1152]{1,0:T(8,128)(2,1)S(1)} %get-tuple-element.120), channel_id=1, source_target_pairs={{0,1},{1,2},{2,3},{3,0},{4,5},{5,6},{6,7},{7,4},{8,9},{9,10},{10,1... | collective-permute-start | bytes 497672 | tf_op jit(solution)/shard_map/ppermute | solution.py:586
  83.0 5.5 %collective-permute-start.26 = (bf16[72,1152]{1,0:T(8,128)(2,1)S(1)}, bf16[72,1152]{1,0:T(8,128)(2,1)S(1)}, u32[]{:S(2)}, u32[]{:S(2)}) collective-permute-start(bf16[72,1152]{1,0:T(8,128)(2,1)S(1)} %get-tuple-element.121), channel_id=1, source_target_pairs={{0,96},{16,112},{32,0},{48,16},{64,32},{80,48},{96,64},{112,80},{1... | collective-permute-start | bytes 497672 | tf_op jit(solution)/shard_map/ppermute | solution.py:582
  85.3 6.7 %collective-permute-start.27 = (bf16[72,1152]{1,0:T(8,128)(2,1)S(1)}, bf16[72,1152]{1,0:T(8,128)(2,1)S(1)}, u32[]{:S(2)}, u32[]{:S(2)}) collective-permute-start(bf16[72,1152]{1,0:T(8,128)(2,1)S(1)} %get-tuple-element.122), channel_id=1, source_target_pairs={{0,3},{1,0},{2,1},{3,2},{4,7},{5,4},{6,5},{7,6},{8,11},{9,8},{10,9... | collective-permute-start | bytes 497672 | tf_op jit(solution)/shard_map/ppermute | solution.py:586
  87.9 6.5 %collective-permute-start.28 = (bf16[72,1152]{1,0:T(8,128)(2,1)S(1)}, bf16[72,1152]{1,0:T(8,128)(2,1)S(1)}, u32[]{:S(2)}, u32[]{:S(2)}) collective-permute-start(bf16[72,1152]{1,0:T(8,128)(2,1)S(1)} %get-tuple-element.123), channel_id=1, source_target_pairs={{0,2},{1,3},{2,0},{3,1},{4,6},{5,7},{6,4},{7,5},{8,10},{9,11},{10,... | collective-permute-start | bytes 497672 | tf_op jit(solution)/shard_map/ppermute | solution.py:586
  87.9 7.4 %collective-permute-start.29 = (bf16[72,1152]{1,0:T(8,128)(2,1)S(1)}, bf16[72,1152]{1,0:T(8,128)(2,1)S(1)}, u32[]{:S(2)}, u32[]{:S(2)}) collective-permute-start(bf16[72,1152]{1,0:T(8,128)(2,1)S(1)} %get-tuple-element.124), channel_id=1, source_target_pairs={{0,64},{16,80},{32,96},{48,112},{64,0},{80,16},{96,32},{112,48},{1... | collective-permute-start | bytes 497672 | tf_op jit(solution)/shard_map/ppermute | solution.py:582
  95.6 6.9 %collective-permute-start.30 = (bf16[40,1152]{1,0:T(8,128)(2,1)S(1)}, bf16[40,1152]{1,0:T(8,128)(2,1)S(1)}, u32[]{:S(2)}, u32[]{:S(2)}) collective-permute-start(bf16[40,1152]{1,0:T(8,128)(2,1)S(1)} %get-tuple-element.126), channel_id=1, source_target_pairs={{0,4},{1,5},{2,6},{3,7},{4,8},{5,9},{6,10},{7,11},{8,12},{9,13},{1... | collective-permute-start | bytes 276488 | tf_op jit(solution)/shard_map/ppermute | solution.py:597
  97.4 5.6 %collective-permute-start.31 = (bf16[40,1152]{1,0:T(8,128)(2,1)S(1)}, bf16[40,1152]{1,0:T(8,128)(2,1)S(1)}, u32[]{:S(2)}, u32[]{:S(2)}) collective-permute-start(bf16[40,1152]{1,0:T(8,128)(2,1)S(1)} %get-tuple-element.127), channel_id=1, source_target_pairs={{0,8},{1,9},{2,10},{3,11},{4,12},{5,13},{6,14},{7,15},{8,128},{9,1... | collective-permute-start | bytes 276488 | tf_op jit(solution)/shard_map/ppermute | solution.py:597
  101.2 3.4 %collective-permute-start.32 = (bf16[40,1152]{1,0:T(8,128)(2,1)S(1)}, bf16[40,1152]{1,0:T(8,128)(2,1)S(1)}, u32[]{:S(2)}, u32[]{:S(2)}) collective-permute-start(bf16[40,1152]{1,0:T(8,128)(2,1)S(1)} %get-tuple-element.128), channel_id=1, source_target_pairs={{0,140},{1,141},{2,142},{3,143},{4,0},{5,1},{6,2},{7,3},{8,4},{9,5... | collective-permute-start | bytes 276488 | tf_op jit(solution)/shard_map/ppermute | solution.py:597
  104.6 8.0 %collective-permute-start.33 = (bf16[40,1152]{1,0:T(8,128)(2,1)S(1)}, bf16[40,1152]{1,0:T(8,128)(2,1)S(1)}, u32[]{:S(2)}, u32[]{:S(2)}) collective-permute-start(bf16[40,1152]{1,0:T(8,128)(2,1)S(1)} %plain_sum.2.refs_0_), channel_id=1, source_target_pairs={{0,128},{16,144},{32,160},{48,176},{64,192},{80,208},{96,224},{112... | collective-permute-start | bytes 276488 | tf_op jit(solution)/shard_map/ppermute | solution.py:578
  112.6 3.5 %collective-permute-start.36 = (bf16[40,1152]{1,0:T(8,128)(2,1)S(1)}, bf16[40,1152]{1,0:T(8,128)(2,1)S(1)}, u32[]{:S(2)}, u32[]{:S(2)}) collective-permute-start(bf16[40,1152]{1,0:T(8,128)(2,1)S(1)} %plain_sum.3.refs_0_), channel_id=1, source_target_pairs={{0,96},{16,112},{32,0},{48,16},{64,32},{80,48},{96,64},{112,80},{1... | collective-permute-start | bytes 276488 | tf_op jit(solution)/shard_map/ppermute | solution.py:582
  112.7 5.0 %collective-permute-start.35 = (bf16[40,1152]{1,0:T(8,128)(2,1)S(1)}, bf16[40,1152]{1,0:T(8,128)(2,1)S(1)}, u32[]{:S(2)}, u32[]{:S(2)}) collective-permute-start(bf16[40,1152]{1,0:T(8,128)(2,1)S(1)} %plain_sum.3.refs_0_), channel_id=1, source_target_pairs={{0,64},{16,80},{32,96},{48,112},{64,0},{80,16},{96,32},{112,48},{1... | collective-permute-start | bytes 276488 | tf_op jit(solution)/shard_map/ppermute | solution.py:582
  113.5 5.5 %collective-permute-start.34 = (bf16[40,1152]{1,0:T(8,128)(2,1)S(1)}, bf16[40,1152]{1,0:T(8,128)(2,1)S(1)}, u32[]{:S(2)}, u32[]{:S(2)}) collective-permute-start(bf16[40,1152]{1,0:T(8,128)(2,1)S(1)} %plain_sum.3.refs_0_), channel_id=1, source_target_pairs={{0,32},{16,48},{32,64},{48,80},{64,96},{80,112},{96,0},{112,16},{1... | collective-permute-start | bytes 276488 | tf_op jit(solution)/shard_map/ppermute | solution.py:582
  119.0 14.1 %collective-permute-start.37 = (bf16[4,40,1152]{2,1,0:T(8,128)(2,1)S(1)}, bf16[4,40,1152]{2,1,0:T(8,128)(2,1)S(1)}, u32[]{:S(2)}, u32[]{:S(2)}) collective-permute-start(bf16[4,40,1152]{2,1,0:T(8,128)(2,1)S(1)} %stack.1.mine), channel_id=1, source_target_pairs={{0,16},{16,0},{32,48},{48,32},{64,80},{80,64},{96,112},{112,96},{1... | collective-permute-start | bytes 1105928 | tf_op jit(solution)/shard_map/ppermute | solution.py:574
where the time goes:
time: 135 us; the launch traced here: 134 us
  starting transfers between devices  75 us (56%)
  waiting for transfers between devices  41.3 us (31%)
  Pallas kernels  16.4 us (12%)
    ppermute x3, starting transfers between devices, to_far(): return lax.ppermute(block, 'tm', [(i, i ^ 8) for i in range(16)])  20.1 us
    ppermute x5, starting transfers between devices, to_core(): return lax.ppermute(block, 'tm', [(i, i ^ 1) for i in range(16)])  19.7 us
    ppermute x9, waiting for transfers between devices, along_x(): lax.ppermute(block, 'dp', [(i, i & 12 | i + k & 3) for i in range(16)])  18.8 us
    ppermute x18, starting transfers between devices, along_y(): lax.ppermute(block, 'tm', [(i, i & 9 | i + 2 * k & 6) for i in range(16)])  18.6 us
    ppermute x18, waiting for transfers between devices, along_y(): lax.ppermute(block, 'tm', [(i, i & 9 | i + 2 * k & 6) for i in range(16)])  11.6 us
    ppermute x9, starting transfers between devices, along_x(): lax.ppermute(block, 'dp', [(i, i & 12 | i + k & 3) for i in range(16)])  9.61 us
    ppermute x3, starting transfers between devices, around_z(): return lax.ppermute(block, ('tm', 'dp'), route)  6.94 us
    ppermute x5, waiting for transfers between devices, to_core(): return lax.ppermute(block, 'tm', [(i, i ^ 1) for i in range(16)])  4.77 us
  transfers between devices with their start and end apart: 38, of which 24 were waited for; matrix products, arithmetic and copies ran while one was open for 0% of the time, Pallas kernels for 6%

commit v1 on v0

--- a/solution.py
+++ b/solution.py
@@ -86,34 +86,16 @@
     )
 
 
-def halves_kernel(x_ref, keep_ref, send_ref):
+def deal_kernel(x_ref, far_ref, small, loaded, *outs):
+    _, y, _, _ = position()
     z = lax.axis_index("tm") >> 3
-    for a in range(2):
-        keep_ref[a] = x_ref[a, z]
-        send_ref[a] = x_ref[a, 1 - z]
-
-
-def halves(tokens):
-    return call(
-        halves_kernel,
-        (shape((2, 4, 8, D), bf16),) * 2,
-        [VMEM],
-        [],
-        4,
-        "halves",
-        moved=600_000,
-    )(tokens.reshape(2, 2, 4, 8, D))
-
-
-def deal_kernel(keep_ref, far_ref, small, loaded, *outs):
-    _, y, _, _ = position()
     for k in range(4):
         for a in range(2):
-            outs[k][a] = keep_ref[a, (y + k) & 3]
+            outs[k][a] = x_ref[a, z, (y + k) & 3]
             outs[k][2 + a] = far_ref[a, (y + k) & 3]
 
 
-def deal(keep, far, small, loaded):
+def deal(tokens, far, small, loaded):
     return call(
         deal_kernel,
         (shape((4, 8, D), bf16),) * 4,
@@ -122,7 +104,7 @@
         4,
         "deal",
         moved=600_000,
-    )(keep, far, small, loaded)
+    )(tokens, far, small, loaded)
 
 
 def pack_kernel(lens_ref, teacher_ref, ln_ref, og_ref, rh_ref, small):
@@ -609,11 +591,7 @@
     on, back = (along_x, along_y), 3
     halves = (x_half, y_half)
     arrived = [on[i](halves[i][j], 1 if j == 0 else back) for j in range(2) for i in range(2)]
-    plain = []
-    for j in range(2):
-        for i in range(2):
-            block, _ = lax.optimization_barrier((halves[i][2 + j], arrived[2 * j + i]))
-            plain.append(on[i](block, 1 if j == 0 else back))
+    plain = [on[i](halves[i][2 + j], 1 if j == 0 else back) for j in range(2) for i in range(2)]
     own = [halves[i][4 + j] for j in range(2) for i in range(2)]
     sums = relay(arrived, own)
     relayed = [on[i](sums[2 * j + i], 1 if j == 0 else back) for j in range(2) for i in range(2)]
@@ -621,10 +599,11 @@
 
 
 def on_device(tokens, clip_frames, teacher_scores, ln_gain, w_qkv, w_out, out_gain, reward_head):
-    keep, send = halves(tokens[0])
+    tokens = tokens.reshape(2, 2, 4, 8, D)
+    send = lax.dynamic_index_in_dim(tokens, 1 - (lax.axis_index("tm") >> 3), 1, keepdims=False)
     small = pack(clip_frames, teacher_scores[0], ln_gain, out_gain, reward_head.T)
-    wq, wk, loaded = load([(w_qkv, 0), (w_qkv, D)], keep, 44)
-    parts = deal(keep, to_far(send), small, loaded)
+    wq, wk, loaded = load([(w_qkv, 0), (w_qkv, D)], send, 44)
+    parts = deal(tokens, to_far(send), small, loaded)
     wv, wo, loaded = load([(w_qkv, 2 * D), (w_out, None)], parts[0], 42)
     weights = wq, wk, wv, wo
     keep, send = split([parts[0]] + [along_y(parts[k], k) for k in (1, 2, 3)], loaded)

time: 135 us -> 129 us (0.956)
  starting transfers between devices: 75 us -> 71.2 us
  waiting for transfers between devices: 41.3 us -> 39.4 us
    ppermute x9, waiting for transfers between devices: 18.8 us -> 13.3 us  [along_x(): lax.ppermute(block, 'dp', [(i, i & 12 | i + k & 3) for i in range(16)])]
    ppermute x5, starting transfers between devices: 19.7 us -> 15.1 us  [to_core(): return lax.ppermute(block, 'tm', [(i, i ^ 1) for i in range(16)])]
    ppermute x18, waiting for transfers between devices: 11.6 us -> 15.3 us  [along_y(): lax.ppermute(block, 'tm', [(i, i & 9 | i + 2 * k & 6) for i in range(16)])]
    ppermute x18, starting transfers between devices: 18.6 us -> 21.1 us  [along_y(): lax.ppermute(block, 'tm', [(i, i & 9 | i + 2 * k & 6) for i in range(16)])]
    ppermute x9, starting transfers between devices: 9.61 us -> 7.92 us  [along_x(): lax.ppermute(block, 'dp', [(i, i & 12 | i + k & 3) for i in range(16)])]
  transfers between devices with their start and end apart: 38 -> 38, of which waited for: 24 -> 23; matrix products, arithmetic and copies ran while one was open for 0% -> 0% of each run, Pallas kernels for 6% -> 7%
where the time goes in v1:
time: 129 us
  starting transfers between devices  71.2 us (55%)
  waiting for transfers between devices  39.4 us (31%)
  Pallas kernels  16.2 us (13%)
    ppermute x18, starting transfers between devices, along_y(): lax.ppermute(block, 'tm', [(i, i & 9 | i + 2 * k & 6) for i in range(16)])  21.1 us
    ppermute x3, starting transfers between devices, to_far(): return lax.ppermute(block, 'tm', [(i, i ^ 8) for i in range(16)])  20.1 us
    ppermute x18, waiting for transfers between devices, along_y(): lax.ppermute(block, 'tm', [(i, i & 9 | i + 2 * k & 6) for i in range(16)])  15.3 us
    ppermute x5, starting transfers between devices, to_core(): return lax.ppermute(block, 'tm', [(i, i ^ 1) for i in range(16)])  15.1 us
    ppermute x9, waiting for transfers between devices, along_x(): lax.ppermute(block, 'dp', [(i, i & 12 | i + k & 3) for i in range(16)])  13.3 us
    ppermute x9, starting transfers between devices, along_x(): lax.ppermute(block, 'dp', [(i, i & 12 | i + k & 3) for i in range(16)])  7.92 us
    ppermute x3, starting transfers between devices, around_z(): return lax.ppermute(block, ('tm', 'dp'), route)  6.93 us
    ppermute x5, waiting for transfers between devices, to_core(): return lax.ppermute(block, 'tm', [(i, i ^ 1) for i in range(16)])  4.77 us
  transfers between devices with their start and end apart: 38, of which 23 were waited for; matrix products, arithmetic and copies ran while one was open for 0% of the time, Pallas kernels for 7%

profile of v1, /device:TPU:1, one launch (start us, length us, event | category | flops | bytes accessed | tf_op | source)
XLA Modules:
  0.0 128.7 jit_solution(8653324529206038237)
XLA Ops:
  0.6 0.9 dynamic-slice_bitcast_fusion.refs_2_
  1.7 7.8 %collective-permute-start = (bf16[2,4,8,1152]{3,2,1,0:T(8,128)(2,1)S(1)}, bf16[2,4,8,1152]{3,2,1,0:T(8,128)(2,1)S(1)}, u32[]{:S(2)}, u32[]{:S(2)}) collective-permute-start(bf16[2,4,8,1152]{3,2,1,0:T(8,128)(2,1)S(1)} %dynamic-slice_bitcast_fusion.refs_2_), channel_id=1, source_target_pairs={{0,128},{16,144},{32,160},{48,176},{64,192},{80,208},{96,224},{112... | collective-permute-start | bytes 442376 | tf_op jit(solution)/shard_map/ppermute | solution.py:560
  9.5 2.6 %load.2 = (bf16[1152,1152]{1,0:T(8,128)(2,1)S(1)}, bf16[1152,1152]{1,0:T(8,128)(2,1)S(1)}, f32[8,128]{1,0:T(8,128)S(1)}) custom-call(bf16[1152,3456]{1,0:T(8,128)(2,1)} %refs_0_.3, bf16[1152,3456]{1,0:T(8,128)(2,1)} %refs_0_.3, bf16[2,4,8,1152]{3,2,1,0:T(8,128)(2,1)S(1)} %dynamic-slice_bitcast_fusion.refs_2_), custom_call_target="tpu_custom_call" | custom-call | bytes 10000000 | tf_op jit(solution)/shard_map/load/pallas_call | solution.py:172
  12.2 0.3 collective-permute-done.far_ref
  12.5 1.9 %collective-permute-start.1 = (bf16[4,8,1152]{2,1,0:T(8,128)(2,1)S(1)}, bf16[4,8,1152]{2,1,0:T(8,128)(2,1)S(1)}, u32[]{:S(2)}, u32[]{:S(2)}) collective-permute-start(bf16[4,8,1152]{2,1,0:T(8,128)(2,1)S(1)} %get-tuple-element.64), channel_id=1, source_target_pairs={{0,32},{16,48},{32,64},{48,80},{64,96},{80,112},{96,0},{112,16},{1... | collective-permute-start | bytes 221192 | tf_op jit(solution)/shard_map/ppermute | solution.py:564
  14.5 2.6 %collective-permute-start.2 = (bf16[4,8,1152]{2,1,0:T(8,128)(2,1)S(1)}, bf16[4,8,1152]{2,1,0:T(8,128)(2,1)S(1)}, u32[]{:S(2)}, u32[]{:S(2)}) collective-permute-start(bf16[4,8,1152]{2,1,0:T(8,128)(2,1)S(1)} %get-tuple-element.65), channel_id=1, source_target_pairs={{0,64},{16,80},{32,96},{48,112},{64,0},{80,16},{96,32},{112,48},{1... | collective-permute-start | bytes 221192 | tf_op jit(solution)/shard_map/ppermute | solution.py:564
  17.1 1.1 collective-permute-start.3
  18.1 1.8 %load.3 = (bf16[1152,1152]{1,0:T(8,128)(2,1)S(1)}, bf16[1152,1152]{1,0:T(8,128)(2,1)S(1)}, f32[8,128]{1,0:T(8,128)S(1)}) custom-call(bf16[1152,3456]{1,0:T(8,128)(2,1)} %refs_0_.3, bf16[1152,1152]{1,0:T(8,128)(2,1)S(1)} %copy-done, bf16[4,8,1152]{2,1,0:T(8,128)(2,1)S(1)} %get-tuple-element.62.refs_2_.refs_0_), custom_call_target="tpu_custom_call" | custom-call | bytes 10000000 | tf_op jit(solution)/shard_map/load/pallas_call | solution.py:172
  19.9 1.4 %collective-permute-done.3.refs_3_ = bf16[4,8,1152]{2,1,0:T(8,128)(2,1)S(1)} collective-permute-done((bf16[4,8,1152]{2,1,0:T(8,128)(2,1)S(1)}, bf16[4,8,1152]{2,1,0:T(8,128)(2,1)S(1)}, u32[]{:S(2)}, u32[]{:S(2)}) %collective-permute-start.3) | collective-permute-done | bytes 73760 | tf_op jit(solution)/shard_map/ppermute | solution.py:564
  21.4 2.1 %collective-permute-start.4 = (bf16[8,8,1152]{2,1,0:T(8,128)(2,1)S(1)}, bf16[8,8,1152]{2,1,0:T(8,128)(2,1)S(1)}, u32[]{:S(2)}, u32[]{:S(2)}) collective-permute-start(bf16[8,8,1152]{2,1,0:T(8,128)(2,1)S(1)} %get-tuple-element.68), channel_id=1, source_target_pairs={{0,16},{16,0},{32,48},{48,32},{64,80},{80,64},{96,112},{112,96},{1... | collective-permute-start | bytes 442376 | tf_op jit(solution)/shard_map/ppermute | solution.py:556
  23.5 1.0 collective-permute-done.4.x1
  24.5 3.8 %forward.1 = (bf16[128,1152]{1,0:T(8,128)(2,1)S(1)}, bf16[128,1152]{1,0:T(8,128)(2,1)S(1)}, bf16[128,3456]{1,0:T(8,128)(2,1)S(1)}, f32[16,128,128]{2,1,0:T(8,128...) custom-call(bf16[8,8,1152]{2,1,0:T(8,128)(2,1)S(1)} %get-tuple-element.67.x0, ...), custom_call_target="tpu_custom_call" | custom-call | flops 2000000000 | bytes 14000000 | tf_op jit(solution)/shard_map/forward/pallas_call | solution.py:241
  28.3 0.4 collective-permute-start.5
  28.7 0.8 collective-permute-done.5.b
  29.5 7.7 %collective-permute-start.6 = (f32[8,8]{1,0:T(8,128)S(1)}, f32[8,8]{1,0:T(8,128)S(1)}, u32[]{:S(2)}, u32[]{:S(2)}) collective-permute-start(f32[8,8]{1,0:T(8,128)S(1)} %pair_sum.2.a), channel_id=1, source_target_pairs={{0,128},{16,144},{32,160},{48,176},{64,192},{80,208},{96,224},{112... | collective-permute-start | bytes 776 | tf_op jit(solution)/shard_map/ppermute | solution.py:560
  37.2 0.5 turn.1
  37.7 0.5 collective-permute-done.6.b
  38.2 2.3 %collective-permute-start.9 = (f32[8,8]{1,0:T(8,128)S(1)}, f32[8,8]{1,0:T(8,128)S(1)}, u32[]{:S(2)}, u32[]{:S(2)}) collective-permute-start(f32[8,8]{1,0:T(8,128)S(1)} %pair_sum.3.t0), channel_id=1, source_target_pairs={{0,96},{16,112},{32,0},{48,16},{64,32},{80,48},{96,64},{112,80},{1... | collective-permute-start | bytes 776 | tf_op jit(solution)/shard_map/ppermute | solution.py:564
  40.5 0.6 collective-permute-start.7
  41.1 1.8 %collective-permute-start.10 = (bf16[2,1152,128]{2,1,0:T(8,128)(2,1)S(1)}, bf16[2,1152,128]{2,1,0:T(8,128)(2,1)S(1)}, u32[]{:S(2)}, u32[]{:S(2)}) collective-permute-start(bf16[2,1152,128]{2,1,0:T(8,128)(2,1)S(1)} %get-tuple-element.84), channel_id=1, source_target_pairs={{0,16},{16,0},{32,48},{48,32},{64,80},{80,64},{96,112},{112,96},{1... | collective-permute-start | bytes 1769480 | tf_op jit(solution)/shard_map/ppermute | solution.py:556
  42.9 1.6 %collective-permute-done.8.t2 = f32[8,8]{1,0:T(8,128)S(1)} collective-permute-done((f32[8,8]{1,0:T(8,128)S(1)}, f32[8,8]{1,0:T(8,128)S(1)}, u32[]{:S(2)}, u32[]{:S(2)}) %collective-permute-start.8) | collective-permute-done | bytes 288 | tf_op jit(solution)/shard_map/ppermute | solution.py:564
  44.5 3.3 %backward.1 = (f32[4,8]{1,0:T(4,128)}, bf16[2,128,1152]{2,1,0:T(8,128)(2,1)S(1)}, bf16[2,128,1152]{2,1,0:T(8,128)(2,1)S(1)}) custom-call(f32[8,8]{1,0:T(8,128)S(1)} %pair_sum.3.t0, f32[8,8]{1,0:T(8,128)S(1)} %collective-permute-done.7.t1, f32[8,8]{1,0:T(8,128)S(1)} %collective-permute-done.8.t2, f32[8,8]{1,0:T(8,128)S(1)} %collective-permute-done.9.t3, ...), custom_call_target="tpu_custom_call" | custom-call | flops 1500000000 | bytes 8000000 | tf_op jit(solution)/shard_map/backward/pallas_call | solution.py:363
  47.8 2.6 %collective-permute-start.11 = (bf16[2,128,1152]{2,1,0:T(8,128)(2,1)S(1)}, bf16[2,128,1152]{2,1,0:T(8,128)(2,1)S(1)}, u32[]{:S(2)}, u32[]{:S(2)}) collective-permute-start(bf16[2,128,1152]{2,1,0:T(8,128)(2,1)S(1)} %get-tuple-element.86), channel_id=1, source_target_pairs={{0,16},{16,0},{32,48},{48,32},{64,80},{80,64},{96,112},{112,96},{1... | collective-permute-start | bytes 1769480 | tf_op jit(solution)/shard_map/ppermute | solution.py:556
  50.4 1.6 %collective-permute-done.11.rr = bf16[2,128,1152]{2,1,0:T(8,128)(2,1)S(1)} collective-permute-done((bf16[2,128,1152]{2,1,0:T(8,128)(2,1)S(1)}, bf16[2,128,1152]{2,1,0:T(8,128)(2,1)S(1)}, u32[]{:S(2)}, u32[]{:S(2)}) %collective-permute-start.11) | collective-permute-done | bytes 589856 | tf_op jit(solution)/shard_map/ppermute | solution.py:556
  52.0 1.7 %gradient.1 = (bf16[144,1152]{1,0:T(8,128)(2,1)S(1)}, bf16[144,1152]{1,0:T(8,128)(2,1)S(1)}, bf16[144,1152]{1,0:T(8,128)(2,1)S(1)}, bf16[144,1152]{1,0:T(8,128)(...) custom-call(bf16[2,1152,128]{2,1,0:T(8,128)(2,1)S(1)} %get-tuple-ele, ...), custom_call_target="tpu_custom_call" | custom-call | flops 1400000000 | bytes 8000000 | tf_op jit(solution)/shard_map/gradient/pallas_call | solution.py:402
  53.7 1.3 %collective-permute-start.16 = (bf16[144,1152]{1,0:T(8,128)(2,1)S(1)}, bf16[144,1152]{1,0:T(8,128)(2,1)S(1)}, u32[]{:S(2)}, u32[]{:S(2)}) collective-permute-start(bf16[144,1152]{1,0:T(8,128)(2,1)S(1)} %get-tuple-element.91), channel_id=1, source_target_pairs={{0,1},{1,2},{2,3},{3,0},{4,5},{5,6},{6,7},{7,4},{8,9},{9,10},{10,1... | collective-permute-start | bytes 995336 | tf_op jit(solution)/shard_map/ppermute | solution.py:568
  55.0 1.5 %collective-permute-start.18 = (bf16[144,1152]{1,0:T(8,128)(2,1)S(1)}, bf16[144,1152]{1,0:T(8,128)(2,1)S(1)}, u32[]{:S(2)}, u32[]{:S(2)}) collective-permute-start(bf16[144,1152]{1,0:T(8,128)(2,1)S(1)} %get-tuple-element.93), channel_id=1, source_target_pairs={{0,3},{1,0},{2,1},{3,2},{4,7},{5,4},{6,5},{7,6},{8,11},{9,8},{10,9... | collective-permute-start | bytes 995336 | tf_op jit(solution)/shard_map/ppermute | solution.py:568
  56.5 2.7 %collective-permute-start.19 = (bf16[144,1152]{1,0:T(8,128)(2,1)S(1)}, bf16[144,1152]{1,0:T(8,128)(2,1)S(1)}, u32[]{:S(2)}, u32[]{:S(2)}) collective-permute-start(bf16[144,1152]{1,0:T(8,128)(2,1)S(1)} %get-tuple-element.94), channel_id=1, source_target_pairs={{0,96},{16,112},{32,0},{48,16},{64,32},{80,48},{96,64},{112,80},{1... | collective-permute-start | bytes 995336 | tf_op jit(solution)/shard_map/ppermute | solution.py:564
  59.2 4.9 %collective-permute-done.16.refs_0_ = bf16[144,1152]{1,0:T(8,128)(2,1)S(1)} collective-permute-done((bf16[144,1152]{1,0:T(8,128)(2,1)S(1)}, bf16[144,1152]{1,0:T(8,128)(2,1)S(1)}, u32[]{:S(2)}, u32[]{:S(2)}) %collective-permute-start.16) | collective-permute-done | bytes 331808 | tf_op jit(solution)/shard_map/ppermute | solution.py:568
  64.0 0.9 collective-permute-done.17.refs_1_
  64.9 1.5 %collective-permute-start.14 = (bf16[144,1152]{1,0:T(8,128)(2,1)S(1)}, bf16[144,1152]{1,0:T(8,128)(2,1)S(1)}, u32[]{:S(2)}, u32[]{:S(2)}) collective-permute-start(bf16[144,1152]{1,0:T(8,128)(2,1)S(1)} %get-tuple-element.89), channel_id=1, source_target_pairs={{0,3},{1,0},{2,1},{3,2},{4,7},{5,4},{6,5},{7,6},{8,11},{9,8},{10,9... | collective-permute-start | bytes 995336 | tf_op jit(solution)/shard_map/ppermute | solution.py:568
  66.4 1.6 %collective-permute-start.15 = (bf16[144,1152]{1,0:T(8,128)(2,1)S(1)}, bf16[144,1152]{1,0:T(8,128)(2,1)S(1)}, u32[]{:S(2)}, u32[]{:S(2)}) collective-permute-start(bf16[144,1152]{1,0:T(8,128)(2,1)S(1)} %get-tuple-element.90), channel_id=1, source_target_pairs={{0,96},{16,112},{32,0},{48,16},{64,32},{80,48},{96,64},{112,80},{1... | collective-permute-start | bytes 995336 | tf_op jit(solution)/shard_map/ppermute | solution.py:564
  68.0 0.3 relay.1
  68.3 0.3 collective-permute-start.20
  68.6 2.6 %collective-permute-done.12.refs_0_ = bf16[144,1152]{1,0:T(8,128)(2,1)S(1)} collective-permute-done((bf16[144,1152]{1,0:T(8,128)(2,1)S(1)}, bf16[144,1152]{1,0:T(8,128)(2,1)S(1)}, u32[]{:S(2)}, u32[]{:S(2)}) %collective-permute-start.12) | collective-permute-done | bytes 331808 | tf_op jit(solution)/shard_map/ppermute | solution.py:568
  71.1 1.4 %collective-permute-done.13.refs_1_ = bf16[144,1152]{1,0:T(8,128)(2,1)S(1)} collective-permute-done((bf16[144,1152]{1,0:T(8,128)(2,1)S(1)}, bf16[144,1152]{1,0:T(8,128)(2,1)S(1)}, u32[]{:S(2)}, u32[]{:S(2)}) %collective-permute-start.13) | collective-permute-done | bytes 331808 | tf_op jit(solution)/shard_map/ppermute | solution.py:564
  72.5 1.3 %collective-permute-start.22 = (bf16[144,1152]{1,0:T(8,128)(2,1)S(1)}, bf16[144,1152]{1,0:T(8,128)(2,1)S(1)}, u32[]{:S(2)}, u32[]{:S(2)}) collective-permute-start(bf16[144,1152]{1,0:T(8,128)(2,1)S(1)} %get-tuple-element.101), channel_id=1, source_target_pairs={{0,3},{1,0},{2,1},{3,2},{4,7},{5,4},{6,5},{7,6},{8,11},{9,8},{10,9... | collective-permute-start | bytes 995336 | tf_op jit(solution)/shard_map/ppermute | solution.py:568
  73.8 1.3 %collective-permute-start.23 = (bf16[144,1152]{1,0:T(8,128)(2,1)S(1)}, bf16[144,1152]{1,0:T(8,128)(2,1)S(1)}, u32[]{:S(2)}, u32[]{:S(2)}) collective-permute-start(bf16[144,1152]{1,0:T(8,128)(2,1)S(1)} %get-tuple-element.102), channel_id=1, source_target_pairs={{0,96},{16,112},{32,0},{48,16},{64,32},{80,48},{96,64},{112,80},{1... | collective-permute-start | bytes 995336 | tf_op jit(solution)/shard_map/ppermute | solution.py:564
  75.1 0.9 collective-permute-done.20.refs_4_
  76.1 4.4 %collective-permute-done.21.refs_5_ = bf16[144,1152]{1,0:T(8,128)(2,1)S(1)} collective-permute-done((bf16[144,1152]{1,0:T(8,128)(2,1)S(1)}, bf16[144,1152]{1,0:T(8,128)(2,1)S(1)}, u32[]{:S(2)}, u32[]{:S(2)}) %collective-permute-start.21) | collective-permute-done | bytes 331808 | tf_op jit(solution)/shard_map/ppermute | solution.py:564
  80.4 0.5 first_sum.1
  81.3 3.4 %collective-permute-start.26 = (bf16[72,1152]{1,0:T(8,128)(2,1)S(1)}, bf16[72,1152]{1,0:T(8,128)(2,1)S(1)}, u32[]{:S(2)}, u32[]{:S(2)}) collective-permute-start(bf16[72,1152]{1,0:T(8,128)(2,1)S(1)} %get-tuple-element.109), channel_id=1, source_target_pairs={{0,96},{16,112},{32,0},{48,16},{64,32},{80,48},{96,64},{112,80},{1... | collective-permute-start | bytes 497672 | tf_op jit(solution)/shard_map/ppermute | solution.py:564
  84.7 1.7 %collective-permute-start.27 = (bf16[72,1152]{1,0:T(8,128)(2,1)S(1)}, bf16[72,1152]{1,0:T(8,128)(2,1)S(1)}, u32[]{:S(2)}, u32[]{:S(2)}) collective-permute-start(bf16[72,1152]{1,0:T(8,128)(2,1)S(1)} %get-tuple-element.110), channel_id=1, source_target_pairs={{0,3},{1,0},{2,1},{3,2},{4,7},{5,4},{6,5},{7,6},{8,11},{9,8},{10,9... | collective-permute-start | bytes 497672 | tf_op jit(solution)/shard_map/ppermute | solution.py:568
  86.4 0.3 collective-permute-start.28
  86.7 0.9 collective-permute-start.29
  87.6 2.9 %collective-permute-done.27.refs_5_ = bf16[72,1152]{1,0:T(8,128)(2,1)S(1)} collective-permute-done((bf16[72,1152]{1,0:T(8,128)(2,1)S(1)}, bf16[72,1152]{1,0:T(8,128)(2,1)S(1)}, u32[]{:S(2)}, u32[]{:S(2)}) %collective-permute-start.27) | collective-permute-done | bytes 165920 | tf_op jit(solution)/shard_map/ppermute | solution.py:568
  90.5 2.0 %collective-permute-done.28.refs_6_ = bf16[72,1152]{1,0:T(8,128)(2,1)S(1)} collective-permute-done((bf16[72,1152]{1,0:T(8,128)(2,1)S(1)}, bf16[72,1152]{1,0:T(8,128)(2,1)S(1)}, u32[]{:S(2)}, u32[]{:S(2)}) %collective-permute-start.28) | collective-permute-done | bytes 165920 | tf_op jit(solution)/shard_map/ppermute | solution.py:568
  92.5 0.7 collective-permute-done.29.refs_7_
  93.2 0.2 second_sum.1
  93.5 1.8 %collective-permute-start.30 = (bf16[40,1152]{1,0:T(8,128)(2,1)S(1)}, bf16[40,1152]{1,0:T(8,128)(2,1)S(1)}, u32[]{:S(2)}, u32[]{:S(2)}) collective-permute-start(bf16[40,1152]{1,0:T(8,128)(2,1)S(1)} %get-tuple-element.114), channel_id=1, source_target_pairs={{0,4},{1,5},{2,6},{3,7},{4,8},{5,9},{6,10},{7,11},{8,12},{9,13},{1... | collective-permute-start | bytes 276488 | tf_op jit(solution)/shard_map/ppermute | solution.py:579
  95.3 3.7 %collective-permute-start.31 = (bf16[40,1152]{1,0:T(8,128)(2,1)S(1)}, bf16[40,1152]{1,0:T(8,128)(2,1)S(1)}, u32[]{:S(2)}, u32[]{:S(2)}) collective-permute-start(bf16[40,1152]{1,0:T(8,128)(2,1)S(1)} %get-tuple-element.115), channel_id=1, source_target_pairs={{0,8},{1,9},{2,10},{3,11},{4,12},{5,13},{6,14},{7,15},{8,128},{9,1... | collective-permute-start | bytes 276488 | tf_op jit(solution)/shard_map/ppermute | solution.py:579
  99.0 1.4 %collective-permute-start.32 = (bf16[40,1152]{1,0:T(8,128)(2,1)S(1)}, bf16[40,1152]{1,0:T(8,128)(2,1)S(1)}, u32[]{:S(2)}, u32[]{:S(2)}) collective-permute-start(bf16[40,1152]{1,0:T(8,128)(2,1)S(1)} %get-tuple-element.116), channel_id=1, source_target_pairs={{0,140},{1,141},{2,142},{3,143},{4,0},{5,1},{6,2},{7,3},{8,4},{9,5... | collective-permute-start | bytes 276488 | tf_op jit(solution)/shard_map/ppermute | solution.py:579
  100.4 0.5 collective-permute-done.31.refs_2_
  100.9 1.6 %collective-permute-done.32.refs_3_ = bf16[40,1152]{1,0:T(8,128)(2,1)S(1)} collective-permute-done((bf16[40,1152]{1,0:T(8,128)(2,1)S(1)}, bf16[40,1152]{1,0:T(8,128)(2,1)S(1)}, u32[]{:S(2)}, u32[]{:S(2)}) %collective-permute-start.32) | collective-permute-done | bytes 92192 | tf_op jit(solution)/shard_map/ppermute | solution.py:579
  102.5 4.6 %collective-permute-start.33 = (bf16[40,1152]{1,0:T(8,128)(2,1)S(1)}, bf16[40,1152]{1,0:T(8,128)(2,1)S(1)}, u32[]{:S(2)}, u32[]{:S(2)}) collective-permute-start(bf16[40,1152]{1,0:T(8,128)(2,1)S(1)} %plain_sum.2.refs_0_), channel_id=1, source_target_pairs={{0,128},{16,144},{32,160},{48,176},{64,192},{80,208},{96,224},{112... | collective-permute-start | bytes 276488 | tf_op jit(solution)/shard_map/ppermute | solution.py:560
  107.0 3.1 %collective-permute-done.33.refs_1_ = bf16[40,1152]{1,0:T(8,128)(2,1)S(1)} collective-permute-done((bf16[40,1152]{1,0:T(8,128)(2,1)S(1)}, bf16[40,1152]{1,0:T(8,128)(2,1)S(1)}, u32[]{:S(2)}, u32[]{:S(2)}) %collective-permute-start.33) | collective-permute-done | bytes 92192 | tf_op jit(solution)/shard_map/ppermute | solution.py:560
  110.2 1.9 %collective-permute-start.36 = (bf16[40,1152]{1,0:T(8,128)(2,1)S(1)}, bf16[40,1152]{1,0:T(8,128)(2,1)S(1)}, u32[]{:S(2)}, u32[]{:S(2)}) collective-permute-start(bf16[40,1152]{1,0:T(8,128)(2,1)S(1)} %plain_sum.3.refs_0_), channel_id=1, source_target_pairs={{0,96},{16,112},{32,0},{48,16},{64,32},{80,48},{96,64},{112,80},{1... | collective-permute-start | bytes 276488 | tf_op jit(solution)/shard_map/ppermute | solution.py:564
  112.2 0.7 collective-permute-start.34
  112.8 1.8 %collective-permute-done.36.refs_3_ = bf16[40,1152]{1,0:T(8,128)(2,1)S(1)} collective-permute-done((bf16[40,1152]{1,0:T(8,128)(2,1)S(1)}, bf16[40,1152]{1,0:T(8,128)(2,1)S(1)}, u32[]{:S(2)}, u32[]{:S(2)}) %collective-permute-start.36) | collective-permute-done | bytes 92192 | tf_op jit(solution)/shard_map/ppermute | solution.py:564
  114.6 2.5 %collective-permute-done.35.refs_2_ = bf16[40,1152]{1,0:T(8,128)(2,1)S(1)} collective-permute-done((bf16[40,1152]{1,0:T(8,128)(2,1)S(1)}, bf16[40,1152]{1,0:T(8,128)(2,1)S(1)}, u32[]{:S(2)}, u32[]{:S(2)}) %collective-permute-start.35) | collective-permute-done | bytes 92192 | tf_op jit(solution)/shard_map/ppermute | solution.py:564
  117.2 0.6 collective-permute-done.34.refs_1_
  117.8 8.3 %collective-permute-start.37 = (bf16[4,40,1152]{2,1,0:T(8,128)(2,1)S(1)}, bf16[4,40,1152]{2,1,0:T(8,128)(2,1)S(1)}, u32[]{:S(2)}, u32[]{:S(2)}) collective-permute-start(bf16[4,40,1152]{2,1,0:T(8,128)(2,1)S(1)} %stack.1.mine), channel_id=1, source_target_pairs={{0,16},{16,0},{32,48},{48,32},{64,80},{80,64},{96,112},{112,96},{1... | collective-permute-start | bytes 1105928 | tf_op jit(solution)/shard_map/ppermute | solution.py:556
  126.0 1.3 %collective-permute-done.37.other = bf16[4,40,1152]{2,1,0:T(8,128)(2,1)S(1)} collective-permute-done((bf16[4,40,1152]{2,1,0:T(8,128)(2,1)S(1)}, bf16[4,40,1152]{2,1,0:T(8,128)(2,1)S(1)}, u32[]{:S(2)}, u32[]{:S(2)}) %collective-permute-start.37) | collective-permute-done | bytes 368672 | tf_op jit(solution)/shard_map/ppermute | solution.py:556
  127.4 1.3 %last.1 = (f32[72,3456]{1,0:T(8,128)}, f32[72,1152]{1,0:T(8,128)}) custom-call(bf16[4,40,1152]{2,1,0:T(8,128)(2,1)S(1)} %stack.1.mine, bf16[4,40,1152]{2,1,0:T(8,128)(2,1)S(1)} %collective-permute-done.37.other), custom_call_target="tpu_custom_call" | custom-call | bytes 2000000 | tf_op jit(solution)/shard_map/last/pallas_call | solution.py:544
  (45 shorter events, 0.8 us)
Async XLA Ops:
  1.6 10.5 %copy-start.2 = (f32[1152,8]{0,1:T(8,128)S(1)}, f32[1152,8]{0,1:T(8,128)}, u32[]{:S(2)}) copy-start(f32[1152,8]{0,1:T(8,128)} %param.15) | copy-start | bytes 110596
  1.6 10.5 %copy-start.3 = (f32[1152]{0:T(1024)S(1)}, f32[1152]{0:T(1024)}, u32[]{:S(2)}) copy-start(f32[1152]{0:T(1024)} %ln_ref.1) | copy-start | bytes 13828
  1.6 10.5 %copy-start.4 = (f32[1152]{0:T(1024)S(1)}, f32[1152]{0:T(1024)}, u32[]{:S(2)}) copy-start(f32[1152]{0:T(1024)} %og_ref.1) | copy-start | bytes 13828
  1.6 10.5 %copy-start.5 = (f32[1,4,8]{2,1,0:T(4,128)S(1)}, f32[1,4,8]{2,1,0:T(4,128)}, u32[]{:S(2)}) copy-start(f32[1,4,8]{2,1,0:T(4,128)} %param.10) | copy-start | bytes 388
  1.6 10.5 %copy-start.6 = (s32[1,4]{1,0:T(1,128)S(1)}, s32[1,4]{1,0:T(1,128)}, u32[]{:S(2)}) copy-start(s32[1,4]{1,0:T(1,128)} %lens_ref.1) | copy-start | bytes 52
  1.6 10.9 %copy-start.1 = (bf16[1,2,64,1152]{3,2,1,0:T(8,128)(2,1)S(1)}, bf16[1,2,64,1152]{3,2,1,0:T(8,128)(2,1)}, u32[]{:S(2)}) copy-start(bf16[1,2,64,1152]{3,2,1,0:T(8,128)(2,1)} %param.8) | copy-start | bytes 884740
  1.6 16.5 %copy-start = (bf16[1152,1152]{1,0:T(8,128)(2,1)S(1)}, bf16[1152,1152]{1,0:T(8,128)(2,1)}, u32[]{:S(2)}) copy-start(bf16[1152,1152]{1,0:T(8,128)(2,1)} %refs_1_.3) | copy-start | bytes 7962628
  1.7 10.9 %collective-permute-start = (bf16[2,4,8,1152]{3,2,1,0:T(8,128)(2,1)S(1)}, bf16[2,4,8,1152]{3,2,1,0:T(8,128)(2,1)S(1)}, u32[]{:S(2)}, u32[]{:S(2)}) collective-permute-start(bf16[2,4,8,1152]{3,2,1,0:T(8,128)(2,1)S(1)} %dynamic-slice_bitcast_fusion.refs_2_), channel_id=1, source_target_pairs={{0,128},{16,144},{32,160},{48,176},{64,192},{80,208},{96,224},{112... | collective-permute-start | bytes 442376 | tf_op jit(solution)/shard_map/ppermute | solution.py:560
  12.5 7.4 %collective-permute-start.1 = (bf16[4,8,1152]{2,1,0:T(8,128)(2,1)S(1)}, bf16[4,8,1152]{2,1,0:T(8,128)(2,1)S(1)}, u32[]{:S(2)}, u32[]{:S(2)}) collective-permute-start(bf16[4,8,1152]{2,1,0:T(8,128)(2,1)S(1)} %get-tuple-element.64), channel_id=1, source_target_pairs={{0,32},{16,48},{32,64},{48,80},{64,96},{80,112},{96,0},{112,16},{1... | collective-permute-start | bytes 221192 | tf_op jit(solution)/shard_map/ppermute | solution.py:564
  14.5 5.5 %collective-permute-start.2 = (bf16[4,8,1152]{2,1,0:T(8,128)(2,1)S(1)}, bf16[4,8,1152]{2,1,0:T(8,128)(2,1)S(1)}, u32[]{:S(2)}, u32[]{:S(2)}) collective-permute-start(bf16[4,8,1152]{2,1,0:T(8,128)(2,1)S(1)} %get-tuple-element.65), channel_id=1, source_target_pairs={{0,64},{16,80},{32,96},{48,112},{64,0},{80,16},{96,32},{112,48},{1... | collective-permute-start | bytes 221192 | tf_op jit(solution)/shard_map/ppermute | solution.py:564
  17.1 4.2 %collective-permute-start.3 = (bf16[4,8,1152]{2,1,0:T(8,128)(2,1)S(1)}, bf16[4,8,1152]{2,1,0:T(8,128)(2,1)S(1)}, u32[]{:S(2)}, u32[]{:S(2)}) collective-permute-start(bf16[4,8,1152]{2,1,0:T(8,128)(2,1)S(1)} %get-tuple-element.66), channel_id=1, source_target_pairs={{0,96},{16,112},{32,0},{48,16},{64,32},{80,48},{96,64},{112,80},{1... | collective-permute-start | bytes 221192 | tf_op jit(solution)/shard_map/ppermute | solution.py:564
  21.4 3.1 %collective-permute-start.4 = (bf16[8,8,1152]{2,1,0:T(8,128)(2,1)S(1)}, bf16[8,8,1152]{2,1,0:T(8,128)(2,1)S(1)}, u32[]{:S(2)}, u32[]{:S(2)}) collective-permute-start(bf16[8,8,1152]{2,1,0:T(8,128)(2,1)S(1)} %get-tuple-element.68), channel_id=1, source_target_pairs={{0,16},{16,0},{32,48},{48,32},{64,80},{80,64},{96,112},{112,96},{1... | collective-permute-start | bytes 442376 | tf_op jit(solution)/shard_map/ppermute | solution.py:556
  28.3 1.2 collective-permute-start.5
  29.5 8.7 %collective-permute-start.6 = (f32[8,8]{1,0:T(8,128)S(1)}, f32[8,8]{1,0:T(8,128)S(1)}, u32[]{:S(2)}, u32[]{:S(2)}) collective-permute-start(f32[8,8]{1,0:T(8,128)S(1)} %pair_sum.2.a), channel_id=1, source_target_pairs={{0,128},{16,144},{32,160},{48,176},{64,192},{80,208},{96,224},{112... | collective-permute-start | bytes 776 | tf_op jit(solution)/shard_map/ppermute | solution.py:560
  38.2 4.6 %collective-permute-start.9 = (f32[8,8]{1,0:T(8,128)S(1)}, f32[8,8]{1,0:T(8,128)S(1)}, u32[]{:S(2)}, u32[]{:S(2)}) collective-permute-start(f32[8,8]{1,0:T(8,128)S(1)} %pair_sum.3.t0), channel_id=1, source_target_pairs={{0,96},{16,112},{32,0},{48,16},{64,32},{80,48},{96,64},{112,80},{1... | collective-permute-start | bytes 776 | tf_op jit(solution)/shard_map/ppermute | solution.py:564
  40.5 4.0 %collective-permute-start.8 = (f32[8,8]{1,0:T(8,128)S(1)}, f32[8,8]{1,0:T(8,128)S(1)}, u32[]{:S(2)}, u32[]{:S(2)}) collective-permute-start(f32[8,8]{1,0:T(8,128)S(1)} %pair_sum.3.t0), channel_id=1, source_target_pairs={{0,64},{16,80},{32,96},{48,112},{64,0},{80,16},{96,32},{112,48},{1... | collective-permute-start | bytes 776 | tf_op jit(solution)/shard_map/ppermute | solution.py:564
  40.5 4.0 %collective-permute-start.7 = (f32[8,8]{1,0:T(8,128)S(1)}, f32[8,8]{1,0:T(8,128)S(1)}, u32[]{:S(2)}, u32[]{:S(2)}) collective-permute-start(f32[8,8]{1,0:T(8,128)S(1)} %pair_sum.3.t0), channel_id=1, source_target_pairs={{0,32},{16,48},{32,64},{48,80},{64,96},{80,112},{96,0},{112,16},{1... | collective-permute-start | bytes 776 | tf_op jit(solution)/shard_map/ppermute | solution.py:564
  41.1 9.3 %collective-permute-start.10 = (bf16[2,1152,128]{2,1,0:T(8,128)(2,1)S(1)}, bf16[2,1152,128]{2,1,0:T(8,128)(2,1)S(1)}, u32[]{:S(2)}, u32[]{:S(2)}) collective-permute-start(bf16[2,1152,128]{2,1,0:T(8,128)(2,1)S(1)} %get-tuple-element.84), channel_id=1, source_target_pairs={{0,16},{16,0},{32,48},{48,32},{64,80},{80,64},{96,112},{112,96},{1... | collective-permute-start | bytes 1769480 | tf_op jit(solution)/shard_map/ppermute | solution.py:556
  47.8 4.3 %collective-permute-start.11 = (bf16[2,128,1152]{2,1,0:T(8,128)(2,1)S(1)}, bf16[2,128,1152]{2,1,0:T(8,128)(2,1)S(1)}, u32[]{:S(2)}, u32[]{:S(2)}) collective-permute-start(bf16[2,128,1152]{2,1,0:T(8,128)(2,1)S(1)} %get-tuple-element.86), channel_id=1, source_target_pairs={{0,16},{16,0},{32,48},{48,32},{64,80},{80,64},{96,112},{112,96},{1... | collective-permute-start | bytes 1769480 | tf_op jit(solution)/shard_map/ppermute | solution.py:556
  53.7 10.3 %collective-permute-start.16 = (bf16[144,1152]{1,0:T(8,128)(2,1)S(1)}, bf16[144,1152]{1,0:T(8,128)(2,1)S(1)}, u32[]{:S(2)}, u32[]{:S(2)}) collective-permute-start(bf16[144,1152]{1,0:T(8,128)(2,1)S(1)} %get-tuple-element.91), channel_id=1, source_target_pairs={{0,1},{1,2},{2,3},{3,0},{4,5},{5,6},{6,7},{7,4},{8,9},{9,10},{10,1... | collective-permute-start | bytes 995336 | tf_op jit(solution)/shard_map/ppermute | solution.py:568
  55.0 9.9 %collective-permute-start.17 = (bf16[144,1152]{1,0:T(8,128)(2,1)S(1)}, bf16[144,1152]{1,0:T(8,128)(2,1)S(1)}, u32[]{:S(2)}, u32[]{:S(2)}) collective-permute-start(bf16[144,1152]{1,0:T(8,128)(2,1)S(1)} %get-tuple-element.92), channel_id=1, source_target_pairs={{0,32},{16,48},{32,64},{48,80},{64,96},{80,112},{96,0},{112,16},{1... | collective-permute-start | bytes 995336 | tf_op jit(solution)/shard_map/ppermute | solution.py:564
  55.0 11.4 %collective-permute-start.18 = (bf16[144,1152]{1,0:T(8,128)(2,1)S(1)}, bf16[144,1152]{1,0:T(8,128)(2,1)S(1)}, u32[]{:S(2)}, u32[]{:S(2)}) collective-permute-start(bf16[144,1152]{1,0:T(8,128)(2,1)S(1)} %get-tuple-element.93), channel_id=1, source_target_pairs={{0,3},{1,0},{2,1},{3,2},{4,7},{5,4},{6,5},{7,6},{8,11},{9,8},{10,9... | collective-permute-start | bytes 995336 | tf_op jit(solution)/shard_map/ppermute | solution.py:568
  56.5 11.5 %collective-permute-start.19 = (bf16[144,1152]{1,0:T(8,128)(2,1)S(1)}, bf16[144,1152]{1,0:T(8,128)(2,1)S(1)}, u32[]{:S(2)}, u32[]{:S(2)}) collective-permute-start(bf16[144,1152]{1,0:T(8,128)(2,1)S(1)} %get-tuple-element.94), channel_id=1, source_target_pairs={{0,96},{16,112},{32,0},{48,16},{64,32},{80,48},{96,64},{112,80},{1... | collective-permute-start | bytes 995336 | tf_op jit(solution)/shard_map/ppermute | solution.py:564
  59.2 12.0 %collective-permute-start.12 = (bf16[144,1152]{1,0:T(8,128)(2,1)S(1)}, bf16[144,1152]{1,0:T(8,128)(2,1)S(1)}, u32[]{:S(2)}, u32[]{:S(2)}) collective-permute-start(bf16[144,1152]{1,0:T(8,128)(2,1)S(1)} %get-tuple-element.87), channel_id=1, source_target_pairs={{0,1},{1,2},{2,3},{3,0},{4,5},{5,6},{6,7},{7,4},{8,9},{9,10},{10,1... | collective-permute-start | bytes 995336 | tf_op jit(solution)/shard_map/ppermute | solution.py:568
  64.0 8.5 %collective-permute-start.13 = (bf16[144,1152]{1,0:T(8,128)(2,1)S(1)}, bf16[144,1152]{1,0:T(8,128)(2,1)S(1)}, u32[]{:S(2)}, u32[]{:S(2)}) collective-permute-start(bf16[144,1152]{1,0:T(8,128)(2,1)S(1)} %get-tuple-element.88), channel_id=1, source_target_pairs={{0,32},{16,48},{32,64},{48,80},{64,96},{80,112},{96,0},{112,16},{1... | collective-permute-start | bytes 995336 | tf_op jit(solution)/shard_map/ppermute | solution.py:564
  64.9 8.9 %collective-permute-start.14 = (bf16[144,1152]{1,0:T(8,128)(2,1)S(1)}, bf16[144,1152]{1,0:T(8,128)(2,1)S(1)}, u32[]{:S(2)}, u32[]{:S(2)}) collective-permute-start(bf16[144,1152]{1,0:T(8,128)(2,1)S(1)} %get-tuple-element.89), channel_id=1, source_target_pairs={{0,3},{1,0},{2,1},{3,2},{4,7},{5,4},{6,5},{7,6},{8,11},{9,8},{10,9... | collective-permute-start | bytes 995336 | tf_op jit(solution)/shard_map/ppermute | solution.py:568
  66.4 8.7 %collective-permute-start.15 = (bf16[144,1152]{1,0:T(8,128)(2,1)S(1)}, bf16[144,1152]{1,0:T(8,128)(2,1)S(1)}, u32[]{:S(2)}, u32[]{:S(2)}) collective-permute-start(bf16[144,1152]{1,0:T(8,128)(2,1)S(1)} %get-tuple-element.90), channel_id=1, source_target_pairs={{0,96},{16,112},{32,0},{48,16},{64,32},{80,48},{96,64},{112,80},{1... | collective-permute-start | bytes 995336 | tf_op jit(solution)/shard_map/ppermute | solution.py:564
  68.3 7.7 %collective-permute-start.20 = (bf16[144,1152]{1,0:T(8,128)(2,1)S(1)}, bf16[144,1152]{1,0:T(8,128)(2,1)S(1)}, u32[]{:S(2)}, u32[]{:S(2)}) collective-permute-start(bf16[144,1152]{1,0:T(8,128)(2,1)S(1)} %get-tuple-element.99), channel_id=1, source_target_pairs={{0,1},{1,2},{2,3},{3,0},{4,5},{5,6},{6,7},{7,4},{8,9},{9,10},{10,1... | collective-permute-start | bytes 995336 | tf_op jit(solution)/shard_map/ppermute | solution.py:568
  71.1 9.3 %collective-permute-start.21 = (bf16[144,1152]{1,0:T(8,128)(2,1)S(1)}, bf16[144,1152]{1,0:T(8,128)(2,1)S(1)}, u32[]{:S(2)}, u32[]{:S(2)}) collective-permute-start(bf16[144,1152]{1,0:T(8,128)(2,1)S(1)} %get-tuple-element.100), channel_id=1, source_target_pairs={{0,32},{16,48},{32,64},{48,80},{64,96},{80,112},{96,0},{112,16},{1... | collective-permute-start | bytes 995336 | tf_op jit(solution)/shard_map/ppermute | solution.py:564
  72.5 7.9 %collective-permute-start.22 = (bf16[144,1152]{1,0:T(8,128)(2,1)S(1)}, bf16[144,1152]{1,0:T(8,128)(2,1)S(1)}, u32[]{:S(2)}, u32[]{:S(2)}) collective-permute-start(bf16[144,1152]{1,0:T(8,128)(2,1)S(1)} %get-tuple-element.101), channel_id=1, source_target_pairs={{0,3},{1,0},{2,1},{3,2},{4,7},{5,4},{6,5},{7,6},{8,11},{9,8},{10,9... | collective-permute-start | bytes 995336 | tf_op jit(solution)/shard_map/ppermute | solution.py:568
  73.8 6.6 %collective-permute-start.23 = (bf16[144,1152]{1,0:T(8,128)(2,1)S(1)}, bf16[144,1152]{1,0:T(8,128)(2,1)S(1)}, u32[]{:S(2)}, u32[]{:S(2)}) collective-permute-start(bf16[144,1152]{1,0:T(8,128)(2,1)S(1)} %get-tuple-element.102), channel_id=1, source_target_pairs={{0,96},{16,112},{32,0},{48,16},{64,32},{80,48},{96,64},{112,80},{1... | collective-permute-start | bytes 995336 | tf_op jit(solution)/shard_map/ppermute | solution.py:564
  80.9 5.7 %collective-permute-start.24 = (bf16[72,1152]{1,0:T(8,128)(2,1)S(1)}, bf16[72,1152]{1,0:T(8,128)(2,1)S(1)}, u32[]{:S(2)}, u32[]{:S(2)}) collective-permute-start(bf16[72,1152]{1,0:T(8,128)(2,1)S(1)} %get-tuple-element.107), channel_id=1, source_target_pairs={{0,32},{16,48},{32,64},{48,80},{64,96},{80,112},{96,0},{112,16},{1... | collective-permute-start | bytes 497672 | tf_op jit(solution)/shard_map/ppermute | solution.py:564
  81.1 6.5 %collective-permute-start.25 = (bf16[72,1152]{1,0:T(8,128)(2,1)S(1)}, bf16[72,1152]{1,0:T(8,128)(2,1)S(1)}, u32[]{:S(2)}, u32[]{:S(2)}) collective-permute-start(bf16[72,1152]{1,0:T(8,128)(2,1)S(1)} %get-tuple-element.108), channel_id=1, source_target_pairs={{0,1},{1,2},{2,3},{3,0},{4,5},{5,6},{6,7},{7,4},{8,9},{9,10},{10,1... | collective-permute-start | bytes 497672 | tf_op jit(solution)/shard_map/ppermute | solution.py:568
  81.3 6.3 %collective-permute-start.26 = (bf16[72,1152]{1,0:T(8,128)(2,1)S(1)}, bf16[72,1152]{1,0:T(8,128)(2,1)S(1)}, u32[]{:S(2)}, u32[]{:S(2)}) collective-permute-start(bf16[72,1152]{1,0:T(8,128)(2,1)S(1)} %get-tuple-element.109), channel_id=1, source_target_pairs={{0,96},{16,112},{32,0},{48,16},{64,32},{80,48},{96,64},{112,80},{1... | collective-permute-start | bytes 497672 | tf_op jit(solution)/shard_map/ppermute | solution.py:564
  84.7 5.8 %collective-permute-start.27 = (bf16[72,1152]{1,0:T(8,128)(2,1)S(1)}, bf16[72,1152]{1,0:T(8,128)(2,1)S(1)}, u32[]{:S(2)}, u32[]{:S(2)}) collective-permute-start(bf16[72,1152]{1,0:T(8,128)(2,1)S(1)} %get-tuple-element.110), channel_id=1, source_target_pairs={{0,3},{1,0},{2,1},{3,2},{4,7},{5,4},{6,5},{7,6},{8,11},{9,8},{10,9... | collective-permute-start | bytes 497672 | tf_op jit(solution)/shard_map/ppermute | solution.py:568
  86.4 6.1 %collective-permute-start.28 = (bf16[72,1152]{1,0:T(8,128)(2,1)S(1)}, bf16[72,1152]{1,0:T(8,128)(2,1)S(1)}, u32[]{:S(2)}, u32[]{:S(2)}) collective-permute-start(bf16[72,1152]{1,0:T(8,128)(2,1)S(1)} %get-tuple-element.111), channel_id=1, source_target_pairs={{0,2},{1,3},{2,0},{3,1},{4,6},{5,7},{6,4},{7,5},{8,10},{9,11},{10,... | collective-permute-start | bytes 497672 | tf_op jit(solution)/shard_map/ppermute | solution.py:568
  86.7 6.6 %collective-permute-start.29 = (bf16[72,1152]{1,0:T(8,128)(2,1)S(1)}, bf16[72,1152]{1,0:T(8,128)(2,1)S(1)}, u32[]{:S(2)}, u32[]{:S(2)}) collective-permute-start(bf16[72,1152]{1,0:T(8,128)(2,1)S(1)} %get-tuple-element.112), channel_id=1, source_target_pairs={{0,64},{16,80},{32,96},{48,112},{64,0},{80,16},{96,32},{112,48},{1... | collective-permute-start | bytes 497672 | tf_op jit(solution)/shard_map/ppermute | solution.py:564
  93.5 6.9 %collective-permute-start.30 = (bf16[40,1152]{1,0:T(8,128)(2,1)S(1)}, bf16[40,1152]{1,0:T(8,128)(2,1)S(1)}, u32[]{:S(2)}, u32[]{:S(2)}) collective-permute-start(bf16[40,1152]{1,0:T(8,128)(2,1)S(1)} %get-tuple-element.114), channel_id=1, source_target_pairs={{0,4},{1,5},{2,6},{3,7},{4,8},{5,9},{6,10},{7,11},{8,12},{9,13},{1... | collective-permute-start | bytes 276488 | tf_op jit(solution)/shard_map/ppermute | solution.py:579
  95.3 5.6 %collective-permute-start.31 = (bf16[40,1152]{1,0:T(8,128)(2,1)S(1)}, bf16[40,1152]{1,0:T(8,128)(2,1)S(1)}, u32[]{:S(2)}, u32[]{:S(2)}) collective-permute-start(bf16[40,1152]{1,0:T(8,128)(2,1)S(1)} %get-tuple-element.115), channel_id=1, source_target_pairs={{0,8},{1,9},{2,10},{3,11},{4,12},{5,13},{6,14},{7,15},{8,128},{9,1... | collective-permute-start | bytes 276488 | tf_op jit(solution)/shard_map/ppermute | solution.py:579
  99.0 3.4 %collective-permute-start.32 = (bf16[40,1152]{1,0:T(8,128)(2,1)S(1)}, bf16[40,1152]{1,0:T(8,128)(2,1)S(1)}, u32[]{:S(2)}, u32[]{:S(2)}) collective-permute-start(bf16[40,1152]{1,0:T(8,128)(2,1)S(1)} %get-tuple-element.116), channel_id=1, source_target_pairs={{0,140},{1,141},{2,142},{3,143},{4,0},{5,1},{6,2},{7,3},{8,4},{9,5... | collective-permute-start | bytes 276488 | tf_op jit(solution)/shard_map/ppermute | solution.py:579
  102.5 7.7 %collective-permute-start.33 = (bf16[40,1152]{1,0:T(8,128)(2,1)S(1)}, bf16[40,1152]{1,0:T(8,128)(2,1)S(1)}, u32[]{:S(2)}, u32[]{:S(2)}) collective-permute-start(bf16[40,1152]{1,0:T(8,128)(2,1)S(1)} %plain_sum.2.refs_0_), channel_id=1, source_target_pairs={{0,128},{16,144},{32,160},{48,176},{64,192},{80,208},{96,224},{112... | collective-permute-start | bytes 276488 | tf_op jit(solution)/shard_map/ppermute | solution.py:560
  110.2 4.4 %collective-permute-start.36 = (bf16[40,1152]{1,0:T(8,128)(2,1)S(1)}, bf16[40,1152]{1,0:T(8,128)(2,1)S(1)}, u32[]{:S(2)}, u32[]{:S(2)}) collective-permute-start(bf16[40,1152]{1,0:T(8,128)(2,1)S(1)} %plain_sum.3.refs_0_), channel_id=1, source_target_pairs={{0,96},{16,112},{32,0},{48,16},{64,32},{80,48},{96,64},{112,80},{1... | collective-permute-start | bytes 276488 | tf_op jit(solution)/shard_map/ppermute | solution.py:564
  112.2 5.0 %collective-permute-start.35 = (bf16[40,1152]{1,0:T(8,128)(2,1)S(1)}, bf16[40,1152]{1,0:T(8,128)(2,1)S(1)}, u32[]{:S(2)}, u32[]{:S(2)}) collective-permute-start(bf16[40,1152]{1,0:T(8,128)(2,1)S(1)} %plain_sum.3.refs_0_), channel_id=1, source_target_pairs={{0,64},{16,80},{32,96},{48,112},{64,0},{80,16},{96,32},{112,48},{1... | collective-permute-start | bytes 276488 | tf_op jit(solution)/shard_map/ppermute | solution.py:564
  112.2 5.6 %collective-permute-start.34 = (bf16[40,1152]{1,0:T(8,128)(2,1)S(1)}, bf16[40,1152]{1,0:T(8,128)(2,1)S(1)}, u32[]{:S(2)}, u32[]{:S(2)}) collective-permute-start(bf16[40,1152]{1,0:T(8,128)(2,1)S(1)} %plain_sum.3.refs_0_), channel_id=1, source_target_pairs={{0,32},{16,48},{32,64},{48,80},{64,96},{80,112},{96,0},{112,16},{1... | collective-permute-start | bytes 276488 | tf_op jit(solution)/shard_map/ppermute | solution.py:564
  117.8 9.6 %collective-permute-start.37 = (bf16[4,40,1152]{2,1,0:T(8,128)(2,1)S(1)}, bf16[4,40,1152]{2,1,0:T(8,128)(2,1)S(1)}, u32[]{:S(2)}, u32[]{:S(2)}) collective-permute-start(bf16[4,40,1152]{2,1,0:T(8,128)(2,1)S(1)} %stack.1.mine), channel_id=1, source_target_pairs={{0,16},{16,0},{32,48},{48,32},{64,80},{80,64},{96,112},{112,96},{1... | collective-permute-start | bytes 1105928 | tf_op jit(solution)/shard_map/ppermute | solution.py:556

commit v2 on v1

--- a/solution.py
+++ b/solution.py
@@ -132,15 +132,15 @@
     )(clip_frames, teacher, ln_gain, out_gain, reward)
 
 
-def split_kernel(loaded, *refs):
+def split_kernel(loaded, r0, r2, r1, r3, keep_ref, send_ref):
     core = position()[3]
     for k in range(4):
         for z in range(2):
-            rows = [refs[k][2 * z + a].astype(f32) for a in range(2)]
+            rows = [(r0, r1, r2, r3)[k][2 * z + a].astype(f32) for a in range(2)]
             low = jnp.concatenate([r[0:4] for r in rows], axis=0)
             high = jnp.concatenate([r[4:8] for r in rows], axis=0)
-            refs[4][2 * k + z] = jnp.where(core == 0, low, high).astype(bf16)
-            refs[5][2 * k + z] = jnp.where(core == 0, high, low).astype(bf16)
+            keep_ref[2 * k + z] = jnp.where(core == 0, low, high).astype(bf16)
+            send_ref[2 * k + z] = jnp.where(core == 0, high, low).astype(bf16)
 
 
 def split(parts, loaded):
@@ -295,7 +295,7 @@
 
 
 def backward_kernel(
-    t0, t1, t2, t3, small, proj_ref, p_ref, cen_ref, inv_ref, wo_ref,
+    t0, t1, t3, t2, small, proj_ref, p_ref, cen_ref, inv_ref, wo_ref,
     scores_ref, keep_ref, send_ref,
     dq, dk, dv, wg, da_ref,
 ):
@@ -436,7 +436,7 @@
     return result
 
 
-SLOT = ((0, 3, 6, 5), (1, 2, 7, 4))
+SLOT = ((0, 5, 3, 7), (1, 4, 2, 6))
 
 
 def first_sum_kernel(*refs):
@@ -516,8 +516,8 @@
 
 
 def stack_kernel(*refs):
-    for k in range(4):
-        refs[4][k] = refs[k][...]
+    for j, k in enumerate((0, 1, 3, 2)):
+        refs[4][k] = refs[j][...]
 
 
 def stack(parts):
@@ -581,7 +581,7 @@
 
 def exchange(slots):
     moved = list(slots)
-    for k in (1, 3, 2):
+    for k in (2, 1, 3):
         moved[SLOT[1][k]] = along_y(slots[SLOT[1][k]], k)
         moved[SLOT[0][k]] = along_x(slots[SLOT[0][k]], k)
     return moved
@@ -606,7 +606,7 @@
     parts = deal(tokens, to_far(send), small, loaded)
     wv, wo, loaded = load([(w_qkv, 2 * D), (w_out, None)], parts[0], 42)
     weights = wq, wk, wv, wo
-    keep, send = split([parts[0]] + [along_y(parts[k], k) for k in (1, 2, 3)], loaded)
+    keep, send = split([parts[0]] + [along_y(parts[k], k) for k in (2, 1, 3)], loaded)
     x = [keep, to_core(send)]
     normed, attended, proj, p, centred, inv, partial = forward(x, weights, small)
     partial = pair_sum(partial, to_core(partial))
@@ -614,13 +614,13 @@
     left_keep, left_send = turn(normed, attended)
     left_recv = to_core(left_send)
     partial = pair_sum(partial, to_far(partial), left_keep)
-    totals = [partial] + [along_y(partial, k) for k in (1, 2, 3)]
+    totals = [partial] + [along_y(partial, k) for k in (1, 3, 2)]
     scores, right_keep, right_send = backward(totals, small, proj, p, centred, inv, weights[3])
     parts = gradient(left_keep, left_recv, right_keep, to_core(right_send))
     parts = second_sum(exchange(around(*parts)))
-    part = plain_sum([parts[0]] + [around_z(parts[k], k) for k in (1, 2, 3)])
+    part = plain_sum([parts[0]] + [around_z(parts[k], k) for k in (2, 1, 3)])
     part = plain_sum([part, to_far(part)])
-    mine = stack([part] + [along_y(part, k) for k in (1, 2, 3)])
+    mine = stack([part] + [along_y(part, k) for k in (1, 3, 2)])
     qkv_total, out_total = last(mine, to_core(mine))
     return (scores[None], qkv_total, out_total)
 

time: 129 us -> 131 us (1.016)
  waiting for transfers between devices: 39.4 us -> 40.9 us
    ppermute x3, starting transfers between devices: 20.1 us -> 16.2 us  [to_far(): return lax.ppermute(block, 'tm', [(i, i ^ 8) for i in range(16)])]
    ppermute x3, waiting for transfers between devices: 3.96 us -> 7.53 us  [to_far(): return lax.ppermute(block, 'tm', [(i, i ^ 8) for i in range(16)])]
    ppermute x18, waiting for transfers between devices: 15.3 us -> 13.5 us  [along_y(): lax.ppermute(block, 'tm', [(i, i & 9 | i + 2 * k & 6) for i in range(16)])]
    ppermute x18, starting transfers between devices: 21.1 us -> 22.4 us  [along_y(): lax.ppermute(block, 'tm', [(i, i & 9 | i + 2 * k & 6) for i in range(16)])]
  transfers between devices with their start and end apart: 38 -> 38, of which waited for: 23 -> 22; matrix products, arithmetic and copies ran while one was open for 0% -> 0% of each run, Pallas kernels for 7% -> 7%
where the time goes in v2:
time: 131 us; the launch traced here: 130 us
  starting transfers between devices  71.5 us (55%)
  waiting for transfers between devices  40.9 us (31%)
  Pallas kernels  16.2 us (12%)
    ppermute x18, starting transfers between devices, along_y(): lax.ppermute(block, 'tm', [(i, i & 9 | i + 2 * k & 6) for i in range(16)])  22.4 us
    ppermute x3, starting transfers between devices, to_far(): return lax.ppermute(block, 'tm', [(i, i ^ 8) for i in range(16)])  16.2 us
    ppermute x5, starting transfers between devices, to_core(): return lax.ppermute(block, 'tm', [(i, i ^ 1) for i in range(16)])  16.1 us
    ppermute x18, waiting for transfers between devices, along_y(): lax.ppermute(block, 'tm', [(i, i & 9 | i + 2 * k & 6) for i in range(16)])  13.5 us
    ppermute x9, waiting for transfers between devices, along_x(): lax.ppermute(block, 'dp', [(i, i & 12 | i + k & 3) for i in range(16)])  12.7 us
    ppermute x9, starting transfers between devices, along_x(): lax.ppermute(block, 'dp', [(i, i & 12 | i + k & 3) for i in range(16)])  8.58 us
    ppermute x3, starting transfers between devices, around_z(): return lax.ppermute(block, ('tm', 'dp'), route)  8.14 us
    ppermute x3, waiting for transfers between devices, to_far(): return lax.ppermute(block, 'tm', [(i, i ^ 8) for i in range(16)])  7.53 us
  transfers between devices with their start and end apart: 38, of which 22 were waited for; matrix products, arithmetic and copies ran while one was open for 0% of the time, Pallas kernels for 7%

profile of v2, /device:TPU:1, one launch (start us, length us, event | category | flops | bytes accessed | tf_op | source)
XLA Modules:
  0.0 130.4 jit_solution(16947899119538934988)
XLA Ops:
  0.6 0.9 dynamic-slice_bitcast_fusion.refs_2_
  1.7 7.8 %collective-permute-start = (bf16[2,4,8,1152]{3,2,1,0:T(8,128)(2,1)S(1)}, bf16[2,4,8,1152]{3,2,1,0:T(8,128)(2,1)S(1)}, u32[]{:S(2)}, u32[]{:S(2)}) collective-permute-start(bf16[2,4,8,1152]{3,2,1,0:T(8,128)(2,1)S(1)} %dynamic-slice_bitcast_fusion.refs_2_), channel_id=1, source_target_pairs={{0,128},{16,144},{32,160},{48,176},{64,192},{80,208},{96,224},{112... | collective-permute-start | bytes 442376 | tf_op jit(solution)/shard_map/ppermute | solution.py:560
  9.5 2.6 %load.2 = (bf16[1152,1152]{1,0:T(8,128)(2,1)S(1)}, bf16[1152,1152]{1,0:T(8,128)(2,1)S(1)}, f32[8,128]{1,0:T(8,128)S(1)}) custom-call(bf16[1152,3456]{1,0:T(8,128)(2,1)} %refs_0_.3, bf16[1152,3456]{1,0:T(8,128)(2,1)} %refs_0_.3, bf16[2,4,8,1152]{3,2,1,0:T(8,128)(2,1)S(1)} %dynamic-slice_bitcast_fusion.refs_2_), custom_call_target="tpu_custom_call" | custom-call | bytes 10000000 | tf_op jit(solution)/shard_map/load/pallas_call | solution.py:172
  12.2 0.3 collective-permute-done.far_ref
  12.5 3.5 %collective-permute-start.1 = (bf16[4,8,1152]{2,1,0:T(8,128)(2,1)S(1)}, bf16[4,8,1152]{2,1,0:T(8,128)(2,1)S(1)}, u32[]{:S(2)}, u32[]{:S(2)}) collective-permute-start(bf16[4,8,1152]{2,1,0:T(8,128)(2,1)S(1)} %get-tuple-element.64), channel_id=1, source_target_pairs={{0,64},{16,80},{32,96},{48,112},{64,0},{80,16},{96,32},{112,48},{1... | collective-permute-start | bytes 221192 | tf_op jit(solution)/shard_map/ppermute | solution.py:564
  16.1 0.4 collective-permute-start.2
  16.5 2.3 %collective-permute-start.3 = (bf16[4,8,1152]{2,1,0:T(8,128)(2,1)S(1)}, bf16[4,8,1152]{2,1,0:T(8,128)(2,1)S(1)}, u32[]{:S(2)}, u32[]{:S(2)}) collective-permute-start(bf16[4,8,1152]{2,1,0:T(8,128)(2,1)S(1)} %get-tuple-element.66), channel_id=1, source_target_pairs={{0,96},{16,112},{32,0},{48,16},{64,32},{80,48},{96,64},{112,80},{1... | collective-permute-start | bytes 221192 | tf_op jit(solution)/shard_map/ppermute | solution.py:564
  18.8 1.8 %load.3 = (bf16[1152,1152]{1,0:T(8,128)(2,1)S(1)}, bf16[1152,1152]{1,0:T(8,128)(2,1)S(1)}, f32[8,128]{1,0:T(8,128)S(1)}) custom-call(bf16[1152,3456]{1,0:T(8,128)(2,1)} %refs_0_.3, bf16[1152,1152]{1,0:T(8,128)(2,1)S(1)} %copy-done, bf16[4,8,1152]{2,1,0:T(8,128)(2,1)S(1)} %get-tuple-element.62.refs_2_.r0), custom_call_target="tpu_custom_call" | custom-call | bytes 10000000 | tf_op jit(solution)/shard_map/load/pallas_call | solution.py:172
  20.6 0.3 collective-permute-done.2.r1
  20.9 2.5 %collective-permute-start.4 = (bf16[8,8,1152]{2,1,0:T(8,128)(2,1)S(1)}, bf16[8,8,1152]{2,1,0:T(8,128)(2,1)S(1)}, u32[]{:S(2)}, u32[]{:S(2)}) collective-permute-start(bf16[8,8,1152]{2,1,0:T(8,128)(2,1)S(1)} %get-tuple-element.68), channel_id=1, source_target_pairs={{0,16},{16,0},{32,48},{48,32},{64,80},{80,64},{96,112},{112,96},{1... | collective-permute-start | bytes 442376 | tf_op jit(solution)/shard_map/ppermute | solution.py:556
  23.4 1.0 collective-permute-done.4.x1
  24.5 3.8 %forward.1 = (bf16[128,1152]{1,0:T(8,128)(2,1)S(1)}, bf16[128,1152]{1,0:T(8,128)(2,1)S(1)}, bf16[128,3456]{1,0:T(8,128)(2,1)S(1)}, f32[16,128,128]{2,1,0:T(8,128...) custom-call(bf16[8,8,1152]{2,1,0:T(8,128)(2,1)S(1)} %get-tuple-element.67.x0, ...), custom_call_target="tpu_custom_call" | custom-call | flops 2000000000 | bytes 14000000 | tf_op jit(solution)/shard_map/forward/pallas_call | solution.py:241
  28.2 0.4 collective-permute-start.5
  28.6 0.8 collective-permute-done.5.b
  29.4 7.7 %collective-permute-start.6 = (f32[8,8]{1,0:T(8,128)S(1)}, f32[8,8]{1,0:T(8,128)S(1)}, u32[]{:S(2)}, u32[]{:S(2)}) collective-permute-start(f32[8,8]{1,0:T(8,128)S(1)} %pair_sum.2.a), channel_id=1, source_target_pairs={{0,128},{16,144},{32,160},{48,176},{64,192},{80,208},{96,224},{112... | collective-permute-start | bytes 776 | tf_op jit(solution)/shard_map/ppermute | solution.py:560
  37.2 0.5 turn.1
  37.7 0.5 collective-permute-done.6.b
  38.2 1.2 collective-permute-start.9
  39.4 1.8 %collective-permute-start.8 = (f32[8,8]{1,0:T(8,128)S(1)}, f32[8,8]{1,0:T(8,128)S(1)}, u32[]{:S(2)}, u32[]{:S(2)}) collective-permute-start(f32[8,8]{1,0:T(8,128)S(1)} %pair_sum.3.t0), channel_id=1, source_target_pairs={{0,96},{16,112},{32,0},{48,16},{64,32},{80,48},{96,64},{112,80},{1... | collective-permute-start | bytes 776 | tf_op jit(solution)/shard_map/ppermute | solution.py:564
  41.1 0.6 collective-permute-start.7
  41.7 1.8 %collective-permute-start.10 = (bf16[2,1152,128]{2,1,0:T(8,128)(2,1)S(1)}, bf16[2,1152,128]{2,1,0:T(8,128)(2,1)S(1)}, u32[]{:S(2)}, u32[]{:S(2)}) collective-permute-start(bf16[2,1152,128]{2,1,0:T(8,128)(2,1)S(1)} %get-tuple-element.84), channel_id=1, source_target_pairs={{0,16},{16,0},{32,48},{48,32},{64,80},{80,64},{96,112},{112,96},{1... | collective-permute-start | bytes 1769480 | tf_op jit(solution)/shard_map/ppermute | solution.py:556
  43.5 1.3 %collective-permute-done.7.t1 = f32[8,8]{1,0:T(8,128)S(1)} collective-permute-done((f32[8,8]{1,0:T(8,128)S(1)}, f32[8,8]{1,0:T(8,128)S(1)}, u32[]{:S(2)}, u32[]{:S(2)}) %collective-permute-start.7) | collective-permute-done | bytes 288 | tf_op jit(solution)/shard_map/ppermute | solution.py:564
  44.8 3.3 %backward.1 = (f32[4,8]{1,0:T(4,128)}, bf16[2,128,1152]{2,1,0:T(8,128)(2,1)S(1)}, bf16[2,128,1152]{2,1,0:T(8,128)(2,1)S(1)}) custom-call(f32[8,8]{1,0:T(8,128)S(1)} %pair_sum.3.t0, f32[8,8]{1,0:T(8,128)S(1)} %collective-permute-done.7.t1, f32[8,8]{1,0:T(8,128)S(1)} %collective-permute-done.8.t3, f32[8,8]{1,0:T(8,128)S(1)} %collective-permute-done.9.t2, ...), custom_call_target="tpu_custom_call" | custom-call | flops 1500000000 | bytes 8000000 | tf_op jit(solution)/shard_map/backward/pallas_call | solution.py:363
  48.1 2.6 %collective-permute-start.11 = (bf16[2,128,1152]{2,1,0:T(8,128)(2,1)S(1)}, bf16[2,128,1152]{2,1,0:T(8,128)(2,1)S(1)}, u32[]{:S(2)}, u32[]{:S(2)}) collective-permute-start(bf16[2,128,1152]{2,1,0:T(8,128)(2,1)S(1)} %get-tuple-element.86), channel_id=1, source_target_pairs={{0,16},{16,0},{32,48},{48,32},{64,80},{80,64},{96,112},{112,96},{1... | collective-permute-start | bytes 1769480 | tf_op jit(solution)/shard_map/ppermute | solution.py:556
  50.7 1.6 %collective-permute-done.11.rr = bf16[2,128,1152]{2,1,0:T(8,128)(2,1)S(1)} collective-permute-done((bf16[2,128,1152]{2,1,0:T(8,128)(2,1)S(1)}, bf16[2,128,1152]{2,1,0:T(8,128)(2,1)S(1)}, u32[]{:S(2)}, u32[]{:S(2)}) %collective-permute-start.11) | collective-permute-done | bytes 589856 | tf_op jit(solution)/shard_map/ppermute | solution.py:556
  52.3 1.7 %gradient.1 = (bf16[144,1152]{1,0:T(8,128)(2,1)S(1)}, bf16[144,1152]{1,0:T(8,128)(2,1)S(1)}, bf16[144,1152]{1,0:T(8,128)(2,1)S(1)}, bf16[144,1152]{1,0:T(8,128)(...) custom-call(bf16[2,1152,128]{2,1,0:T(8,128)(2,1)S(1)} %get-tuple-ele, ...), custom_call_target="tpu_custom_call" | custom-call | flops 1400000000 | bytes 8000000 | tf_op jit(solution)/shard_map/gradient/pallas_call | solution.py:402
  54.1 1.3 collective-permute-start.16
  55.4 1.5 %collective-permute-start.18 = (bf16[144,1152]{1,0:T(8,128)(2,1)S(1)}, bf16[144,1152]{1,0:T(8,128)(2,1)S(1)}, u32[]{:S(2)}, u32[]{:S(2)}) collective-permute-start(bf16[144,1152]{1,0:T(8,128)(2,1)S(1)} %get-tuple-element.93), channel_id=1, source_target_pairs={{0,3},{1,0},{2,1},{3,2},{4,7},{5,4},{6,5},{7,6},{8,11},{9,8},{10,9... | collective-permute-start | bytes 995336 | tf_op jit(solution)/shard_map/ppermute | solution.py:568
  56.8 2.7 %collective-permute-start.19 = (bf16[144,1152]{1,0:T(8,128)(2,1)S(1)}, bf16[144,1152]{1,0:T(8,128)(2,1)S(1)}, u32[]{:S(2)}, u32[]{:S(2)}) collective-permute-start(bf16[144,1152]{1,0:T(8,128)(2,1)S(1)} %get-tuple-element.94), channel_id=1, source_target_pairs={{0,96},{16,112},{32,0},{48,16},{64,32},{80,48},{96,64},{112,80},{1... | collective-permute-start | bytes 995336 | tf_op jit(solution)/shard_map/ppermute | solution.py:564
  59.5 4.9 %collective-permute-done.16.refs_0_ = bf16[144,1152]{1,0:T(8,128)(2,1)S(1)} collective-permute-done((bf16[144,1152]{1,0:T(8,128)(2,1)S(1)}, bf16[144,1152]{1,0:T(8,128)(2,1)S(1)}, u32[]{:S(2)}, u32[]{:S(2)}) %collective-permute-start.16) | collective-permute-done | bytes 331808 | tf_op jit(solution)/shard_map/ppermute | solution.py:568
  64.4 0.9 collective-permute-done.17.refs_1_
  65.3 1.5 %collective-permute-start.14 = (bf16[144,1152]{1,0:T(8,128)(2,1)S(1)}, bf16[144,1152]{1,0:T(8,128)(2,1)S(1)}, u32[]{:S(2)}, u32[]{:S(2)}) collective-permute-start(bf16[144,1152]{1,0:T(8,128)(2,1)S(1)} %get-tuple-element.89), channel_id=1, source_target_pairs={{0,3},{1,0},{2,1},{3,2},{4,7},{5,4},{6,5},{7,6},{8,11},{9,8},{10,9... | collective-permute-start | bytes 995336 | tf_op jit(solution)/shard_map/ppermute | solution.py:568
  66.7 1.6 %collective-permute-start.15 = (bf16[144,1152]{1,0:T(8,128)(2,1)S(1)}, bf16[144,1152]{1,0:T(8,128)(2,1)S(1)}, u32[]{:S(2)}, u32[]{:S(2)}) collective-permute-start(bf16[144,1152]{1,0:T(8,128)(2,1)S(1)} %get-tuple-element.90), channel_id=1, source_target_pairs={{0,96},{16,112},{32,0},{48,16},{64,32},{80,48},{96,64},{112,80},{1... | collective-permute-start | bytes 995336 | tf_op jit(solution)/shard_map/ppermute | solution.py:564
  68.3 0.3 relay.1
  68.6 0.3 collective-permute-start.20
  68.9 2.6 %collective-permute-done.12.refs_0_ = bf16[144,1152]{1,0:T(8,128)(2,1)S(1)} collective-permute-done((bf16[144,1152]{1,0:T(8,128)(2,1)S(1)}, bf16[144,1152]{1,0:T(8,128)(2,1)S(1)}, u32[]{:S(2)}, u32[]{:S(2)}) %collective-permute-start.12) | collective-permute-done | bytes 331808 | tf_op jit(solution)/shard_map/ppermute | solution.py:568
  71.5 1.4 %collective-permute-done.13.refs_1_ = bf16[144,1152]{1,0:T(8,128)(2,1)S(1)} collective-permute-done((bf16[144,1152]{1,0:T(8,128)(2,1)S(1)}, bf16[144,1152]{1,0:T(8,128)(2,1)S(1)}, u32[]{:S(2)}, u32[]{:S(2)}) %collective-permute-start.13) | collective-permute-done | bytes 331808 | tf_op jit(solution)/shard_map/ppermute | solution.py:564
  72.8 1.3 collective-permute-start.22
  74.1 1.3 collective-permute-start.23
  75.4 0.9 collective-permute-done.20.refs_4_
  76.4 4.4 %collective-permute-done.21.refs_5_ = bf16[144,1152]{1,0:T(8,128)(2,1)S(1)} collective-permute-done((bf16[144,1152]{1,0:T(8,128)(2,1)S(1)}, bf16[144,1152]{1,0:T(8,128)(2,1)S(1)}, u32[]{:S(2)}, u32[]{:S(2)}) %collective-permute-start.21) | collective-permute-done | bytes 331808 | tf_op jit(solution)/shard_map/ppermute | solution.py:564
  80.8 0.5 first_sum.1
  81.3 1.3 %collective-permute-start.24 = (bf16[72,1152]{1,0:T(8,128)(2,1)S(1)}, bf16[72,1152]{1,0:T(8,128)(2,1)S(1)}, u32[]{:S(2)}, u32[]{:S(2)}) collective-permute-start(bf16[72,1152]{1,0:T(8,128)(2,1)S(1)} %get-tuple-element.107), channel_id=1, source_target_pairs={{0,64},{16,80},{32,96},{48,112},{64,0},{80,16},{96,32},{112,48},{1... | collective-permute-start | bytes 497672 | tf_op jit(solution)/shard_map/ppermute | solution.py:564
  82.8 2.0 %collective-permute-start.26 = (bf16[72,1152]{1,0:T(8,128)(2,1)S(1)}, bf16[72,1152]{1,0:T(8,128)(2,1)S(1)}, u32[]{:S(2)}, u32[]{:S(2)}) collective-permute-start(bf16[72,1152]{1,0:T(8,128)(2,1)S(1)} %get-tuple-element.109), channel_id=1, source_target_pairs={{0,32},{16,48},{32,64},{48,80},{64,96},{80,112},{96,0},{112,16},{1... | collective-permute-start | bytes 497672 | tf_op jit(solution)/shard_map/ppermute | solution.py:564
  84.8 0.9 collective-permute-start.27
  85.7 0.7 collective-permute-start.28
  86.5 0.6 collective-permute-done.24.refs_2_
  87.1 1.7 %collective-permute-start.29 = (bf16[72,1152]{1,0:T(8,128)(2,1)S(1)}, bf16[72,1152]{1,0:T(8,128)(2,1)S(1)}, u32[]{:S(2)}, u32[]{:S(2)}) collective-permute-start(bf16[72,1152]{1,0:T(8,128)(2,1)S(1)} %get-tuple-element.112), channel_id=1, source_target_pairs={{0,3},{1,0},{2,1},{3,2},{4,7},{5,4},{6,5},{7,6},{8,11},{9,8},{10,9... | collective-permute-start | bytes 497672 | tf_op jit(solution)/shard_map/ppermute | solution.py:568
  88.8 2.1 %collective-permute-done.27.refs_5_ = bf16[72,1152]{1,0:T(8,128)(2,1)S(1)} collective-permute-done((bf16[72,1152]{1,0:T(8,128)(2,1)S(1)}, bf16[72,1152]{1,0:T(8,128)(2,1)S(1)}, u32[]{:S(2)}, u32[]{:S(2)}) %collective-permute-start.27) | collective-permute-done | bytes 165920 | tf_op jit(solution)/shard_map/ppermute | solution.py:568
  90.9 2.2 %collective-permute-done.29.refs_7_ = bf16[72,1152]{1,0:T(8,128)(2,1)S(1)} collective-permute-done((bf16[72,1152]{1,0:T(8,128)(2,1)S(1)}, bf16[72,1152]{1,0:T(8,128)(2,1)S(1)}, u32[]{:S(2)}, u32[]{:S(2)}) %collective-permute-start.29) | collective-permute-done | bytes 165920 | tf_op jit(solution)/shard_map/ppermute | solution.py:568
  93.1 0.2 second_sum.1
  93.4 5.5 %collective-permute-start.30 = (bf16[40,1152]{1,0:T(8,128)(2,1)S(1)}, bf16[40,1152]{1,0:T(8,128)(2,1)S(1)}, u32[]{:S(2)}, u32[]{:S(2)}) collective-permute-start(bf16[40,1152]{1,0:T(8,128)(2,1)S(1)} %get-tuple-element.114), channel_id=1, source_target_pairs={{0,8},{1,9},{2,10},{3,11},{4,12},{5,13},{6,14},{7,15},{8,128},{9,1... | collective-permute-start | bytes 276488 | tf_op jit(solution)/shard_map/ppermute | solution.py:579
  98.8 2.7 %collective-permute-start.32 = (bf16[40,1152]{1,0:T(8,128)(2,1)S(1)}, bf16[40,1152]{1,0:T(8,128)(2,1)S(1)}, u32[]{:S(2)}, u32[]{:S(2)}) collective-permute-start(bf16[40,1152]{1,0:T(8,128)(2,1)S(1)} %get-tuple-element.116), channel_id=1, source_target_pairs={{0,140},{1,141},{2,142},{3,143},{4,0},{5,1},{6,2},{7,3},{8,4},{9,5... | collective-permute-start | bytes 276488 | tf_op jit(solution)/shard_map/ppermute | solution.py:579
  101.5 2.3 %collective-permute-done.31.refs_2_ = bf16[40,1152]{1,0:T(8,128)(2,1)S(1)} collective-permute-done((bf16[40,1152]{1,0:T(8,128)(2,1)S(1)}, bf16[40,1152]{1,0:T(8,128)(2,1)S(1)}, u32[]{:S(2)}, u32[]{:S(2)}) %collective-permute-start.31) | collective-permute-done | bytes 92192 | tf_op jit(solution)/shard_map/ppermute | solution.py:579
  103.9 0.7 collective-permute-start.33
  104.6 6.7 %collective-permute-done.33.refs_1_ = bf16[40,1152]{1,0:T(8,128)(2,1)S(1)} collective-permute-done((bf16[40,1152]{1,0:T(8,128)(2,1)S(1)}, bf16[40,1152]{1,0:T(8,128)(2,1)S(1)}, u32[]{:S(2)}, u32[]{:S(2)}) %collective-permute-start.33) | collective-permute-done | bytes 92192 | tf_op jit(solution)/shard_map/ppermute | solution.py:560
  111.3 0.8 collective-permute-start.36
  112.2 2.2 %collective-permute-start.35 = (bf16[40,1152]{1,0:T(8,128)(2,1)S(1)}, bf16[40,1152]{1,0:T(8,128)(2,1)S(1)}, u32[]{:S(2)}, u32[]{:S(2)}) collective-permute-start(bf16[40,1152]{1,0:T(8,128)(2,1)S(1)} %plain_sum.3.refs_0_), channel_id=1, source_target_pairs={{0,96},{16,112},{32,0},{48,16},{64,32},{80,48},{96,64},{112,80},{1... | collective-permute-start | bytes 276488 | tf_op jit(solution)/shard_map/ppermute | solution.py:564
  114.4 2.3 %collective-permute-done.36.refs_3_ = bf16[40,1152]{1,0:T(8,128)(2,1)S(1)} collective-permute-done((bf16[40,1152]{1,0:T(8,128)(2,1)S(1)}, bf16[40,1152]{1,0:T(8,128)(2,1)S(1)}, u32[]{:S(2)}, u32[]{:S(2)}) %collective-permute-start.36) | collective-permute-done | bytes 92192 | tf_op jit(solution)/shard_map/ppermute | solution.py:564
  116.6 0.4 collective-permute-done.35.refs_2_
  117.0 1.9 %collective-permute-done.34.refs_1_ = bf16[40,1152]{1,0:T(8,128)(2,1)S(1)} collective-permute-done((bf16[40,1152]{1,0:T(8,128)(2,1)S(1)}, bf16[40,1152]{1,0:T(8,128)(2,1)S(1)}, u32[]{:S(2)}, u32[]{:S(2)}) %collective-permute-start.34) | collective-permute-done | bytes 92192 | tf_op jit(solution)/shard_map/ppermute | solution.py:564
  119.0 8.8 %collective-permute-start.37 = (bf16[4,40,1152]{2,1,0:T(8,128)(2,1)S(1)}, bf16[4,40,1152]{2,1,0:T(8,128)(2,1)S(1)}, u32[]{:S(2)}, u32[]{:S(2)}) collective-permute-start(bf16[4,40,1152]{2,1,0:T(8,128)(2,1)S(1)} %stack.1.mine), channel_id=1, source_target_pairs={{0,16},{16,0},{32,48},{48,32},{64,80},{80,64},{96,112},{112,96},{1... | collective-permute-start | bytes 1105928 | tf_op jit(solution)/shard_map/ppermute | solution.py:556
  127.8 1.3 %collective-permute-done.37.other = bf16[4,40,1152]{2,1,0:T(8,128)(2,1)S(1)} collective-permute-done((bf16[4,40,1152]{2,1,0:T(8,128)(2,1)S(1)}, bf16[4,40,1152]{2,1,0:T(8,128)(2,1)S(1)}, u32[]{:S(2)}, u32[]{:S(2)}) %collective-permute-start.37) | collective-permute-done | bytes 368672 | tf_op jit(solution)/shard_map/ppermute | solution.py:556
  129.1 1.3 last.1
  (45 shorter events, 0.6 us)
Async XLA Ops:
  1.6 10.5 %copy-start.2 = (f32[1152,8]{0,1:T(8,128)S(1)}, f32[1152,8]{0,1:T(8,128)}, u32[]{:S(2)}) copy-start(f32[1152,8]{0,1:T(8,128)} %param.15) | copy-start | bytes 110596
  1.6 10.5 %copy-start.3 = (f32[1152]{0:T(1024)S(1)}, f32[1152]{0:T(1024)}, u32[]{:S(2)}) copy-start(f32[1152]{0:T(1024)} %ln_ref.1) | copy-start | bytes 13828
  1.6 10.5 %copy-start.4 = (f32[1152]{0:T(1024)S(1)}, f32[1152]{0:T(1024)}, u32[]{:S(2)}) copy-start(f32[1152]{0:T(1024)} %og_ref.1) | copy-start | bytes 13828
  1.6 10.5 %copy-start.5 = (f32[1,4,8]{2,1,0:T(4,128)S(1)}, f32[1,4,8]{2,1,0:T(4,128)}, u32[]{:S(2)}) copy-start(f32[1,4,8]{2,1,0:T(4,128)} %param.10) | copy-start | bytes 388
  1.6 10.5 %copy-start.6 = (s32[1,4]{1,0:T(1,128)S(1)}, s32[1,4]{1,0:T(1,128)}, u32[]{:S(2)}) copy-start(s32[1,4]{1,0:T(1,128)} %lens_ref.1) | copy-start | bytes 52
  1.6 10.9 %copy-start.1 = (bf16[1,2,64,1152]{3,2,1,0:T(8,128)(2,1)S(1)}, bf16[1,2,64,1152]{3,2,1,0:T(8,128)(2,1)}, u32[]{:S(2)}) copy-start(bf16[1,2,64,1152]{3,2,1,0:T(8,128)(2,1)} %param.8) | copy-start | bytes 884740
  1.6 17.1 %copy-start = (bf16[1152,1152]{1,0:T(8,128)(2,1)S(1)}, bf16[1152,1152]{1,0:T(8,128)(2,1)}, u32[]{:S(2)}) copy-start(bf16[1152,1152]{1,0:T(8,128)(2,1)} %refs_1_.3) | copy-start | bytes 7962628
  1.7 10.9 %collective-permute-start = (bf16[2,4,8,1152]{3,2,1,0:T(8,128)(2,1)S(1)}, bf16[2,4,8,1152]{3,2,1,0:T(8,128)(2,1)S(1)}, u32[]{:S(2)}, u32[]{:S(2)}) collective-permute-start(bf16[2,4,8,1152]{3,2,1,0:T(8,128)(2,1)S(1)} %dynamic-slice_bitcast_fusion.refs_2_), channel_id=1, source_target_pairs={{0,128},{16,144},{32,160},{48,176},{64,192},{80,208},{96,224},{112... | collective-permute-start | bytes 442376 | tf_op jit(solution)/shard_map/ppermute | solution.py:560
  12.5 8.0 %collective-permute-start.1 = (bf16[4,8,1152]{2,1,0:T(8,128)(2,1)S(1)}, bf16[4,8,1152]{2,1,0:T(8,128)(2,1)S(1)}, u32[]{:S(2)}, u32[]{:S(2)}) collective-permute-start(bf16[4,8,1152]{2,1,0:T(8,128)(2,1)S(1)} %get-tuple-element.64), channel_id=1, source_target_pairs={{0,64},{16,80},{32,96},{48,112},{64,0},{80,16},{96,32},{112,48},{1... | collective-permute-start | bytes 221192 | tf_op jit(solution)/shard_map/ppermute | solution.py:564
  16.1 4.7 %collective-permute-start.2 = (bf16[4,8,1152]{2,1,0:T(8,128)(2,1)S(1)}, bf16[4,8,1152]{2,1,0:T(8,128)(2,1)S(1)}, u32[]{:S(2)}, u32[]{:S(2)}) collective-permute-start(bf16[4,8,1152]{2,1,0:T(8,128)(2,1)S(1)} %get-tuple-element.65), channel_id=1, source_target_pairs={{0,32},{16,48},{32,64},{48,80},{64,96},{80,112},{96,0},{112,16},{1... | collective-permute-start | bytes 221192 | tf_op jit(solution)/shard_map/ppermute | solution.py:564
  16.5 4.3 %collective-permute-start.3 = (bf16[4,8,1152]{2,1,0:T(8,128)(2,1)S(1)}, bf16[4,8,1152]{2,1,0:T(8,128)(2,1)S(1)}, u32[]{:S(2)}, u32[]{:S(2)}) collective-permute-start(bf16[4,8,1152]{2,1,0:T(8,128)(2,1)S(1)} %get-tuple-element.66), channel_id=1, source_target_pairs={{0,96},{16,112},{32,0},{48,16},{64,32},{80,48},{96,64},{112,80},{1... | collective-permute-start | bytes 221192 | tf_op jit(solution)/shard_map/ppermute | solution.py:564
  20.9 3.5 %collective-permute-start.4 = (bf16[8,8,1152]{2,1,0:T(8,128)(2,1)S(1)}, bf16[8,8,1152]{2,1,0:T(8,128)(2,1)S(1)}, u32[]{:S(2)}, u32[]{:S(2)}) collective-permute-start(bf16[8,8,1152]{2,1,0:T(8,128)(2,1)S(1)} %get-tuple-element.68), channel_id=1, source_target_pairs={{0,16},{16,0},{32,48},{48,32},{64,80},{80,64},{96,112},{112,96},{1... | collective-permute-start | bytes 442376 | tf_op jit(solution)/shard_map/ppermute | solution.py:556
  28.2 1.2 collective-permute-start.5
  29.4 8.7 %collective-permute-start.6 = (f32[8,8]{1,0:T(8,128)S(1)}, f32[8,8]{1,0:T(8,128)S(1)}, u32[]{:S(2)}, u32[]{:S(2)}) collective-permute-start(f32[8,8]{1,0:T(8,128)S(1)} %pair_sum.2.a), channel_id=1, source_target_pairs={{0,128},{16,144},{32,160},{48,176},{64,192},{80,208},{96,224},{112... | collective-permute-start | bytes 776 | tf_op jit(solution)/shard_map/ppermute | solution.py:560
  38.2 5.3 %collective-permute-start.9 = (f32[8,8]{1,0:T(8,128)S(1)}, f32[8,8]{1,0:T(8,128)S(1)}, u32[]{:S(2)}, u32[]{:S(2)}) collective-permute-start(f32[8,8]{1,0:T(8,128)S(1)} %pair_sum.3.t0), channel_id=1, source_target_pairs={{0,64},{16,80},{32,96},{48,112},{64,0},{80,16},{96,32},{112,48},{1... | collective-permute-start | bytes 776 | tf_op jit(solution)/shard_map/ppermute | solution.py:564
  39.4 4.1 %collective-permute-start.8 = (f32[8,8]{1,0:T(8,128)S(1)}, f32[8,8]{1,0:T(8,128)S(1)}, u32[]{:S(2)}, u32[]{:S(2)}) collective-permute-start(f32[8,8]{1,0:T(8,128)S(1)} %pair_sum.3.t0), channel_id=1, source_target_pairs={{0,96},{16,112},{32,0},{48,16},{64,32},{80,48},{96,64},{112,80},{1... | collective-permute-start | bytes 776 | tf_op jit(solution)/shard_map/ppermute | solution.py:564
  41.1 3.7 %collective-permute-start.7 = (f32[8,8]{1,0:T(8,128)S(1)}, f32[8,8]{1,0:T(8,128)S(1)}, u32[]{:S(2)}, u32[]{:S(2)}) collective-permute-start(f32[8,8]{1,0:T(8,128)S(1)} %pair_sum.3.t0), channel_id=1, source_target_pairs={{0,32},{16,48},{32,64},{48,80},{64,96},{80,112},{96,0},{112,16},{1... | collective-permute-start | bytes 776 | tf_op jit(solution)/shard_map/ppermute | solution.py:564
  41.7 9.0 %collective-permute-start.10 = (bf16[2,1152,128]{2,1,0:T(8,128)(2,1)S(1)}, bf16[2,1152,128]{2,1,0:T(8,128)(2,1)S(1)}, u32[]{:S(2)}, u32[]{:S(2)}) collective-permute-start(bf16[2,1152,128]{2,1,0:T(8,128)(2,1)S(1)} %get-tuple-element.84), channel_id=1, source_target_pairs={{0,16},{16,0},{32,48},{48,32},{64,80},{80,64},{96,112},{112,96},{1... | collective-permute-start | bytes 1769480 | tf_op jit(solution)/shard_map/ppermute | solution.py:556
  48.1 4.2 %collective-permute-start.11 = (bf16[2,128,1152]{2,1,0:T(8,128)(2,1)S(1)}, bf16[2,128,1152]{2,1,0:T(8,128)(2,1)S(1)}, u32[]{:S(2)}, u32[]{:S(2)}) collective-permute-start(bf16[2,128,1152]{2,1,0:T(8,128)(2,1)S(1)} %get-tuple-element.86), channel_id=1, source_target_pairs={{0,16},{16,0},{32,48},{48,32},{64,80},{80,64},{96,112},{112,96},{1... | collective-permute-start | bytes 1769480 | tf_op jit(solution)/shard_map/ppermute | solution.py:556
  54.1 10.3 %collective-permute-start.16 = (bf16[144,1152]{1,0:T(8,128)(2,1)S(1)}, bf16[144,1152]{1,0:T(8,128)(2,1)S(1)}, u32[]{:S(2)}, u32[]{:S(2)}) collective-permute-start(bf16[144,1152]{1,0:T(8,128)(2,1)S(1)} %get-tuple-element.91), channel_id=1, source_target_pairs={{0,1},{1,2},{2,3},{3,0},{4,5},{5,6},{6,7},{7,4},{8,9},{9,10},{10,1... | collective-permute-start | bytes 995336 | tf_op jit(solution)/shard_map/ppermute | solution.py:568
  55.4 9.9 %collective-permute-start.17 = (bf16[144,1152]{1,0:T(8,128)(2,1)S(1)}, bf16[144,1152]{1,0:T(8,128)(2,1)S(1)}, u32[]{:S(2)}, u32[]{:S(2)}) collective-permute-start(bf16[144,1152]{1,0:T(8,128)(2,1)S(1)} %get-tuple-element.92), channel_id=1, source_target_pairs={{0,32},{16,48},{32,64},{48,80},{64,96},{80,112},{96,0},{112,16},{1... | collective-permute-start | bytes 995336 | tf_op jit(solution)/shard_map/ppermute | solution.py:564
  55.4 11.4 %collective-permute-start.18 = (bf16[144,1152]{1,0:T(8,128)(2,1)S(1)}, bf16[144,1152]{1,0:T(8,128)(2,1)S(1)}, u32[]{:S(2)}, u32[]{:S(2)}) collective-permute-start(bf16[144,1152]{1,0:T(8,128)(2,1)S(1)} %get-tuple-element.93), channel_id=1, source_target_pairs={{0,3},{1,0},{2,1},{3,2},{4,7},{5,4},{6,5},{7,6},{8,11},{9,8},{10,9... | collective-permute-start | bytes 995336 | tf_op jit(solution)/shard_map/ppermute | solution.py:568
  56.8 11.5 %collective-permute-start.19 = (bf16[144,1152]{1,0:T(8,128)(2,1)S(1)}, bf16[144,1152]{1,0:T(8,128)(2,1)S(1)}, u32[]{:S(2)}, u32[]{:S(2)}) collective-permute-start(bf16[144,1152]{1,0:T(8,128)(2,1)S(1)} %get-tuple-element.94), channel_id=1, source_target_pairs={{0,96},{16,112},{32,0},{48,16},{64,32},{80,48},{96,64},{112,80},{1... | collective-permute-start | bytes 995336 | tf_op jit(solution)/shard_map/ppermute | solution.py:564
  59.5 12.0 %collective-permute-start.12 = (bf16[144,1152]{1,0:T(8,128)(2,1)S(1)}, bf16[144,1152]{1,0:T(8,128)(2,1)S(1)}, u32[]{:S(2)}, u32[]{:S(2)}) collective-permute-start(bf16[144,1152]{1,0:T(8,128)(2,1)S(1)} %get-tuple-element.87), channel_id=1, source_target_pairs={{0,1},{1,2},{2,3},{3,0},{4,5},{5,6},{6,7},{7,4},{8,9},{9,10},{10,1... | collective-permute-start | bytes 995336 | tf_op jit(solution)/shard_map/ppermute | solution.py:568
  64.4 8.5 %collective-permute-start.13 = (bf16[144,1152]{1,0:T(8,128)(2,1)S(1)}, bf16[144,1152]{1,0:T(8,128)(2,1)S(1)}, u32[]{:S(2)}, u32[]{:S(2)}) collective-permute-start(bf16[144,1152]{1,0:T(8,128)(2,1)S(1)} %get-tuple-element.88), channel_id=1, source_target_pairs={{0,32},{16,48},{32,64},{48,80},{64,96},{80,112},{96,0},{112,16},{1... | collective-permute-start | bytes 995336 | tf_op jit(solution)/shard_map/ppermute | solution.py:564
  65.3 8.9 %collective-permute-start.14 = (bf16[144,1152]{1,0:T(8,128)(2,1)S(1)}, bf16[144,1152]{1,0:T(8,128)(2,1)S(1)}, u32[]{:S(2)}, u32[]{:S(2)}) collective-permute-start(bf16[144,1152]{1,0:T(8,128)(2,1)S(1)} %get-tuple-element.89), channel_id=1, source_target_pairs={{0,3},{1,0},{2,1},{3,2},{4,7},{5,4},{6,5},{7,6},{8,11},{9,8},{10,9... | collective-permute-start | bytes 995336 | tf_op jit(solution)/shard_map/ppermute | solution.py:568
  66.7 8.7 %collective-permute-start.15 = (bf16[144,1152]{1,0:T(8,128)(2,1)S(1)}, bf16[144,1152]{1,0:T(8,128)(2,1)S(1)}, u32[]{:S(2)}, u32[]{:S(2)}) collective-permute-start(bf16[144,1152]{1,0:T(8,128)(2,1)S(1)} %get-tuple-element.90), channel_id=1, source_target_pairs={{0,96},{16,112},{32,0},{48,16},{64,32},{80,48},{96,64},{112,80},{1... | collective-permute-start | bytes 995336 | tf_op jit(solution)/shard_map/ppermute | solution.py:564
  68.6 7.7 %collective-permute-start.20 = (bf16[144,1152]{1,0:T(8,128)(2,1)S(1)}, bf16[144,1152]{1,0:T(8,128)(2,1)S(1)}, u32[]{:S(2)}, u32[]{:S(2)}) collective-permute-start(bf16[144,1152]{1,0:T(8,128)(2,1)S(1)} %get-tuple-element.99), channel_id=1, source_target_pairs={{0,1},{1,2},{2,3},{3,0},{4,5},{5,6},{6,7},{7,4},{8,9},{9,10},{10,1... | collective-permute-start | bytes 995336 | tf_op jit(solution)/shard_map/ppermute | solution.py:568
  71.5 9.3 %collective-permute-start.21 = (bf16[144,1152]{1,0:T(8,128)(2,1)S(1)}, bf16[144,1152]{1,0:T(8,128)(2,1)S(1)}, u32[]{:S(2)}, u32[]{:S(2)}) collective-permute-start(bf16[144,1152]{1,0:T(8,128)(2,1)S(1)} %get-tuple-element.100), channel_id=1, source_target_pairs={{0,32},{16,48},{32,64},{48,80},{64,96},{80,112},{96,0},{112,16},{1... | collective-permute-start | bytes 995336 | tf_op jit(solution)/shard_map/ppermute | solution.py:564
  72.8 7.9 %collective-permute-start.22 = (bf16[144,1152]{1,0:T(8,128)(2,1)S(1)}, bf16[144,1152]{1,0:T(8,128)(2,1)S(1)}, u32[]{:S(2)}, u32[]{:S(2)}) collective-permute-start(bf16[144,1152]{1,0:T(8,128)(2,1)S(1)} %get-tuple-element.101), channel_id=1, source_target_pairs={{0,3},{1,0},{2,1},{3,2},{4,7},{5,4},{6,5},{7,6},{8,11},{9,8},{10,9... | collective-permute-start | bytes 995336 | tf_op jit(solution)/shard_map/ppermute | solution.py:568
  74.1 6.6 %collective-permute-start.23 = (bf16[144,1152]{1,0:T(8,128)(2,1)S(1)}, bf16[144,1152]{1,0:T(8,128)(2,1)S(1)}, u32[]{:S(2)}, u32[]{:S(2)}) collective-permute-start(bf16[144,1152]{1,0:T(8,128)(2,1)S(1)} %get-tuple-element.102), channel_id=1, source_target_pairs={{0,96},{16,112},{32,0},{48,16},{64,32},{80,48},{96,64},{112,80},{1... | collective-permute-start | bytes 995336 | tf_op jit(solution)/shard_map/ppermute | solution.py:564
  81.3 5.9 %collective-permute-start.24 = (bf16[72,1152]{1,0:T(8,128)(2,1)S(1)}, bf16[72,1152]{1,0:T(8,128)(2,1)S(1)}, u32[]{:S(2)}, u32[]{:S(2)}) collective-permute-start(bf16[72,1152]{1,0:T(8,128)(2,1)S(1)} %get-tuple-element.107), channel_id=1, source_target_pairs={{0,64},{16,80},{32,96},{48,112},{64,0},{80,16},{96,32},{112,48},{1... | collective-permute-start | bytes 497672 | tf_op jit(solution)/shard_map/ppermute | solution.py:564
  82.6 6.2 %collective-permute-start.25 = (bf16[72,1152]{1,0:T(8,128)(2,1)S(1)}, bf16[72,1152]{1,0:T(8,128)(2,1)S(1)}, u32[]{:S(2)}, u32[]{:S(2)}) collective-permute-start(bf16[72,1152]{1,0:T(8,128)(2,1)S(1)} %get-tuple-element.108), channel_id=1, source_target_pairs={{0,2},{1,3},{2,0},{3,1},{4,6},{5,7},{6,4},{7,5},{8,10},{9,11},{10,... | collective-permute-start | bytes 497672 | tf_op jit(solution)/shard_map/ppermute | solution.py:568
  82.8 6.1 %collective-permute-start.26 = (bf16[72,1152]{1,0:T(8,128)(2,1)S(1)}, bf16[72,1152]{1,0:T(8,128)(2,1)S(1)}, u32[]{:S(2)}, u32[]{:S(2)}) collective-permute-start(bf16[72,1152]{1,0:T(8,128)(2,1)S(1)} %get-tuple-element.109), channel_id=1, source_target_pairs={{0,32},{16,48},{32,64},{48,80},{64,96},{80,112},{96,0},{112,16},{1... | collective-permute-start | bytes 497672 | tf_op jit(solution)/shard_map/ppermute | solution.py:564
  84.8 6.2 %collective-permute-start.27 = (bf16[72,1152]{1,0:T(8,128)(2,1)S(1)}, bf16[72,1152]{1,0:T(8,128)(2,1)S(1)}, u32[]{:S(2)}, u32[]{:S(2)}) collective-permute-start(bf16[72,1152]{1,0:T(8,128)(2,1)S(1)} %get-tuple-element.110), channel_id=1, source_target_pairs={{0,1},{1,2},{2,3},{3,0},{4,5},{5,6},{6,7},{7,4},{8,9},{9,10},{10,1... | collective-permute-start | bytes 497672 | tf_op jit(solution)/shard_map/ppermute | solution.py:568
  85.7 5.2 %collective-permute-start.28 = (bf16[72,1152]{1,0:T(8,128)(2,1)S(1)}, bf16[72,1152]{1,0:T(8,128)(2,1)S(1)}, u32[]{:S(2)}, u32[]{:S(2)}) collective-permute-start(bf16[72,1152]{1,0:T(8,128)(2,1)S(1)} %get-tuple-element.111), channel_id=1, source_target_pairs={{0,96},{16,112},{32,0},{48,16},{64,32},{80,48},{96,64},{112,80},{1... | collective-permute-start | bytes 497672 | tf_op jit(solution)/shard_map/ppermute | solution.py:564
  87.1 6.0 %collective-permute-start.29 = (bf16[72,1152]{1,0:T(8,128)(2,1)S(1)}, bf16[72,1152]{1,0:T(8,128)(2,1)S(1)}, u32[]{:S(2)}, u32[]{:S(2)}) collective-permute-start(bf16[72,1152]{1,0:T(8,128)(2,1)S(1)} %get-tuple-element.112), channel_id=1, source_target_pairs={{0,3},{1,0},{2,1},{3,2},{4,7},{5,4},{6,5},{7,6},{8,11},{9,8},{10,9... | collective-permute-start | bytes 497672 | tf_op jit(solution)/shard_map/ppermute | solution.py:568
  93.4 8.1 %collective-permute-start.30 = (bf16[40,1152]{1,0:T(8,128)(2,1)S(1)}, bf16[40,1152]{1,0:T(8,128)(2,1)S(1)}, u32[]{:S(2)}, u32[]{:S(2)}) collective-permute-start(bf16[40,1152]{1,0:T(8,128)(2,1)S(1)} %get-tuple-element.114), channel_id=1, source_target_pairs={{0,8},{1,9},{2,10},{3,11},{4,12},{5,13},{6,14},{7,15},{8,128},{9,1... | collective-permute-start | bytes 276488 | tf_op jit(solution)/shard_map/ppermute | solution.py:579
  98.8 5.0 %collective-permute-start.31 = (bf16[40,1152]{1,0:T(8,128)(2,1)S(1)}, bf16[40,1152]{1,0:T(8,128)(2,1)S(1)}, u32[]{:S(2)}, u32[]{:S(2)}) collective-permute-start(bf16[40,1152]{1,0:T(8,128)(2,1)S(1)} %get-tuple-element.115), channel_id=1, source_target_pairs={{0,4},{1,5},{2,6},{3,7},{4,8},{5,9},{6,10},{7,11},{8,12},{9,13},{1... | collective-permute-start | bytes 276488 | tf_op jit(solution)/shard_map/ppermute | solution.py:579
  98.8 5.0 %collective-permute-start.32 = (bf16[40,1152]{1,0:T(8,128)(2,1)S(1)}, bf16[40,1152]{1,0:T(8,128)(2,1)S(1)}, u32[]{:S(2)}, u32[]{:S(2)}) collective-permute-start(bf16[40,1152]{1,0:T(8,128)(2,1)S(1)} %get-tuple-element.116), channel_id=1, source_target_pairs={{0,140},{1,141},{2,142},{3,143},{4,0},{5,1},{6,2},{7,3},{8,4},{9,5... | collective-permute-start | bytes 276488 | tf_op jit(solution)/shard_map/ppermute | solution.py:579
  103.9 7.4 %collective-permute-start.33 = (bf16[40,1152]{1,0:T(8,128)(2,1)S(1)}, bf16[40,1152]{1,0:T(8,128)(2,1)S(1)}, u32[]{:S(2)}, u32[]{:S(2)}) collective-permute-start(bf16[40,1152]{1,0:T(8,128)(2,1)S(1)} %plain_sum.2.refs_0_), channel_id=1, source_target_pairs={{0,128},{16,144},{32,160},{48,176},{64,192},{80,208},{96,224},{112... | collective-permute-start | bytes 276488 | tf_op jit(solution)/shard_map/ppermute | solution.py:560
  111.3 5.3 %collective-permute-start.36 = (bf16[40,1152]{1,0:T(8,128)(2,1)S(1)}, bf16[40,1152]{1,0:T(8,128)(2,1)S(1)}, u32[]{:S(2)}, u32[]{:S(2)}) collective-permute-start(bf16[40,1152]{1,0:T(8,128)(2,1)S(1)} %plain_sum.3.refs_0_), channel_id=1, source_target_pairs={{0,64},{16,80},{32,96},{48,112},{64,0},{80,16},{96,32},{112,48},{1... | collective-permute-start | bytes 276488 | tf_op jit(solution)/shard_map/ppermute | solution.py:564
  112.2 4.9 %collective-permute-start.35 = (bf16[40,1152]{1,0:T(8,128)(2,1)S(1)}, bf16[40,1152]{1,0:T(8,128)(2,1)S(1)}, u32[]{:S(2)}, u32[]{:S(2)}) collective-permute-start(bf16[40,1152]{1,0:T(8,128)(2,1)S(1)} %plain_sum.3.refs_0_), channel_id=1, source_target_pairs={{0,96},{16,112},{32,0},{48,16},{64,32},{80,48},{96,64},{112,80},{1... | collective-permute-start | bytes 276488 | tf_op jit(solution)/shard_map/ppermute | solution.py:564
  114.4 4.6 %collective-permute-start.34 = (bf16[40,1152]{1,0:T(8,128)(2,1)S(1)}, bf16[40,1152]{1,0:T(8,128)(2,1)S(1)}, u32[]{:S(2)}, u32[]{:S(2)}) collective-permute-start(bf16[40,1152]{1,0:T(8,128)(2,1)S(1)} %plain_sum.3.refs_0_), channel_id=1, source_target_pairs={{0,32},{16,48},{32,64},{48,80},{64,96},{80,112},{96,0},{112,16},{1... | collective-permute-start | bytes 276488 | tf_op jit(solution)/shard_map/ppermute | solution.py:564
  119.0 10.1 %collective-permute-start.37 = (bf16[4,40,1152]{2,1,0:T(8,128)(2,1)S(1)}, bf16[4,40,1152]{2,1,0:T(8,128)(2,1)S(1)}, u32[]{:S(2)}, u32[]{:S(2)}) collective-permute-start(bf16[4,40,1152]{2,1,0:T(8,128)(2,1)S(1)} %stack.1.mine), channel_id=1, source_target_pairs={{0,16},{16,0},{32,48},{48,32},{64,80},{80,64},{96,112},{112,96},{1... | collective-permute-start | bytes 1105928 | tf_op jit(solution)/shard_map/ppermute | solution.py:556

commit v3 on v2

--- a/solution.py
+++ b/solution.py
@@ -380,28 +380,32 @@
     )(*totals, small, proj, p, centred, inv, w_out)
 
 
-PARTS = ((2, 0), (2, 1), (1, 1), (3, 0), (1, 0), (3, 1))
-
-
 def gradient_kernel(lk, lr, rk, rr, *outs):
     for i in range(2):
+        on, back, plain, own_on, own_back, own = outs[6 * i : 6 * i + 6]
         right = jnp.concatenate([rk[i], rr[i]], axis=0)
-        for k in (2, 1, 3, 0):
+        for k in (2, 3, 1, 0):
             rows = slice(288 * k, 288 * (k + 1))
             left = jnp.concatenate([lk[i, rows], lr[i, rows]], axis=1)
             part = dot(left, right, 1, 0).astype(bf16)
-            if k == 0:
-                outs[7 * i + 6][...] = part
+            if k == 2:
+                on[...] = part[:144]
+                back[0:144] = part[144:]
+            elif k == 3:
+                back[144:288] = part[:144]
+                own_back[...] = part[144:]
+            elif k == 1:
+                own_on[...] = part[:144]
+                plain[...] = part[144:]
             else:
-                for j, (distance, piece) in enumerate(PARTS):
-                    if distance == k:
-                        outs[7 * i + j][...] = part[144 * piece : 144 * (piece + 1)]
+                own[...] = part
 
 
 def gradient(left_keep, left_recv, right_keep, right_recv):
+    rows = (144, 288, 144, 144, 144, 288)
     parts = call(
         gradient_kernel,
-        ((shape((144, D), bf16),) * 6 + (shape((288, D), bf16),)) * 2,
+        tuple(shape((r, D), bf16) for r in rows) * 2,
         [VMEM] * 4,
         [],
         16,
@@ -409,23 +413,24 @@
         flops=1_400_000_000,
         moved=8_000_000,
     )(left_keep, left_recv, right_keep, right_recv)
-    return parts[:7], parts[7:]
+    return parts[:6], parts[6:]
 
 
 def relay_kernel(*refs):
-    for k in range(4):
-        refs[8 + k][...] = (refs[k][...].astype(f32) + refs[4 + k][...].astype(f32)).astype(bf16)
+    for k in range(2):
+        arrived = refs[k][0:144].astype(f32)
+        refs[4 + k][...] = (arrived + refs[2 + k][...].astype(f32)).astype(bf16)
 
 
 def relay(arrived, own):
     return call(
         relay_kernel,
-        (shape((144, D), bf16),) * 4,
-        [VMEM] * 8,
+        (shape((144, D), bf16),) * 2,
+        [VMEM] * 4,
         [],
-        8,
+        6,
         "relay",
-        moved=4_000_000,
+        moved=2_000_000,
     )(*arrived, *own)
 
 
@@ -444,7 +449,7 @@
         plain_on, plain_back, relayed_on, relayed_back, own = (refs[2 * j + i] for j in range(5))
         result = own[...].astype(f32) + jnp.concatenate(
             [
-                plain_back[...].astype(f32) + relayed_on[...].astype(f32),
+                plain_back[144:288].astype(f32) + relayed_on[...].astype(f32),
                 plain_on[...].astype(f32) + relayed_back[...].astype(f32),
             ],
             axis=0,
@@ -588,14 +593,15 @@
 
 
 def around(x_half, y_half):
-    on, back = (along_x, along_y), 3
-    halves = (x_half, y_half)
-    arrived = [on[i](halves[i][j], 1 if j == 0 else back) for j in range(2) for i in range(2)]
-    plain = [on[i](halves[i][2 + j], 1 if j == 0 else back) for j in range(2) for i in range(2)]
-    own = [halves[i][4 + j] for j in range(2) for i in range(2)]
-    sums = relay(arrived, own)
-    relayed = [on[i](sums[2 * j + i], 1 if j == 0 else back) for j in range(2) for i in range(2)]
-    return first_sum(plain + relayed + [x_half[6], y_half[6]])
+    halves = ((x_half, along_x), (y_half, along_y))
+    first = [move(half[0], 1) for half, move in halves]
+    back = [move(half[1], 3) for half, move in halves]
+    plain = [move(half[2], 1) for half, move in halves]
+    sums = relay(first, [half[3] for half, _ in halves])
+    relayed_on = [move(block, 1) for block, (_, move) in zip(sums, halves)]
+    sums = relay(back, [half[4] for half, _ in halves])
+    relayed_back = [move(block, 3) for block, (_, move) in zip(sums, halves)]
+    return first_sum(plain + back + relayed_on + relayed_back + [x_half[5], y_half[5]])
 
 
 def on_device(tokens, clip_frames, teacher_scores, ln_gain, w_qkv, w_out, out_gain, reward_head):

time: 131 us -> 132 us (level)
    ppermute x9 -> x8, waiting for transfers between devices: 12.7 us -> 16.9 us  [along_x(): lax.ppermute(block, 'dp', [(i, i & 12 | i + k & 3) for i in range(16)])]
    ppermute x18 -> x17, waiting for transfers between devices: 13.5 us -> 10.5 us  [along_y(): lax.ppermute(block, 'tm', [(i, i & 9 | i + 2 * k & 6) for i in range(16)])]
    ppermute x18 -> x17, starting transfers between devices: 22.4 us -> 24.6 us  [along_y(): lax.ppermute(block, 'tm', [(i, i & 9 | i + 2 * k & 6) for i in range(16)])]
    ppermute x9 -> x8, starting transfers between devices: 8.58 us -> 7.13 us  [along_x(): lax.ppermute(block, 'dp', [(i, i & 12 | i + k & 3) for i in range(16)])]
  transfers between devices with their start and end apart: 38 -> 36, of which waited for: 22 -> 22; matrix products, arithmetic and copies ran while one was open for 0% -> 0% of each run, Pallas kernels for 7% -> 6%
where the time goes in v3:
time: 132 us
  starting transfers between devices  72.4 us (55%)
  waiting for transfers between devices  41.6 us (32%)
  Pallas kernels  16.3 us (12%)
    ppermute x17, starting transfers between devices, along_y(): lax.ppermute(block, 'tm', [(i, i & 9 | i + 2 * k & 6) for i in range(16)])  24.6 us
    ppermute x8, waiting for transfers between devices, along_x(): lax.ppermute(block, 'dp', [(i, i & 12 | i + k & 3) for i in range(16)])  16.9 us
    ppermute x3, starting transfers between devices, to_far(): return lax.ppermute(block, 'tm', [(i, i ^ 8) for i in range(16)])  16.6 us
    ppermute x5, starting transfers between devices, to_core(): return lax.ppermute(block, 'tm', [(i, i ^ 1) for i in range(16)])  16 us
    ppermute x17, waiting for transfers between devices, along_y(): lax.ppermute(block, 'tm', [(i, i & 9 | i + 2 * k & 6) for i in range(16)])  10.5 us
    ppermute x3, starting transfers between devices, around_z(): return lax.ppermute(block, ('tm', 'dp'), route)  8.14 us
    ppermute x3, waiting for transfers between devices, to_far(): return lax.ppermute(block, 'tm', [(i, i ^ 8) for i in range(16)])  7.37 us
    ppermute x8, starting transfers between devices, along_x(): lax.ppermute(block, 'dp', [(i, i & 12 | i + k & 3) for i in range(16)])  7.13 us
  transfers between devices with their start and end apart: 36, of which 22 were waited for; matrix products, arithmetic and copies ran while one was open for 0% of the time, Pallas kernels for 6%

profile of v3, /device:TPU:1, one launch (start us, length us, event | category | flops | bytes accessed | tf_op | source)
XLA Modules:
  0.0 132.1 jit_solution(16164873173844072732)
XLA Ops:
  0.6 0.9 dynamic-slice_bitcast_fusion.refs_2_
  1.7 7.8 %collective-permute-start = (bf16[2,4,8,1152]{3,2,1,0:T(8,128)(2,1)S(1)}, bf16[2,4,8,1152]{3,2,1,0:T(8,128)(2,1)S(1)}, u32[]{:S(2)}, u32[]{:S(2)}) collective-permute-start(bf16[2,4,8,1152]{3,2,1,0:T(8,128)(2,1)S(1)} %dynamic-slice_bitcast_fusion.refs_2_), channel_id=1, source_target_pairs={{0,128},{16,144},{32,160},{48,176},{64,192},{80,208},{96,224},{112... | collective-permute-start | bytes 442376 | tf_op jit(solution)/shard_map/ppermute | solution.py:565
  9.5 2.6 %load.2 = (bf16[1152,1152]{1,0:T(8,128)(2,1)S(1)}, bf16[1152,1152]{1,0:T(8,128)(2,1)S(1)}, f32[8,128]{1,0:T(8,128)S(1)}) custom-call(bf16[1152,3456]{1,0:T(8,128)(2,1)} %refs_0_.3, bf16[1152,3456]{1,0:T(8,128)(2,1)} %refs_0_.3, bf16[2,4,8,1152]{3,2,1,0:T(8,128)(2,1)S(1)} %dynamic-slice_bitcast_fusion.refs_2_), custom_call_target="tpu_custom_call" | custom-call | bytes 10000000 | tf_op jit(solution)/shard_map/load/pallas_call | solution.py:172
  12.2 0.3 collective-permute-done.far_ref
  12.5 3.5 %collective-permute-start.1 = (bf16[4,8,1152]{2,1,0:T(8,128)(2,1)S(1)}, bf16[4,8,1152]{2,1,0:T(8,128)(2,1)S(1)}, u32[]{:S(2)}, u32[]{:S(2)}) collective-permute-start(bf16[4,8,1152]{2,1,0:T(8,128)(2,1)S(1)} %get-tuple-element.62), channel_id=1, source_target_pairs={{0,64},{16,80},{32,96},{48,112},{64,0},{80,16},{96,32},{112,48},{1... | collective-permute-start | bytes 221192 | tf_op jit(solution)/shard_map/ppermute | solution.py:569
  16.1 0.4 collective-permute-start.2
  16.5 2.3 %collective-permute-start.3 = (bf16[4,8,1152]{2,1,0:T(8,128)(2,1)S(1)}, bf16[4,8,1152]{2,1,0:T(8,128)(2,1)S(1)}, u32[]{:S(2)}, u32[]{:S(2)}) collective-permute-start(bf16[4,8,1152]{2,1,0:T(8,128)(2,1)S(1)} %get-tuple-element.64), channel_id=1, source_target_pairs={{0,96},{16,112},{32,0},{48,16},{64,32},{80,48},{96,64},{112,80},{1... | collective-permute-start | bytes 221192 | tf_op jit(solution)/shard_map/ppermute | solution.py:569
  18.8 1.8 %load.3 = (bf16[1152,1152]{1,0:T(8,128)(2,1)S(1)}, bf16[1152,1152]{1,0:T(8,128)(2,1)S(1)}, f32[8,128]{1,0:T(8,128)S(1)}) custom-call(bf16[1152,3456]{1,0:T(8,128)(2,1)} %refs_0_.3, bf16[1152,1152]{1,0:T(8,128)(2,1)S(1)} %copy-done, bf16[4,8,1152]{2,1,0:T(8,128)(2,1)S(1)} %get-tuple-element.60.refs_2_.r0), custom_call_target="tpu_custom_call" | custom-call | bytes 10000000 | tf_op jit(solution)/shard_map/load/pallas_call | solution.py:172
  20.6 0.3 collective-permute-done.2.r1
  20.8 0.1 split.1
  20.9 2.5 %collective-permute-start.4 = (bf16[8,8,1152]{2,1,0:T(8,128)(2,1)S(1)}, bf16[8,8,1152]{2,1,0:T(8,128)(2,1)S(1)}, u32[]{:S(2)}, u32[]{:S(2)}) collective-permute-start(bf16[8,8,1152]{2,1,0:T(8,128)(2,1)S(1)} %get-tuple-element.66), channel_id=1, source_target_pairs={{0,16},{16,0},{32,48},{48,32},{64,80},{80,64},{96,112},{112,96},{1... | collective-permute-start | bytes 442376 | tf_op jit(solution)/shard_map/ppermute | solution.py:561
  23.4 1.0 collective-permute-done.4.x1
  24.5 3.8 %forward.1 = (bf16[128,1152]{1,0:T(8,128)(2,1)S(1)}, bf16[128,1152]{1,0:T(8,128)(2,1)S(1)}, bf16[128,3456]{1,0:T(8,128)(2,1)S(1)}, f32[16,128,128]{2,1,0:T(8,128...) custom-call(bf16[8,8,1152]{2,1,0:T(8,128)(2,1)S(1)} %get-tuple-element.65.x0, ...), custom_call_target="tpu_custom_call" | custom-call | flops 2000000000 | bytes 14000000 | tf_op jit(solution)/shard_map/forward/pallas_call | solution.py:241
  28.2 0.4 collective-permute-start.5
  28.6 0.8 collective-permute-done.5.b
  29.4 7.7 %collective-permute-start.6 = (f32[8,8]{1,0:T(8,128)S(1)}, f32[8,8]{1,0:T(8,128)S(1)}, u32[]{:S(2)}, u32[]{:S(2)}) collective-permute-start(f32[8,8]{1,0:T(8,128)S(1)} %pair_sum.2.a), channel_id=1, source_target_pairs={{0,128},{16,144},{32,160},{48,176},{64,192},{80,208},{96,224},{112... | collective-permute-start | bytes 776 | tf_op jit(solution)/shard_map/ppermute | solution.py:565
  37.2 0.5 turn.1
  37.7 0.5 collective-permute-done.6.b
  38.2 1.2 collective-permute-start.9
  39.4 1.8 %collective-permute-start.8 = (f32[8,8]{1,0:T(8,128)S(1)}, f32[8,8]{1,0:T(8,128)S(1)}, u32[]{:S(2)}, u32[]{:S(2)}) collective-permute-start(f32[8,8]{1,0:T(8,128)S(1)} %pair_sum.3.t0), channel_id=1, source_target_pairs={{0,96},{16,112},{32,0},{48,16},{64,32},{80,48},{96,64},{112,80},{1... | collective-permute-start | bytes 776 | tf_op jit(solution)/shard_map/ppermute | solution.py:569
  41.1 0.6 collective-permute-start.7
  41.7 1.8 %collective-permute-start.10 = (bf16[2,1152,128]{2,1,0:T(8,128)(2,1)S(1)}, bf16[2,1152,128]{2,1,0:T(8,128)(2,1)S(1)}, u32[]{:S(2)}, u32[]{:S(2)}) collective-permute-start(bf16[2,1152,128]{2,1,0:T(8,128)(2,1)S(1)} %get-tuple-element.82), channel_id=1, source_target_pairs={{0,16},{16,0},{32,48},{48,32},{64,80},{80,64},{96,112},{112,96},{1... | collective-permute-start | bytes 1769480 | tf_op jit(solution)/shard_map/ppermute | solution.py:561
  43.5 1.3 collective-permute-done.7.t1
  44.8 3.3 %backward.1 = (f32[4,8]{1,0:T(4,128)}, bf16[2,128,1152]{2,1,0:T(8,128)(2,1)S(1)}, bf16[2,128,1152]{2,1,0:T(8,128)(2,1)S(1)}) custom-call(f32[8,8]{1,0:T(8,128)S(1)} %pair_sum.3.t0, f32[8,8]{1,0:T(8,128)S(1)} %collective-permute-done.7.t1, f32[8,8]{1,0:T(8,128)S(1)} %collective-permute-done.8.t3, f32[8,8]{1,0:T(8,128)S(1)} %collective-permute-done.9.t2, ...), custom_call_target="tpu_custom_call" | custom-call | flops 1500000000 | bytes 8000000 | tf_op jit(solution)/shard_map/backward/pallas_call | solution.py:363
  48.1 2.6 %collective-permute-start.11 = (bf16[2,128,1152]{2,1,0:T(8,128)(2,1)S(1)}, bf16[2,128,1152]{2,1,0:T(8,128)(2,1)S(1)}, u32[]{:S(2)}, u32[]{:S(2)}) collective-permute-start(bf16[2,128,1152]{2,1,0:T(8,128)(2,1)S(1)} %get-tuple-element.84), channel_id=1, source_target_pairs={{0,16},{16,0},{32,48},{48,32},{64,80},{80,64},{96,112},{112,96},{1... | collective-permute-start | bytes 1769480 | tf_op jit(solution)/shard_map/ppermute | solution.py:561
  50.7 1.6 %collective-permute-done.11.rr = bf16[2,128,1152]{2,1,0:T(8,128)(2,1)S(1)} collective-permute-done((bf16[2,128,1152]{2,1,0:T(8,128)(2,1)S(1)}, bf16[2,128,1152]{2,1,0:T(8,128)(2,1)S(1)}, u32[]{:S(2)}, u32[]{:S(2)}) %collective-permute-start.11) | collective-permute-done | bytes 589856 | tf_op jit(solution)/shard_map/ppermute | solution.py:561
  52.3 1.7 %gradient.1 = (bf16[144,1152]{1,0:T(8,128)(2,1)S(1)}, bf16[288,1152]{1,0:T(8,128)(2,1)S(1)}, bf16[144,1152]{1,0:T(8,128)(2,1)S(1)}, bf16[144,1152]{1,0:T(8,128)(...) custom-call(bf16[2,1152,128]{2,1,0:T(8,128)(2,1)S(1)} %get-tuple-ele, ...), custom_call_target="tpu_custom_call" | custom-call | flops 1400000000 | bytes 8000000 | tf_op jit(solution)/shard_map/gradient/pallas_call | solution.py:406
  54.1 2.6 %collective-permute-start.14 = (bf16[288,1152]{1,0:T(8,128)(2,1)S(1)}, bf16[288,1152]{1,0:T(8,128)(2,1)S(1)}, u32[]{:S(2)}, u32[]{:S(2)}) collective-permute-start(bf16[288,1152]{1,0:T(8,128)(2,1)S(1)} %get-tuple-element.87), channel_id=1, source_target_pairs={{0,3},{1,0},{2,1},{3,2},{4,7},{5,4},{6,5},{7,6},{8,11},{9,8},{10,9... | collective-permute-start | bytes 1990664 | tf_op jit(solution)/shard_map/ppermute | solution.py:573
  56.6 1.4 %collective-permute-start.17 = (bf16[144,1152]{1,0:T(8,128)(2,1)S(1)}, bf16[144,1152]{1,0:T(8,128)(2,1)S(1)}, u32[]{:S(2)}, u32[]{:S(2)}) collective-permute-start(bf16[144,1152]{1,0:T(8,128)(2,1)S(1)} %get-tuple-element.90), channel_id=1, source_target_pairs={{0,32},{16,48},{32,64},{48,80},{64,96},{80,112},{96,0},{112,16},{1... | collective-permute-start | bytes 995336 | tf_op jit(solution)/shard_map/ppermute | solution.py:569
  58.1 0.2 collective-permute-start.12
  58.3 7.9 %collective-permute-done.16.refs_0_ = bf16[144,1152]{1,0:T(8,128)(2,1)S(1)} collective-permute-done((bf16[144,1152]{1,0:T(8,128)(2,1)S(1)}, bf16[144,1152]{1,0:T(8,128)(2,1)S(1)}, u32[]{:S(2)}, u32[]{:S(2)}) %collective-permute-start.16) | collective-permute-done | bytes 331808 | tf_op jit(solution)/shard_map/ppermute | solution.py:573
  66.2 1.4 %collective-permute-start.13 = (bf16[144,1152]{1,0:T(8,128)(2,1)S(1)}, bf16[144,1152]{1,0:T(8,128)(2,1)S(1)}, u32[]{:S(2)}, u32[]{:S(2)}) collective-permute-start(bf16[144,1152]{1,0:T(8,128)(2,1)S(1)} %get-tuple-element.86), channel_id=1, source_target_pairs={{0,32},{16,48},{32,64},{48,80},{64,96},{80,112},{96,0},{112,16},{1... | collective-permute-start | bytes 995336 | tf_op jit(solution)/shard_map/ppermute | solution.py:569
  67.7 0.2 relay.2
  67.9 2.6 %collective-permute-done.14.refs_0_.refs_2_ = bf16[288,1152]{1,0:T(8,128)(2,1)S(1)} collective-permute-done((bf16[288,1152]{1,0:T(8,128)(2,1)S(1)}, bf16[288,1152]{1,0:T(8,128)(2,1)S(1)}, u32[]{:S(2)}, u32[]{:S(2)}) %collective-permute-start.14) | collective-permute-done | bytes 663584 | tf_op jit(solution)/shard_map/ppermute | solution.py:573
  70.5 1.9 %collective-permute-done.15.refs_1_.refs_3_ = bf16[288,1152]{1,0:T(8,128)(2,1)S(1)} collective-permute-done((bf16[288,1152]{1,0:T(8,128)(2,1)S(1)}, bf16[288,1152]{1,0:T(8,128)(2,1)S(1)}, u32[]{:S(2)}, u32[]{:S(2)}) %collective-permute-start.15) | collective-permute-done | bytes 663584 | tf_op jit(solution)/shard_map/ppermute | solution.py:569
  72.4 0.2 relay.3
  72.6 1.6 %collective-permute-start.20 = (bf16[144,1152]{1,0:T(8,128)(2,1)S(1)}, bf16[144,1152]{1,0:T(8,128)(2,1)S(1)}, u32[]{:S(2)}, u32[]{:S(2)}) collective-permute-start(bf16[144,1152]{1,0:T(8,128)(2,1)S(1)} %get-tuple-element.97), channel_id=1, source_target_pairs={{0,3},{1,0},{2,1},{3,2},{4,7},{5,4},{6,5},{7,6},{8,11},{9,8},{10,9... | collective-permute-start | bytes 995336 | tf_op jit(solution)/shard_map/ppermute | solution.py:573
  74.2 2.7 %collective-permute-start.21 = (bf16[144,1152]{1,0:T(8,128)(2,1)S(1)}, bf16[144,1152]{1,0:T(8,128)(2,1)S(1)}, u32[]{:S(2)}, u32[]{:S(2)}) collective-permute-start(bf16[144,1152]{1,0:T(8,128)(2,1)S(1)} %get-tuple-element.98), channel_id=1, source_target_pairs={{0,96},{16,112},{32,0},{48,16},{64,32},{80,48},{96,64},{112,80},{1... | collective-permute-start | bytes 995336 | tf_op jit(solution)/shard_map/ppermute | solution.py:569
  76.9 3.6 %collective-permute-done.18.refs_4_ = bf16[144,1152]{1,0:T(8,128)(2,1)S(1)} collective-permute-done((bf16[144,1152]{1,0:T(8,128)(2,1)S(1)}, bf16[144,1152]{1,0:T(8,128)(2,1)S(1)}, u32[]{:S(2)}, u32[]{:S(2)}) %collective-permute-start.18) | collective-permute-done | bytes 331808 | tf_op jit(solution)/shard_map/ppermute | solution.py:573
  80.4 1.1 collective-permute-done.19.refs_5_
  81.5 0.7 collective-permute-done.21.refs_7_
  82.2 0.5 first_sum.1
  82.7 2.3 %collective-permute-start.22 = (bf16[72,1152]{1,0:T(8,128)(2,1)S(1)}, bf16[72,1152]{1,0:T(8,128)(2,1)S(1)}, u32[]{:S(2)}, u32[]{:S(2)}) collective-permute-start(bf16[72,1152]{1,0:T(8,128)(2,1)S(1)} %get-tuple-element.103), channel_id=1, source_target_pairs={{0,64},{16,80},{32,96},{48,112},{64,0},{80,16},{96,32},{112,48},{1... | collective-permute-start | bytes 497672 | tf_op jit(solution)/shard_map/ppermute | solution.py:569
  85.0 1.8 %collective-permute-start.24 = (bf16[72,1152]{1,0:T(8,128)(2,1)S(1)}, bf16[72,1152]{1,0:T(8,128)(2,1)S(1)}, u32[]{:S(2)}, u32[]{:S(2)}) collective-permute-start(bf16[72,1152]{1,0:T(8,128)(2,1)S(1)} %get-tuple-element.105), channel_id=1, source_target_pairs={{0,32},{16,48},{32,64},{48,80},{64,96},{80,112},{96,0},{112,16},{1... | collective-permute-start | bytes 497672 | tf_op jit(solution)/shard_map/ppermute | solution.py:569
  86.8 1.2 collective-permute-start.25
  88.0 0.9 collective-permute-start.26
  88.9 1.5 %collective-permute-start.27 = (bf16[72,1152]{1,0:T(8,128)(2,1)S(1)}, bf16[72,1152]{1,0:T(8,128)(2,1)S(1)}, u32[]{:S(2)}, u32[]{:S(2)}) collective-permute-start(bf16[72,1152]{1,0:T(8,128)(2,1)S(1)} %get-tuple-element.108), channel_id=1, source_target_pairs={{0,3},{1,0},{2,1},{3,2},{4,7},{5,4},{6,5},{7,6},{8,11},{9,8},{10,9... | collective-permute-start | bytes 497672 | tf_op jit(solution)/shard_map/ppermute | solution.py:573
  90.4 0.6 collective-permute-done.23.refs_3_
  91.0 2.1 %collective-permute-done.25.refs_5_ = bf16[72,1152]{1,0:T(8,128)(2,1)S(1)} collective-permute-done((bf16[72,1152]{1,0:T(8,128)(2,1)S(1)}, bf16[72,1152]{1,0:T(8,128)(2,1)S(1)}, u32[]{:S(2)}, u32[]{:S(2)}) %collective-permute-start.25) | collective-permute-done | bytes 165920 | tf_op jit(solution)/shard_map/ppermute | solution.py:573
  93.1 0.7 collective-permute-done.26.refs_6_
  93.8 0.2 second_sum.1
  94.1 5.5 %collective-permute-start.28 = (bf16[40,1152]{1,0:T(8,128)(2,1)S(1)}, bf16[40,1152]{1,0:T(8,128)(2,1)S(1)}, u32[]{:S(2)}, u32[]{:S(2)}) collective-permute-start(bf16[40,1152]{1,0:T(8,128)(2,1)S(1)} %get-tuple-element.110), channel_id=1, source_target_pairs={{0,8},{1,9},{2,10},{3,11},{4,12},{5,13},{6,14},{7,15},{8,128},{9,1... | collective-permute-start | bytes 276488 | tf_op jit(solution)/shard_map/ppermute | solution.py:584
  99.5 2.7 %collective-permute-start.30 = (bf16[40,1152]{1,0:T(8,128)(2,1)S(1)}, bf16[40,1152]{1,0:T(8,128)(2,1)S(1)}, u32[]{:S(2)}, u32[]{:S(2)}) collective-permute-start(bf16[40,1152]{1,0:T(8,128)(2,1)S(1)} %get-tuple-element.112), channel_id=1, source_target_pairs={{0,140},{1,141},{2,142},{3,143},{4,0},{5,1},{6,2},{7,3},{8,4},{9,5... | collective-permute-start | bytes 276488 | tf_op jit(solution)/shard_map/ppermute | solution.py:584
  102.2 2.0 %collective-permute-done.29.refs_2_ = bf16[40,1152]{1,0:T(8,128)(2,1)S(1)} collective-permute-done((bf16[40,1152]{1,0:T(8,128)(2,1)S(1)}, bf16[40,1152]{1,0:T(8,128)(2,1)S(1)}, u32[]{:S(2)}, u32[]{:S(2)}) %collective-permute-start.29) | collective-permute-done | bytes 92192 | tf_op jit(solution)/shard_map/ppermute | solution.py:584
  104.2 1.0 collective-permute-start.31
  105.3 6.6 %collective-permute-done.31.refs_1_ = bf16[40,1152]{1,0:T(8,128)(2,1)S(1)} collective-permute-done((bf16[40,1152]{1,0:T(8,128)(2,1)S(1)}, bf16[40,1152]{1,0:T(8,128)(2,1)S(1)}, u32[]{:S(2)}, u32[]{:S(2)}) %collective-permute-start.31) | collective-permute-done | bytes 92192 | tf_op jit(solution)/shard_map/ppermute | solution.py:565
  111.9 2.1 %collective-permute-start.34 = (bf16[40,1152]{1,0:T(8,128)(2,1)S(1)}, bf16[40,1152]{1,0:T(8,128)(2,1)S(1)}, u32[]{:S(2)}, u32[]{:S(2)}) collective-permute-start(bf16[40,1152]{1,0:T(8,128)(2,1)S(1)} %plain_sum.3.refs_0_), channel_id=1, source_target_pairs={{0,64},{16,80},{32,96},{48,112},{64,0},{80,16},{96,32},{112,48},{1... | collective-permute-start | bytes 276488 | tf_op jit(solution)/shard_map/ppermute | solution.py:569
  114.0 2.1 %collective-permute-start.33 = (bf16[40,1152]{1,0:T(8,128)(2,1)S(1)}, bf16[40,1152]{1,0:T(8,128)(2,1)S(1)}, u32[]{:S(2)}, u32[]{:S(2)}) collective-permute-start(bf16[40,1152]{1,0:T(8,128)(2,1)S(1)} %plain_sum.3.refs_0_), channel_id=1, source_target_pairs={{0,96},{16,112},{32,0},{48,16},{64,32},{80,48},{96,64},{112,80},{1... | collective-permute-start | bytes 276488 | tf_op jit(solution)/shard_map/ppermute | solution.py:569
  116.1 1.0 collective-permute-done.34.refs_3_
  117.2 1.7 %collective-permute-done.33.refs_2_ = bf16[40,1152]{1,0:T(8,128)(2,1)S(1)} collective-permute-done((bf16[40,1152]{1,0:T(8,128)(2,1)S(1)}, bf16[40,1152]{1,0:T(8,128)(2,1)S(1)}, u32[]{:S(2)}, u32[]{:S(2)}) %collective-permute-start.33) | collective-permute-done | bytes 92192 | tf_op jit(solution)/shard_map/ppermute | solution.py:569
  118.9 1.9 %collective-permute-done.32.refs_1_ = bf16[40,1152]{1,0:T(8,128)(2,1)S(1)} collective-permute-done((bf16[40,1152]{1,0:T(8,128)(2,1)S(1)}, bf16[40,1152]{1,0:T(8,128)(2,1)S(1)}, u32[]{:S(2)}, u32[]{:S(2)}) %collective-permute-start.32) | collective-permute-done | bytes 92192 | tf_op jit(solution)/shard_map/ppermute | solution.py:569
  120.8 8.7 %collective-permute-start.35 = (bf16[4,40,1152]{2,1,0:T(8,128)(2,1)S(1)}, bf16[4,40,1152]{2,1,0:T(8,128)(2,1)S(1)}, u32[]{:S(2)}, u32[]{:S(2)}) collective-permute-start(bf16[4,40,1152]{2,1,0:T(8,128)(2,1)S(1)} %stack.1.mine), channel_id=1, source_target_pairs={{0,16},{16,0},{32,48},{48,32},{64,80},{80,64},{96,112},{112,96},{1... | collective-permute-start | bytes 1105928 | tf_op jit(solution)/shard_map/ppermute | solution.py:561
  129.5 1.3 collective-permute-done.35.other
  130.8 1.3 last.1
  (42 shorter events, 0.5 us)
Async XLA Ops:
  1.6 10.5 %copy-start.2 = (f32[1152,8]{0,1:T(8,128)S(1)}, f32[1152,8]{0,1:T(8,128)}, u32[]{:S(2)}) copy-start(f32[1152,8]{0,1:T(8,128)} %param.15) | copy-start | bytes 110596
  1.6 10.5 %copy-start.3 = (f32[1152]{0:T(1024)S(1)}, f32[1152]{0:T(1024)}, u32[]{:S(2)}) copy-start(f32[1152]{0:T(1024)} %ln_ref.1) | copy-start | bytes 13828
  1.6 10.5 %copy-start.4 = (f32[1152]{0:T(1024)S(1)}, f32[1152]{0:T(1024)}, u32[]{:S(2)}) copy-start(f32[1152]{0:T(1024)} %og_ref.1) | copy-start | bytes 13828
  1.6 10.5 %copy-start.5 = (f32[1,4,8]{2,1,0:T(4,128)S(1)}, f32[1,4,8]{2,1,0:T(4,128)}, u32[]{:S(2)}) copy-start(f32[1,4,8]{2,1,0:T(4,128)} %param.10) | copy-start | bytes 388
  1.6 10.5 %copy-start.6 = (s32[1,4]{1,0:T(1,128)S(1)}, s32[1,4]{1,0:T(1,128)}, u32[]{:S(2)}) copy-start(s32[1,4]{1,0:T(1,128)} %lens_ref.1) | copy-start | bytes 52
  1.6 10.9 %copy-start.1 = (bf16[1,2,64,1152]{3,2,1,0:T(8,128)(2,1)S(1)}, bf16[1,2,64,1152]{3,2,1,0:T(8,128)(2,1)}, u32[]{:S(2)}) copy-start(bf16[1,2,64,1152]{3,2,1,0:T(8,128)(2,1)} %param.8) | copy-start | bytes 884740
  1.6 17.1 %copy-start = (bf16[1152,1152]{1,0:T(8,128)(2,1)S(1)}, bf16[1152,1152]{1,0:T(8,128)(2,1)}, u32[]{:S(2)}) copy-start(bf16[1152,1152]{1,0:T(8,128)(2,1)} %refs_1_.3) | copy-start | bytes 7962628
  1.7 10.9 %collective-permute-start = (bf16[2,4,8,1152]{3,2,1,0:T(8,128)(2,1)S(1)}, bf16[2,4,8,1152]{3,2,1,0:T(8,128)(2,1)S(1)}, u32[]{:S(2)}, u32[]{:S(2)}) collective-permute-start(bf16[2,4,8,1152]{3,2,1,0:T(8,128)(2,1)S(1)} %dynamic-slice_bitcast_fusion.refs_2_), channel_id=1, source_target_pairs={{0,128},{16,144},{32,160},{48,176},{64,192},{80,208},{96,224},{112... | collective-permute-start | bytes 442376 | tf_op jit(solution)/shard_map/ppermute | solution.py:565
  12.5 8.0 %collective-permute-start.1 = (bf16[4,8,1152]{2,1,0:T(8,128)(2,1)S(1)}, bf16[4,8,1152]{2,1,0:T(8,128)(2,1)S(1)}, u32[]{:S(2)}, u32[]{:S(2)}) collective-permute-start(bf16[4,8,1152]{2,1,0:T(8,128)(2,1)S(1)} %get-tuple-element.62), channel_id=1, source_target_pairs={{0,64},{16,80},{32,96},{48,112},{64,0},{80,16},{96,32},{112,48},{1... | collective-permute-start | bytes 221192 | tf_op jit(solution)/shard_map/ppermute | solution.py:569
  16.1 4.7 %collective-permute-start.2 = (bf16[4,8,1152]{2,1,0:T(8,128)(2,1)S(1)}, bf16[4,8,1152]{2,1,0:T(8,128)(2,1)S(1)}, u32[]{:S(2)}, u32[]{:S(2)}) collective-permute-start(bf16[4,8,1152]{2,1,0:T(8,128)(2,1)S(1)} %get-tuple-element.63), channel_id=1, source_target_pairs={{0,32},{16,48},{32,64},{48,80},{64,96},{80,112},{96,0},{112,16},{1... | collective-permute-start | bytes 221192 | tf_op jit(solution)/shard_map/ppermute | solution.py:569
  16.5 4.3 %collective-permute-start.3 = (bf16[4,8,1152]{2,1,0:T(8,128)(2,1)S(1)}, bf16[4,8,1152]{2,1,0:T(8,128)(2,1)S(1)}, u32[]{:S(2)}, u32[]{:S(2)}) collective-permute-start(bf16[4,8,1152]{2,1,0:T(8,128)(2,1)S(1)} %get-tuple-element.64), channel_id=1, source_target_pairs={{0,96},{16,112},{32,0},{48,16},{64,32},{80,48},{96,64},{112,80},{1... | collective-permute-start | bytes 221192 | tf_op jit(solution)/shard_map/ppermute | solution.py:569
  20.9 3.5 %collective-permute-start.4 = (bf16[8,8,1152]{2,1,0:T(8,128)(2,1)S(1)}, bf16[8,8,1152]{2,1,0:T(8,128)(2,1)S(1)}, u32[]{:S(2)}, u32[]{:S(2)}) collective-permute-start(bf16[8,8,1152]{2,1,0:T(8,128)(2,1)S(1)} %get-tuple-element.66), channel_id=1, source_target_pairs={{0,16},{16,0},{32,48},{48,32},{64,80},{80,64},{96,112},{112,96},{1... | collective-permute-start | bytes 442376 | tf_op jit(solution)/shard_map/ppermute | solution.py:561
  28.2 1.2 collective-permute-start.5
  29.4 8.7 %collective-permute-start.6 = (f32[8,8]{1,0:T(8,128)S(1)}, f32[8,8]{1,0:T(8,128)S(1)}, u32[]{:S(2)}, u32[]{:S(2)}) collective-permute-start(f32[8,8]{1,0:T(8,128)S(1)} %pair_sum.2.a), channel_id=1, source_target_pairs={{0,128},{16,144},{32,160},{48,176},{64,192},{80,208},{96,224},{112... | collective-permute-start | bytes 776 | tf_op jit(solution)/shard_map/ppermute | solution.py:565
  38.2 5.3 %collective-permute-start.9 = (f32[8,8]{1,0:T(8,128)S(1)}, f32[8,8]{1,0:T(8,128)S(1)}, u32[]{:S(2)}, u32[]{:S(2)}) collective-permute-start(f32[8,8]{1,0:T(8,128)S(1)} %pair_sum.3.t0), channel_id=1, source_target_pairs={{0,64},{16,80},{32,96},{48,112},{64,0},{80,16},{96,32},{112,48},{1... | collective-permute-start | bytes 776 | tf_op jit(solution)/shard_map/ppermute | solution.py:569
  39.4 4.1 %collective-permute-start.8 = (f32[8,8]{1,0:T(8,128)S(1)}, f32[8,8]{1,0:T(8,128)S(1)}, u32[]{:S(2)}, u32[]{:S(2)}) collective-permute-start(f32[8,8]{1,0:T(8,128)S(1)} %pair_sum.3.t0), channel_id=1, source_target_pairs={{0,96},{16,112},{32,0},{48,16},{64,32},{80,48},{96,64},{112,80},{1... | collective-permute-start | bytes 776 | tf_op jit(solution)/shard_map/ppermute | solution.py:569
  41.1 3.7 %collective-permute-start.7 = (f32[8,8]{1,0:T(8,128)S(1)}, f32[8,8]{1,0:T(8,128)S(1)}, u32[]{:S(2)}, u32[]{:S(2)}) collective-permute-start(f32[8,8]{1,0:T(8,128)S(1)} %pair_sum.3.t0), channel_id=1, source_target_pairs={{0,32},{16,48},{32,64},{48,80},{64,96},{80,112},{96,0},{112,16},{1... | collective-permute-start | bytes 776 | tf_op jit(solution)/shard_map/ppermute | solution.py:569
  41.7 9.0 %collective-permute-start.10 = (bf16[2,1152,128]{2,1,0:T(8,128)(2,1)S(1)}, bf16[2,1152,128]{2,1,0:T(8,128)(2,1)S(1)}, u32[]{:S(2)}, u32[]{:S(2)}) collective-permute-start(bf16[2,1152,128]{2,1,0:T(8,128)(2,1)S(1)} %get-tuple-element.82), channel_id=1, source_target_pairs={{0,16},{16,0},{32,48},{48,32},{64,80},{80,64},{96,112},{112,96},{1... | collective-permute-start | bytes 1769480 | tf_op jit(solution)/shard_map/ppermute | solution.py:561
  48.1 4.2 %collective-permute-start.11 = (bf16[2,128,1152]{2,1,0:T(8,128)(2,1)S(1)}, bf16[2,128,1152]{2,1,0:T(8,128)(2,1)S(1)}, u32[]{:S(2)}, u32[]{:S(2)}) collective-permute-start(bf16[2,128,1152]{2,1,0:T(8,128)(2,1)S(1)} %get-tuple-element.84), channel_id=1, source_target_pairs={{0,16},{16,0},{32,48},{48,32},{64,80},{80,64},{96,112},{112,96},{1... | collective-permute-start | bytes 1769480 | tf_op jit(solution)/shard_map/ppermute | solution.py:561
  54.1 16.5 %collective-permute-start.14 = (bf16[288,1152]{1,0:T(8,128)(2,1)S(1)}, bf16[288,1152]{1,0:T(8,128)(2,1)S(1)}, u32[]{:S(2)}, u32[]{:S(2)}) collective-permute-start(bf16[288,1152]{1,0:T(8,128)(2,1)S(1)} %get-tuple-element.87), channel_id=1, source_target_pairs={{0,3},{1,0},{2,1},{3,2},{4,7},{5,4},{6,5},{7,6},{8,11},{9,8},{10,9... | collective-permute-start | bytes 1990664 | tf_op jit(solution)/shard_map/ppermute | solution.py:573
  56.6 15.8 %collective-permute-start.15 = (bf16[288,1152]{1,0:T(8,128)(2,1)S(1)}, bf16[288,1152]{1,0:T(8,128)(2,1)S(1)}, u32[]{:S(2)}, u32[]{:S(2)}) collective-permute-start(bf16[288,1152]{1,0:T(8,128)(2,1)S(1)} %get-tuple-element.88), channel_id=1, source_target_pairs={{0,96},{16,112},{32,0},{48,16},{64,32},{80,48},{96,64},{112,80},{1... | collective-permute-start | bytes 1990664 | tf_op jit(solution)/shard_map/ppermute | solution.py:569
  56.6 9.6 %collective-permute-start.16 = (bf16[144,1152]{1,0:T(8,128)(2,1)S(1)}, bf16[144,1152]{1,0:T(8,128)(2,1)S(1)}, u32[]{:S(2)}, u32[]{:S(2)}) collective-permute-start(bf16[144,1152]{1,0:T(8,128)(2,1)S(1)} %get-tuple-element.89), channel_id=1, source_target_pairs={{0,1},{1,2},{2,3},{3,0},{4,5},{5,6},{6,7},{7,4},{8,9},{9,10},{10,1... | collective-permute-start | bytes 995336 | tf_op jit(solution)/shard_map/ppermute | solution.py:573
  56.6 11.0 %collective-permute-start.17 = (bf16[144,1152]{1,0:T(8,128)(2,1)S(1)}, bf16[144,1152]{1,0:T(8,128)(2,1)S(1)}, u32[]{:S(2)}, u32[]{:S(2)}) collective-permute-start(bf16[144,1152]{1,0:T(8,128)(2,1)S(1)} %get-tuple-element.90), channel_id=1, source_target_pairs={{0,32},{16,48},{32,64},{48,80},{64,96},{80,112},{96,0},{112,16},{1... | collective-permute-start | bytes 995336 | tf_op jit(solution)/shard_map/ppermute | solution.py:569
  58.1 16.1 %collective-permute-start.12 = (bf16[144,1152]{1,0:T(8,128)(2,1)S(1)}, bf16[144,1152]{1,0:T(8,128)(2,1)S(1)}, u32[]{:S(2)}, u32[]{:S(2)}) collective-permute-start(bf16[144,1152]{1,0:T(8,128)(2,1)S(1)} %get-tuple-element.85), channel_id=1, source_target_pairs={{0,1},{1,2},{2,3},{3,0},{4,5},{5,6},{6,7},{7,4},{8,9},{9,10},{10,1... | collective-permute-start | bytes 995336 | tf_op jit(solution)/shard_map/ppermute | solution.py:573
  66.2 10.7 %collective-permute-start.13 = (bf16[144,1152]{1,0:T(8,128)(2,1)S(1)}, bf16[144,1152]{1,0:T(8,128)(2,1)S(1)}, u32[]{:S(2)}, u32[]{:S(2)}) collective-permute-start(bf16[144,1152]{1,0:T(8,128)(2,1)S(1)} %get-tuple-element.86), channel_id=1, source_target_pairs={{0,32},{16,48},{32,64},{48,80},{64,96},{80,112},{96,0},{112,16},{1... | collective-permute-start | bytes 995336 | tf_op jit(solution)/shard_map/ppermute | solution.py:569
  67.8 12.6 %collective-permute-start.18 = (bf16[144,1152]{1,0:T(8,128)(2,1)S(1)}, bf16[144,1152]{1,0:T(8,128)(2,1)S(1)}, u32[]{:S(2)}, u32[]{:S(2)}) collective-permute-start(bf16[144,1152]{1,0:T(8,128)(2,1)S(1)} %get-tuple-element.93), channel_id=1, source_target_pairs={{0,1},{1,2},{2,3},{3,0},{4,5},{5,6},{6,7},{7,4},{8,9},{9,10},{10,1... | collective-permute-start | bytes 995336 | tf_op jit(solution)/shard_map/ppermute | solution.py:573
  70.5 11.0 %collective-permute-start.19 = (bf16[144,1152]{1,0:T(8,128)(2,1)S(1)}, bf16[144,1152]{1,0:T(8,128)(2,1)S(1)}, u32[]{:S(2)}, u32[]{:S(2)}) collective-permute-start(bf16[144,1152]{1,0:T(8,128)(2,1)S(1)} %get-tuple-element.94), channel_id=1, source_target_pairs={{0,32},{16,48},{32,64},{48,80},{64,96},{80,112},{96,0},{112,16},{1... | collective-permute-start | bytes 995336 | tf_op jit(solution)/shard_map/ppermute | solution.py:569
  72.6 8.9 %collective-permute-start.20 = (bf16[144,1152]{1,0:T(8,128)(2,1)S(1)}, bf16[144,1152]{1,0:T(8,128)(2,1)S(1)}, u32[]{:S(2)}, u32[]{:S(2)}) collective-permute-start(bf16[144,1152]{1,0:T(8,128)(2,1)S(1)} %get-tuple-element.97), channel_id=1, source_target_pairs={{0,3},{1,0},{2,1},{3,2},{4,7},{5,4},{6,5},{7,6},{8,11},{9,8},{10,9... | collective-permute-start | bytes 995336 | tf_op jit(solution)/shard_map/ppermute | solution.py:573
  74.2 8.0 %collective-permute-start.21 = (bf16[144,1152]{1,0:T(8,128)(2,1)S(1)}, bf16[144,1152]{1,0:T(8,128)(2,1)S(1)}, u32[]{:S(2)}, u32[]{:S(2)}) collective-permute-start(bf16[144,1152]{1,0:T(8,128)(2,1)S(1)} %get-tuple-element.98), channel_id=1, source_target_pairs={{0,96},{16,112},{32,0},{48,16},{64,32},{80,48},{96,64},{112,80},{1... | collective-permute-start | bytes 995336 | tf_op jit(solution)/shard_map/ppermute | solution.py:569
  82.7 6.1 %collective-permute-start.22 = (bf16[72,1152]{1,0:T(8,128)(2,1)S(1)}, bf16[72,1152]{1,0:T(8,128)(2,1)S(1)}, u32[]{:S(2)}, u32[]{:S(2)}) collective-permute-start(bf16[72,1152]{1,0:T(8,128)(2,1)S(1)} %get-tuple-element.103), channel_id=1, source_target_pairs={{0,64},{16,80},{32,96},{48,112},{64,0},{80,16},{96,32},{112,48},{1... | collective-permute-start | bytes 497672 | tf_op jit(solution)/shard_map/ppermute | solution.py:569
  85.0 6.0 %collective-permute-start.23 = (bf16[72,1152]{1,0:T(8,128)(2,1)S(1)}, bf16[72,1152]{1,0:T(8,128)(2,1)S(1)}, u32[]{:S(2)}, u32[]{:S(2)}) collective-permute-start(bf16[72,1152]{1,0:T(8,128)(2,1)S(1)} %get-tuple-element.104), channel_id=1, source_target_pairs={{0,2},{1,3},{2,0},{3,1},{4,6},{5,7},{6,4},{7,5},{8,10},{9,11},{10,... | collective-permute-start | bytes 497672 | tf_op jit(solution)/shard_map/ppermute | solution.py:573
  85.0 6.0 %collective-permute-start.24 = (bf16[72,1152]{1,0:T(8,128)(2,1)S(1)}, bf16[72,1152]{1,0:T(8,128)(2,1)S(1)}, u32[]{:S(2)}, u32[]{:S(2)}) collective-permute-start(bf16[72,1152]{1,0:T(8,128)(2,1)S(1)} %get-tuple-element.105), channel_id=1, source_target_pairs={{0,32},{16,48},{32,64},{48,80},{64,96},{80,112},{96,0},{112,16},{1... | collective-permute-start | bytes 497672 | tf_op jit(solution)/shard_map/ppermute | solution.py:569
  86.8 6.3 %collective-permute-start.25 = (bf16[72,1152]{1,0:T(8,128)(2,1)S(1)}, bf16[72,1152]{1,0:T(8,128)(2,1)S(1)}, u32[]{:S(2)}, u32[]{:S(2)}) collective-permute-start(bf16[72,1152]{1,0:T(8,128)(2,1)S(1)} %get-tuple-element.106), channel_id=1, source_target_pairs={{0,1},{1,2},{2,3},{3,0},{4,5},{5,6},{6,7},{7,4},{8,9},{9,10},{10,1... | collective-permute-start | bytes 497672 | tf_op jit(solution)/shard_map/ppermute | solution.py:573
  88.0 5.8 %collective-permute-start.26 = (bf16[72,1152]{1,0:T(8,128)(2,1)S(1)}, bf16[72,1152]{1,0:T(8,128)(2,1)S(1)}, u32[]{:S(2)}, u32[]{:S(2)}) collective-permute-start(bf16[72,1152]{1,0:T(8,128)(2,1)S(1)} %get-tuple-element.107), channel_id=1, source_target_pairs={{0,96},{16,112},{32,0},{48,16},{64,32},{80,48},{96,64},{112,80},{1... | collective-permute-start | bytes 497672 | tf_op jit(solution)/shard_map/ppermute | solution.py:569
  88.9 5.0 %collective-permute-start.27 = (bf16[72,1152]{1,0:T(8,128)(2,1)S(1)}, bf16[72,1152]{1,0:T(8,128)(2,1)S(1)}, u32[]{:S(2)}, u32[]{:S(2)}) collective-permute-start(bf16[72,1152]{1,0:T(8,128)(2,1)S(1)} %get-tuple-element.108), channel_id=1, source_target_pairs={{0,3},{1,0},{2,1},{3,2},{4,7},{5,4},{6,5},{7,6},{8,11},{9,8},{10,9... | collective-permute-start | bytes 497672 | tf_op jit(solution)/shard_map/ppermute | solution.py:573
  94.1 8.1 %collective-permute-start.28 = (bf16[40,1152]{1,0:T(8,128)(2,1)S(1)}, bf16[40,1152]{1,0:T(8,128)(2,1)S(1)}, u32[]{:S(2)}, u32[]{:S(2)}) collective-permute-start(bf16[40,1152]{1,0:T(8,128)(2,1)S(1)} %get-tuple-element.110), channel_id=1, source_target_pairs={{0,8},{1,9},{2,10},{3,11},{4,12},{5,13},{6,14},{7,15},{8,128},{9,1... | collective-permute-start | bytes 276488 | tf_op jit(solution)/shard_map/ppermute | solution.py:584
  99.5 4.7 %collective-permute-start.29 = (bf16[40,1152]{1,0:T(8,128)(2,1)S(1)}, bf16[40,1152]{1,0:T(8,128)(2,1)S(1)}, u32[]{:S(2)}, u32[]{:S(2)}) collective-permute-start(bf16[40,1152]{1,0:T(8,128)(2,1)S(1)} %get-tuple-element.111), channel_id=1, source_target_pairs={{0,4},{1,5},{2,6},{3,7},{4,8},{5,9},{6,10},{7,11},{8,12},{9,13},{1... | collective-permute-start | bytes 276488 | tf_op jit(solution)/shard_map/ppermute | solution.py:584
  99.5 4.7 %collective-permute-start.30 = (bf16[40,1152]{1,0:T(8,128)(2,1)S(1)}, bf16[40,1152]{1,0:T(8,128)(2,1)S(1)}, u32[]{:S(2)}, u32[]{:S(2)}) collective-permute-start(bf16[40,1152]{1,0:T(8,128)(2,1)S(1)} %get-tuple-element.112), channel_id=1, source_target_pairs={{0,140},{1,141},{2,142},{3,143},{4,0},{5,1},{6,2},{7,3},{8,4},{9,5... | collective-permute-start | bytes 276488 | tf_op jit(solution)/shard_map/ppermute | solution.py:584
  104.2 7.6 %collective-permute-start.31 = (bf16[40,1152]{1,0:T(8,128)(2,1)S(1)}, bf16[40,1152]{1,0:T(8,128)(2,1)S(1)}, u32[]{:S(2)}, u32[]{:S(2)}) collective-permute-start(bf16[40,1152]{1,0:T(8,128)(2,1)S(1)} %plain_sum.2.refs_0_), channel_id=1, source_target_pairs={{0,128},{16,144},{32,160},{48,176},{64,192},{80,208},{96,224},{112... | collective-permute-start | bytes 276488 | tf_op jit(solution)/shard_map/ppermute | solution.py:565
  111.9 5.3 %collective-permute-start.34 = (bf16[40,1152]{1,0:T(8,128)(2,1)S(1)}, bf16[40,1152]{1,0:T(8,128)(2,1)S(1)}, u32[]{:S(2)}, u32[]{:S(2)}) collective-permute-start(bf16[40,1152]{1,0:T(8,128)(2,1)S(1)} %plain_sum.3.refs_0_), channel_id=1, source_target_pairs={{0,64},{16,80},{32,96},{48,112},{64,0},{80,16},{96,32},{112,48},{1... | collective-permute-start | bytes 276488 | tf_op jit(solution)/shard_map/ppermute | solution.py:569
  114.0 4.9 %collective-permute-start.33 = (bf16[40,1152]{1,0:T(8,128)(2,1)S(1)}, bf16[40,1152]{1,0:T(8,128)(2,1)S(1)}, u32[]{:S(2)}, u32[]{:S(2)}) collective-permute-start(bf16[40,1152]{1,0:T(8,128)(2,1)S(1)} %plain_sum.3.refs_0_), channel_id=1, source_target_pairs={{0,96},{16,112},{32,0},{48,16},{64,32},{80,48},{96,64},{112,80},{1... | collective-permute-start | bytes 276488 | tf_op jit(solution)/shard_map/ppermute | solution.py:569
  116.1 4.6 %collective-permute-start.32 = (bf16[40,1152]{1,0:T(8,128)(2,1)S(1)}, bf16[40,1152]{1,0:T(8,128)(2,1)S(1)}, u32[]{:S(2)}, u32[]{:S(2)}) collective-permute-start(bf16[40,1152]{1,0:T(8,128)(2,1)S(1)} %plain_sum.3.refs_0_), channel_id=1, source_target_pairs={{0,32},{16,48},{32,64},{48,80},{64,96},{80,112},{96,0},{112,16},{1... | collective-permute-start | bytes 276488 | tf_op jit(solution)/shard_map/ppermute | solution.py:569
  120.8 10.0 %collective-permute-start.35 = (bf16[4,40,1152]{2,1,0:T(8,128)(2,1)S(1)}, bf16[4,40,1152]{2,1,0:T(8,128)(2,1)S(1)}, u32[]{:S(2)}, u32[]{:S(2)}) collective-permute-start(bf16[4,40,1152]{2,1,0:T(8,128)(2,1)S(1)} %stack.1.mine), channel_id=1, source_target_pairs={{0,16},{16,0},{32,48},{48,32},{64,80},{80,64},{96,112},{112,96},{1... | collective-permute-start | bytes 1105928 | tf_op jit(solution)/shard_map/ppermute | solution.py:561

commit v4 on v1

--- a/solution.py
+++ b/solution.py
@@ -295,7 +295,7 @@
 
 
 def backward_kernel(
-    t0, t1, t2, t3, small, proj_ref, p_ref, cen_ref, inv_ref, wo_ref,
+    total_ref, small, proj_ref, p_ref, cen_ref, inv_ref, wo_ref,
     scores_ref, keep_ref, send_ref,
     dq, dk, dv, wg, da_ref,
 ):
@@ -303,7 +303,7 @@
     count = jnp.ones((REWARDS, 8), f32)
     for c in range(CLIPS):
         count = jnp.where(clip_col == c, small[10:11, c : c + 1] * 64.0, count)
-    scores = ((t0[...] + t2[...]) + (t1[...] + t3[...])) / count
+    scores = total_ref[...] / count
     scores = scores[:, 0:CLIPS]
     for c in range(CLIPS):
         column = jnp.where(eye(), scores[:, c : c + 1], 0.0)
@@ -367,7 +367,7 @@
             shape((2, TOK, D), bf16),
             shape((2, TOK, D), bf16),
         ),
-        [VMEM] * 10,
+        [VMEM] * 7,
         [pltpu.VMEM((TOK, D), f32)] * 3
         + [
             pltpu.VMEM((HEADS, TOK, TOK), f32),
@@ -377,7 +377,7 @@
         "backward",
         flops=1_500_000_000,
         moved=8_000_000,
-    )(*totals, small, proj, p, centred, inv, w_out)
+    )(totals, small, proj, p, centred, inv, w_out)
 
 
 PARTS = ((2, 0), (2, 1), (1, 1), (3, 0), (1, 0), (3, 1))
@@ -554,6 +554,10 @@
 
 def to_core(block):
     return lax.ppermute(block, "tm", [(i, i ^ 1) for i in range(16)])
+
+
+def to_partner(block, bit):
+    return lax.ppermute(block, "tm", [(i, i ^ bit) for i in range(16)])
 
 
 def to_far(block):
@@ -614,8 +618,9 @@
     left_keep, left_send = turn(normed, attended)
     left_recv = to_core(left_send)
     partial = pair_sum(partial, to_far(partial), left_keep)
-    totals = [partial] + [along_y(partial, k) for k in (1, 2, 3)]
-    scores, right_keep, right_send = backward(totals, small, proj, p, centred, inv, weights[3])
+    for bit in (2, 4):
+        partial = pair_sum(partial, to_partner(partial, bit))
+    scores, right_keep, right_send = backward(partial, small, proj, p, centred, inv, weights[3])
     parts = gradient(left_keep, left_recv, right_keep, to_core(right_send))
     parts = second_sum(exchange(around(*parts)))
     part = plain_sum([parts[0]] + [around_z(parts[k], k) for k in (1, 2, 3)])

time: 129 us -> 132 us (1.023)
  starting transfers between devices: 71.2 us -> 73.4 us
    ppermute x18 -> x15, starting transfers between devices: 21.1 us -> 17.3 us  [along_y(): lax.ppermute(block, 'tm', [(i, i & 9 | i + 2 * k & 6) for i in range(16)])]
    ppermute x5, starting transfers between devices: 15.1 us -> 17.9 us  [to_core(): return lax.ppermute(block, 'tm', [(i, i ^ 1) for i in range(16)])]
    ppermute x0 -> x2, waiting for transfers between devices: none -> 2.33 us  [to_partner(): return lax.ppermute(block, 'tm', [(i, i ^ bit) for i in range(16)])]
    ppermute x0 -> x2, starting transfers between devices: none -> 2.13 us  [to_partner(): return lax.ppermute(block, 'tm', [(i, i ^ bit) for i in range(16)])]
    ppermute x18 -> x15, waiting for transfers between devices: 15.3 us -> 13.3 us  [along_y(): lax.ppermute(block, 'tm', [(i, i & 9 | i + 2 * k & 6) for i in range(16)])]
  transfers between devices with their start and end apart: 38 -> 37, of which waited for: 23 -> 23; matrix products, arithmetic and copies ran while one was open for 0% -> 0% of each run, Pallas kernels for 7% -> 6%
where the time goes in v4:
time: 132 us; the launch traced here: 131 us
  starting transfers between devices  73.4 us (56%)
  waiting for transfers between devices  39.9 us (30%)
  Pallas kernels  16.2 us (12%)
    ppermute x3, starting transfers between devices, to_far(): return lax.ppermute(block, 'tm', [(i, i ^ 8) for i in range(16)])  20.1 us
    ppermute x5, starting transfers between devices, to_core(): return lax.ppermute(block, 'tm', [(i, i ^ 1) for i in range(16)])  17.9 us
    ppermute x15, starting transfers between devices, along_y(): lax.ppermute(block, 'tm', [(i, i & 9 | i + 2 * k & 6) for i in range(16)])  17.3 us
    ppermute x9, waiting for transfers between devices, along_x(): lax.ppermute(block, 'dp', [(i, i & 12 | i + k & 3) for i in range(16)])  13.5 us
    ppermute x15, waiting for transfers between devices, along_y(): lax.ppermute(block, 'tm', [(i, i & 9 | i + 2 * k & 6) for i in range(16)])  13.3 us
    ppermute x9, starting transfers between devices, along_x(): lax.ppermute(block, 'dp', [(i, i & 12 | i + k & 3) for i in range(16)])  9.04 us
    ppermute x3, starting transfers between devices, around_z(): return lax.ppermute(block, ('tm', 'dp'), route)  6.92 us
    ppermute x5, waiting for transfers between devices, to_core(): return lax.ppermute(block, 'tm', [(i, i ^ 1) for i in range(16)])  4.77 us
  transfers between devices with their start and end apart: 37, of which 23 were waited for; matrix products, arithmetic and copies ran while one was open for 0% of the time, Pallas kernels for 6%

profile of v4, /device:TPU:1, one launch (start us, length us, event | category | flops | bytes accessed | tf_op | source)
XLA Modules:
  0.0 131.4 jit_solution(13401526042637814411)
XLA Ops:
  0.6 0.9 dynamic-slice_bitcast_fusion.refs_2_
  1.7 7.8 %collective-permute-start = (bf16[2,4,8,1152]{3,2,1,0:T(8,128)(2,1)S(1)}, bf16[2,4,8,1152]{3,2,1,0:T(8,128)(2,1)S(1)}, u32[]{:S(2)}, u32[]{:S(2)}) collective-permute-start(bf16[2,4,8,1152]{3,2,1,0:T(8,128)(2,1)S(1)} %dynamic-slice_bitcast_fusion.refs_2_), channel_id=1, source_target_pairs={{0,128},{16,144},{32,160},{48,176},{64,192},{80,208},{96,224},{112... | collective-permute-start | bytes 442376 | tf_op jit(solution)/shard_map/ppermute | solution.py:564
  9.5 2.6 %load.2 = (bf16[1152,1152]{1,0:T(8,128)(2,1)S(1)}, bf16[1152,1152]{1,0:T(8,128)(2,1)S(1)}, f32[8,128]{1,0:T(8,128)S(1)}) custom-call(bf16[1152,3456]{1,0:T(8,128)(2,1)} %refs_0_.3, bf16[1152,3456]{1,0:T(8,128)(2,1)} %refs_0_.3, bf16[2,4,8,1152]{3,2,1,0:T(8,128)(2,1)S(1)} %dynamic-slice_bitcast_fusion.refs_2_), custom_call_target="tpu_custom_call" | custom-call | bytes 10000000 | tf_op jit(solution)/shard_map/load/pallas_call | solution.py:172
  12.2 0.3 collective-permute-done.far_ref
  12.5 1.9 %collective-permute-start.1 = (bf16[4,8,1152]{2,1,0:T(8,128)(2,1)S(1)}, bf16[4,8,1152]{2,1,0:T(8,128)(2,1)S(1)}, u32[]{:S(2)}, u32[]{:S(2)}) collective-permute-start(bf16[4,8,1152]{2,1,0:T(8,128)(2,1)S(1)} %get-tuple-element.64), channel_id=1, source_target_pairs={{0,32},{16,48},{32,64},{48,80},{64,96},{80,112},{96,0},{112,16},{1... | collective-permute-start | bytes 221192 | tf_op jit(solution)/shard_map/ppermute | solution.py:568
  14.5 2.6 %collective-permute-start.2 = (bf16[4,8,1152]{2,1,0:T(8,128)(2,1)S(1)}, bf16[4,8,1152]{2,1,0:T(8,128)(2,1)S(1)}, u32[]{:S(2)}, u32[]{:S(2)}) collective-permute-start(bf16[4,8,1152]{2,1,0:T(8,128)(2,1)S(1)} %get-tuple-element.65), channel_id=1, source_target_pairs={{0,64},{16,80},{32,96},{48,112},{64,0},{80,16},{96,32},{112,48},{1... | collective-permute-start | bytes 221192 | tf_op jit(solution)/shard_map/ppermute | solution.py:568
  17.1 1.1 collective-permute-start.3
  18.1 1.8 %load.3 = (bf16[1152,1152]{1,0:T(8,128)(2,1)S(1)}, bf16[1152,1152]{1,0:T(8,128)(2,1)S(1)}, f32[8,128]{1,0:T(8,128)S(1)}) custom-call(bf16[1152,3456]{1,0:T(8,128)(2,1)} %refs_0_.3, bf16[1152,1152]{1,0:T(8,128)(2,1)S(1)} %copy-done, bf16[4,8,1152]{2,1,0:T(8,128)(2,1)S(1)} %get-tuple-element.62.refs_2_.refs_0_), custom_call_target="tpu_custom_call" | custom-call | bytes 10000000 | tf_op jit(solution)/shard_map/load/pallas_call | solution.py:172
  19.9 1.4 %collective-permute-done.3.refs_3_ = bf16[4,8,1152]{2,1,0:T(8,128)(2,1)S(1)} collective-permute-done((bf16[4,8,1152]{2,1,0:T(8,128)(2,1)S(1)}, bf16[4,8,1152]{2,1,0:T(8,128)(2,1)S(1)}, u32[]{:S(2)}, u32[]{:S(2)}) %collective-permute-start.3) | collective-permute-done | bytes 73760 | tf_op jit(solution)/shard_map/ppermute | solution.py:568
  21.4 2.1 %collective-permute-start.4 = (bf16[8,8,1152]{2,1,0:T(8,128)(2,1)S(1)}, bf16[8,8,1152]{2,1,0:T(8,128)(2,1)S(1)}, u32[]{:S(2)}, u32[]{:S(2)}) collective-permute-start(bf16[8,8,1152]{2,1,0:T(8,128)(2,1)S(1)} %get-tuple-element.68), channel_id=1, source_target_pairs={{0,16},{16,0},{32,48},{48,32},{64,80},{80,64},{96,112},{112,96},{1... | collective-permute-start | bytes 442376 | tf_op jit(solution)/shard_map/ppermute | solution.py:556
  23.5 1.0 collective-permute-done.4.x1
  24.5 3.8 %forward.1 = (bf16[128,1152]{1,0:T(8,128)(2,1)S(1)}, bf16[128,1152]{1,0:T(8,128)(2,1)S(1)}, bf16[128,3456]{1,0:T(8,128)(2,1)S(1)}, f32[16,128,128]{2,1,0:T(8,128...) custom-call(bf16[8,8,1152]{2,1,0:T(8,128)(2,1)S(1)} %get-tuple-element.67.x0, ...), custom_call_target="tpu_custom_call" | custom-call | flops 2000000000 | bytes 14000000 | tf_op jit(solution)/shard_map/forward/pallas_call | solution.py:241
  28.3 0.4 collective-permute-start.5
  28.7 0.8 collective-permute-done.5.b
  29.5 7.7 %collective-permute-start.6 = (f32[8,8]{1,0:T(8,128)S(1)}, f32[8,8]{1,0:T(8,128)S(1)}, u32[]{:S(2)}, u32[]{:S(2)}) collective-permute-start(f32[8,8]{1,0:T(8,128)S(1)} %pair_sum.4.a), channel_id=1, source_target_pairs={{0,128},{16,144},{32,160},{48,176},{64,192},{80,208},{96,224},{112... | collective-permute-start | bytes 776 | tf_op jit(solution)/shard_map/ppermute | solution.py:564
  37.2 0.5 turn.1
  37.7 0.5 collective-permute-done.6.b
  38.4 2.3 %collective-permute-done.7.b = f32[8,8]{1,0:T(8,128)S(1)} collective-permute-done((f32[8,8]{1,0:T(8,128)S(1)}, f32[8,8]{1,0:T(8,128)S(1)}, u32[]{:S(2)}, u32[]{:S(2)}) %collective-permute-start.7) | collective-permute-done | bytes 288 | tf_op jit(solution)/shard_map/ppermute | solution.py:560
  40.7 2.0 %collective-permute-start.8 = (f32[8,8]{1,0:T(8,128)S(1)}, f32[8,8]{1,0:T(8,128)S(1)}, u32[]{:S(2)}, u32[]{:S(2)}) collective-permute-start(f32[8,8]{1,0:T(8,128)S(1)} %pair_sum.6.a), channel_id=1, source_target_pairs={{0,64},{16,80},{32,96},{48,112},{64,0},{80,16},{96,32},{112,48},{1... | collective-permute-start | bytes 776 | tf_op jit(solution)/shard_map/ppermute | solution.py:560
  42.7 2.4 %collective-permute-start.9 = (bf16[2,1152,128]{2,1,0:T(8,128)(2,1)S(1)}, bf16[2,1152,128]{2,1,0:T(8,128)(2,1)S(1)}, u32[]{:S(2)}, u32[]{:S(2)}) collective-permute-start(bf16[2,1152,128]{2,1,0:T(8,128)(2,1)S(1)} %get-tuple-element.84), channel_id=1, source_target_pairs={{0,16},{16,0},{32,48},{48,32},{64,80},{80,64},{96,112},{112,96},{1... | collective-permute-start | bytes 1769480 | tf_op jit(solution)/shard_map/ppermute | solution.py:556
  45.1 3.3 %backward.1 = (f32[4,8]{1,0:T(4,128)}, bf16[2,128,1152]{2,1,0:T(8,128)(2,1)S(1)}, bf16[2,128,1152]{2,1,0:T(8,128)(2,1)S(1)}) custom-call(f32[8,8]{1,0:T(8,128)S(1)} %pair_sum.7.total_ref, f32[24,1152]{1,0:T(8,128)S(1)} %pack.1.small, bf16[128,3456]{1,0:T(8,128)(2,1)S(1)} %get-tuple-element.79.proj_ref, f32[16,128,128]{2,1,0:T(8,128)S(1)} %get-tuple-element.80.p_ref, ...), custom_call_target="tpu_custom_call" | custom-call | flops 1500000000 | bytes 8000000 | tf_op jit(solution)/shard_map/backward/pallas_call | solution.py:363
  48.3 3.1 %collective-permute-start.10 = (bf16[2,128,1152]{2,1,0:T(8,128)(2,1)S(1)}, bf16[2,128,1152]{2,1,0:T(8,128)(2,1)S(1)}, u32[]{:S(2)}, u32[]{:S(2)}) collective-permute-start(bf16[2,128,1152]{2,1,0:T(8,128)(2,1)S(1)} %get-tuple-element.86), channel_id=1, source_target_pairs={{0,16},{16,0},{32,48},{48,32},{64,80},{80,64},{96,112},{112,96},{1... | collective-permute-start | bytes 1769480 | tf_op jit(solution)/shard_map/ppermute | solution.py:556
  51.4 1.6 %collective-permute-done.10.rr = bf16[2,128,1152]{2,1,0:T(8,128)(2,1)S(1)} collective-permute-done((bf16[2,128,1152]{2,1,0:T(8,128)(2,1)S(1)}, bf16[2,128,1152]{2,1,0:T(8,128)(2,1)S(1)}, u32[]{:S(2)}, u32[]{:S(2)}) %collective-permute-start.10) | collective-permute-done | bytes 589856 | tf_op jit(solution)/shard_map/ppermute | solution.py:556
  53.1 1.7 %gradient.1 = (bf16[144,1152]{1,0:T(8,128)(2,1)S(1)}, bf16[144,1152]{1,0:T(8,128)(2,1)S(1)}, bf16[144,1152]{1,0:T(8,128)(2,1)S(1)}, bf16[144,1152]{1,0:T(8,128)(...) custom-call(bf16[2,1152,128]{2,1,0:T(8,128)(2,1)S(1)} %get-tuple-ele, ...), custom_call_target="tpu_custom_call" | custom-call | flops 1400000000 | bytes 8000000 | tf_op jit(solution)/shard_map/gradient/pallas_call | solution.py:402
  54.8 1.3 collective-permute-start.15
  56.2 1.5 %collective-permute-start.17 = (bf16[144,1152]{1,0:T(8,128)(2,1)S(1)}, bf16[144,1152]{1,0:T(8,128)(2,1)S(1)}, u32[]{:S(2)}, u32[]{:S(2)}) collective-permute-start(bf16[144,1152]{1,0:T(8,128)(2,1)S(1)} %get-tuple-element.93), channel_id=1, source_target_pairs={{0,3},{1,0},{2,1},{3,2},{4,7},{5,4},{6,5},{7,6},{8,11},{9,8},{10,9... | collective-permute-start | bytes 995336 | tf_op jit(solution)/shard_map/ppermute | solution.py:572
  57.7 2.5 %collective-permute-start.18 = (bf16[144,1152]{1,0:T(8,128)(2,1)S(1)}, bf16[144,1152]{1,0:T(8,128)(2,1)S(1)}, u32[]{:S(2)}, u32[]{:S(2)}) collective-permute-start(bf16[144,1152]{1,0:T(8,128)(2,1)S(1)} %get-tuple-element.94), channel_id=1, source_target_pairs={{0,96},{16,112},{32,0},{48,16},{64,32},{80,48},{96,64},{112,80},{1... | collective-permute-start | bytes 995336 | tf_op jit(solution)/shard_map/ppermute | solution.py:568
  60.2 4.9 %collective-permute-done.15.refs_0_ = bf16[144,1152]{1,0:T(8,128)(2,1)S(1)} collective-permute-done((bf16[144,1152]{1,0:T(8,128)(2,1)S(1)}, bf16[144,1152]{1,0:T(8,128)(2,1)S(1)}, u32[]{:S(2)}, u32[]{:S(2)}) %collective-permute-start.15) | collective-permute-done | bytes 331808 | tf_op jit(solution)/shard_map/ppermute | solution.py:572
  65.2 0.8 collective-permute-done.16.refs_1_
  66.0 1.5 %collective-permute-start.13 = (bf16[144,1152]{1,0:T(8,128)(2,1)S(1)}, bf16[144,1152]{1,0:T(8,128)(2,1)S(1)}, u32[]{:S(2)}, u32[]{:S(2)}) collective-permute-start(bf16[144,1152]{1,0:T(8,128)(2,1)S(1)} %get-tuple-element.89), channel_id=1, source_target_pairs={{0,3},{1,0},{2,1},{3,2},{4,7},{5,4},{6,5},{7,6},{8,11},{9,8},{10,9... | collective-permute-start | bytes 995336 | tf_op jit(solution)/shard_map/ppermute | solution.py:572
  67.5 1.6 %collective-permute-start.14 = (bf16[144,1152]{1,0:T(8,128)(2,1)S(1)}, bf16[144,1152]{1,0:T(8,128)(2,1)S(1)}, u32[]{:S(2)}, u32[]{:S(2)}) collective-permute-start(bf16[144,1152]{1,0:T(8,128)(2,1)S(1)} %get-tuple-element.90), channel_id=1, source_target_pairs={{0,96},{16,112},{32,0},{48,16},{64,32},{80,48},{96,64},{112,80},{1... | collective-permute-start | bytes 995336 | tf_op jit(solution)/shard_map/ppermute | solution.py:568
  69.1 0.3 relay.1
  69.4 0.3 collective-permute-start.19
  69.6 2.6 %collective-permute-done.11.refs_0_ = bf16[144,1152]{1,0:T(8,128)(2,1)S(1)} collective-permute-done((bf16[144,1152]{1,0:T(8,128)(2,1)S(1)}, bf16[144,1152]{1,0:T(8,128)(2,1)S(1)}, u32[]{:S(2)}, u32[]{:S(2)}) %collective-permute-start.11) | collective-permute-done | bytes 331808 | tf_op jit(solution)/shard_map/ppermute | solution.py:572
  72.3 1.3 collective-permute-done.12.refs_1_
  73.6 1.3 collective-permute-start.21
  74.9 1.3 collective-permute-start.22
  76.2 0.9 collective-permute-done.19.refs_4_
  77.1 4.3 %collective-permute-done.20.refs_5_ = bf16[144,1152]{1,0:T(8,128)(2,1)S(1)} collective-permute-done((bf16[144,1152]{1,0:T(8,128)(2,1)S(1)}, bf16[144,1152]{1,0:T(8,128)(2,1)S(1)}, u32[]{:S(2)}, u32[]{:S(2)}) %collective-permute-start.20) | collective-permute-done | bytes 331808 | tf_op jit(solution)/shard_map/ppermute | solution.py:568
  81.4 0.5 first_sum.1
  81.9 0.9 collective-permute-start.23
  82.9 1.7 %collective-permute-start.25 = (bf16[72,1152]{1,0:T(8,128)(2,1)S(1)}, bf16[72,1152]{1,0:T(8,128)(2,1)S(1)}, u32[]{:S(2)}, u32[]{:S(2)}) collective-permute-start(bf16[72,1152]{1,0:T(8,128)(2,1)S(1)} %get-tuple-element.109), channel_id=1, source_target_pairs={{0,96},{16,112},{32,0},{48,16},{64,32},{80,48},{96,64},{112,80},{1... | collective-permute-start | bytes 497672 | tf_op jit(solution)/shard_map/ppermute | solution.py:568
  84.6 2.7 %collective-permute-start.26 = (bf16[72,1152]{1,0:T(8,128)(2,1)S(1)}, bf16[72,1152]{1,0:T(8,128)(2,1)S(1)}, u32[]{:S(2)}, u32[]{:S(2)}) collective-permute-start(bf16[72,1152]{1,0:T(8,128)(2,1)S(1)} %get-tuple-element.110), channel_id=1, source_target_pairs={{0,3},{1,0},{2,1},{3,2},{4,7},{5,4},{6,5},{7,6},{8,11},{9,8},{10,9... | collective-permute-start | bytes 497672 | tf_op jit(solution)/shard_map/ppermute | solution.py:572
  87.3 0.4 collective-permute-start.27
  87.7 0.7 collective-permute-start.28
  88.4 2.9 %collective-permute-done.26.refs_5_ = bf16[72,1152]{1,0:T(8,128)(2,1)S(1)} collective-permute-done((bf16[72,1152]{1,0:T(8,128)(2,1)S(1)}, bf16[72,1152]{1,0:T(8,128)(2,1)S(1)}, u32[]{:S(2)}, u32[]{:S(2)}) %collective-permute-start.26) | collective-permute-done | bytes 165920 | tf_op jit(solution)/shard_map/ppermute | solution.py:572
  91.4 2.2 %collective-permute-done.27.refs_6_ = bf16[72,1152]{1,0:T(8,128)(2,1)S(1)} collective-permute-done((bf16[72,1152]{1,0:T(8,128)(2,1)S(1)}, bf16[72,1152]{1,0:T(8,128)(2,1)S(1)}, u32[]{:S(2)}, u32[]{:S(2)}) %collective-permute-start.27) | collective-permute-done | bytes 165920 | tf_op jit(solution)/shard_map/ppermute | solution.py:572
  93.6 0.7 collective-permute-done.28.refs_7_
  94.3 0.2 second_sum.1
  94.5 1.8 %collective-permute-start.29 = (bf16[40,1152]{1,0:T(8,128)(2,1)S(1)}, bf16[40,1152]{1,0:T(8,128)(2,1)S(1)}, u32[]{:S(2)}, u32[]{:S(2)}) collective-permute-start(bf16[40,1152]{1,0:T(8,128)(2,1)S(1)} %get-tuple-element.114), channel_id=1, source_target_pairs={{0,4},{1,5},{2,6},{3,7},{4,8},{5,9},{6,10},{7,11},{8,12},{9,13},{1... | collective-permute-start | bytes 276488 | tf_op jit(solution)/shard_map/ppermute | solution.py:583
  96.3 3.7 %collective-permute-start.30 = (bf16[40,1152]{1,0:T(8,128)(2,1)S(1)}, bf16[40,1152]{1,0:T(8,128)(2,1)S(1)}, u32[]{:S(2)}, u32[]{:S(2)}) collective-permute-start(bf16[40,1152]{1,0:T(8,128)(2,1)S(1)} %get-tuple-element.115), channel_id=1, source_target_pairs={{0,8},{1,9},{2,10},{3,11},{4,12},{5,13},{6,14},{7,15},{8,128},{9,1... | collective-permute-start | bytes 276488 | tf_op jit(solution)/shard_map/ppermute | solution.py:583
  100.1 1.4 %collective-permute-start.31 = (bf16[40,1152]{1,0:T(8,128)(2,1)S(1)}, bf16[40,1152]{1,0:T(8,128)(2,1)S(1)}, u32[]{:S(2)}, u32[]{:S(2)}) collective-permute-start(bf16[40,1152]{1,0:T(8,128)(2,1)S(1)} %get-tuple-element.116), channel_id=1, source_target_pairs={{0,140},{1,141},{2,142},{3,143},{4,0},{5,1},{6,2},{7,3},{8,4},{9,5... | collective-permute-start | bytes 276488 | tf_op jit(solution)/shard_map/ppermute | solution.py:583
  101.4 0.5 collective-permute-done.30.refs_2_
  101.9 1.6 %collective-permute-done.31.refs_3_ = bf16[40,1152]{1,0:T(8,128)(2,1)S(1)} collective-permute-done((bf16[40,1152]{1,0:T(8,128)(2,1)S(1)}, bf16[40,1152]{1,0:T(8,128)(2,1)S(1)}, u32[]{:S(2)}, u32[]{:S(2)}) %collective-permute-start.31) | collective-permute-done | bytes 92192 | tf_op jit(solution)/shard_map/ppermute | solution.py:583
  103.5 4.6 %collective-permute-start.32 = (bf16[40,1152]{1,0:T(8,128)(2,1)S(1)}, bf16[40,1152]{1,0:T(8,128)(2,1)S(1)}, u32[]{:S(2)}, u32[]{:S(2)}) collective-permute-start(bf16[40,1152]{1,0:T(8,128)(2,1)S(1)} %plain_sum.2.refs_0_), channel_id=1, source_target_pairs={{0,128},{16,144},{32,160},{48,176},{64,192},{80,208},{96,224},{112... | collective-permute-start | bytes 276488 | tf_op jit(solution)/shard_map/ppermute | solution.py:564
  108.1 3.1 %collective-permute-done.32.refs_1_ = bf16[40,1152]{1,0:T(8,128)(2,1)S(1)} collective-permute-done((bf16[40,1152]{1,0:T(8,128)(2,1)S(1)}, bf16[40,1152]{1,0:T(8,128)(2,1)S(1)}, u32[]{:S(2)}, u32[]{:S(2)}) %collective-permute-start.32) | collective-permute-done | bytes 92192 | tf_op jit(solution)/shard_map/ppermute | solution.py:564
  111.3 1.9 %collective-permute-start.35 = (bf16[40,1152]{1,0:T(8,128)(2,1)S(1)}, bf16[40,1152]{1,0:T(8,128)(2,1)S(1)}, u32[]{:S(2)}, u32[]{:S(2)}) collective-permute-start(bf16[40,1152]{1,0:T(8,128)(2,1)S(1)} %plain_sum.3.refs_0_), channel_id=1, source_target_pairs={{0,96},{16,112},{32,0},{48,16},{64,32},{80,48},{96,64},{112,80},{1... | collective-permute-start | bytes 276488 | tf_op jit(solution)/shard_map/ppermute | solution.py:568
  113.2 0.7 collective-permute-start.33
  113.9 1.8 %collective-permute-done.35.refs_3_ = bf16[40,1152]{1,0:T(8,128)(2,1)S(1)} collective-permute-done((bf16[40,1152]{1,0:T(8,128)(2,1)S(1)}, bf16[40,1152]{1,0:T(8,128)(2,1)S(1)}, u32[]{:S(2)}, u32[]{:S(2)}) %collective-permute-start.35) | collective-permute-done | bytes 92192 | tf_op jit(solution)/shard_map/ppermute | solution.py:568
  115.7 2.5 %collective-permute-done.34.refs_2_ = bf16[40,1152]{1,0:T(8,128)(2,1)S(1)} collective-permute-done((bf16[40,1152]{1,0:T(8,128)(2,1)S(1)}, bf16[40,1152]{1,0:T(8,128)(2,1)S(1)}, u32[]{:S(2)}, u32[]{:S(2)}) %collective-permute-start.34) | collective-permute-done | bytes 92192 | tf_op jit(solution)/shard_map/ppermute | solution.py:568
  118.2 0.6 collective-permute-done.33.refs_1_
  118.8 10.0 %collective-permute-start.36 = (bf16[4,40,1152]{2,1,0:T(8,128)(2,1)S(1)}, bf16[4,40,1152]{2,1,0:T(8,128)(2,1)S(1)}, u32[]{:S(2)}, u32[]{:S(2)}) collective-permute-start(bf16[4,40,1152]{2,1,0:T(8,128)(2,1)S(1)} %stack.1.mine), channel_id=1, source_target_pairs={{0,16},{16,0},{32,48},{48,32},{64,80},{80,64},{96,112},{112,96},{1... | collective-permute-start | bytes 1105928 | tf_op jit(solution)/shard_map/ppermute | solution.py:556
  128.8 1.3 collective-permute-done.36.other
  130.1 1.3 last.1
  (45 shorter events, 1.1 us)
Async XLA Ops:
  1.6 10.5 %copy-start.2 = (f32[1152,8]{0,1:T(8,128)S(1)}, f32[1152,8]{0,1:T(8,128)}, u32[]{:S(2)}) copy-start(f32[1152,8]{0,1:T(8,128)} %param.15) | copy-start | bytes 110596
  1.6 10.5 %copy-start.3 = (f32[1152]{0:T(1024)S(1)}, f32[1152]{0:T(1024)}, u32[]{:S(2)}) copy-start(f32[1152]{0:T(1024)} %ln_ref.1) | copy-start | bytes 13828
  1.6 10.5 %copy-start.4 = (f32[1152]{0:T(1024)S(1)}, f32[1152]{0:T(1024)}, u32[]{:S(2)}) copy-start(f32[1152]{0:T(1024)} %og_ref.1) | copy-start | bytes 13828
  1.6 10.5 %copy-start.5 = (f32[1,4,8]{2,1,0:T(4,128)S(1)}, f32[1,4,8]{2,1,0:T(4,128)}, u32[]{:S(2)}) copy-start(f32[1,4,8]{2,1,0:T(4,128)} %param.10) | copy-start | bytes 388
  1.6 10.5 %copy-start.6 = (s32[1,4]{1,0:T(1,128)S(1)}, s32[1,4]{1,0:T(1,128)}, u32[]{:S(2)}) copy-start(s32[1,4]{1,0:T(1,128)} %lens_ref.1) | copy-start | bytes 52
  1.6 10.9 %copy-start.1 = (bf16[1,2,64,1152]{3,2,1,0:T(8,128)(2,1)S(1)}, bf16[1,2,64,1152]{3,2,1,0:T(8,128)(2,1)}, u32[]{:S(2)}) copy-start(bf16[1,2,64,1152]{3,2,1,0:T(8,128)(2,1)} %param.8) | copy-start | bytes 884740
  1.6 16.5 %copy-start = (bf16[1152,1152]{1,0:T(8,128)(2,1)S(1)}, bf16[1152,1152]{1,0:T(8,128)(2,1)}, u32[]{:S(2)}) copy-start(bf16[1152,1152]{1,0:T(8,128)(2,1)} %refs_1_.3) | copy-start | bytes 7962628
  1.7 10.9 %collective-permute-start = (bf16[2,4,8,1152]{3,2,1,0:T(8,128)(2,1)S(1)}, bf16[2,4,8,1152]{3,2,1,0:T(8,128)(2,1)S(1)}, u32[]{:S(2)}, u32[]{:S(2)}) collective-permute-start(bf16[2,4,8,1152]{3,2,1,0:T(8,128)(2,1)S(1)} %dynamic-slice_bitcast_fusion.refs_2_), channel_id=1, source_target_pairs={{0,128},{16,144},{32,160},{48,176},{64,192},{80,208},{96,224},{112... | collective-permute-start | bytes 442376 | tf_op jit(solution)/shard_map/ppermute | solution.py:564
  12.5 7.4 %collective-permute-start.1 = (bf16[4,8,1152]{2,1,0:T(8,128)(2,1)S(1)}, bf16[4,8,1152]{2,1,0:T(8,128)(2,1)S(1)}, u32[]{:S(2)}, u32[]{:S(2)}) collective-permute-start(bf16[4,8,1152]{2,1,0:T(8,128)(2,1)S(1)} %get-tuple-element.64), channel_id=1, source_target_pairs={{0,32},{16,48},{32,64},{48,80},{64,96},{80,112},{96,0},{112,16},{1... | collective-permute-start | bytes 221192 | tf_op jit(solution)/shard_map/ppermute | solution.py:568
  14.5 5.5 %collective-permute-start.2 = (bf16[4,8,1152]{2,1,0:T(8,128)(2,1)S(1)}, bf16[4,8,1152]{2,1,0:T(8,128)(2,1)S(1)}, u32[]{:S(2)}, u32[]{:S(2)}) collective-permute-start(bf16[4,8,1152]{2,1,0:T(8,128)(2,1)S(1)} %get-tuple-element.65), channel_id=1, source_target_pairs={{0,64},{16,80},{32,96},{48,112},{64,0},{80,16},{96,32},{112,48},{1... | collective-permute-start | bytes 221192 | tf_op jit(solution)/shard_map/ppermute | solution.py:568
  17.1 4.2 %collective-permute-start.3 = (bf16[4,8,1152]{2,1,0:T(8,128)(2,1)S(1)}, bf16[4,8,1152]{2,1,0:T(8,128)(2,1)S(1)}, u32[]{:S(2)}, u32[]{:S(2)}) collective-permute-start(bf16[4,8,1152]{2,1,0:T(8,128)(2,1)S(1)} %get-tuple-element.66), channel_id=1, source_target_pairs={{0,96},{16,112},{32,0},{48,16},{64,32},{80,48},{96,64},{112,80},{1... | collective-permute-start | bytes 221192 | tf_op jit(solution)/shard_map/ppermute | solution.py:568
  21.4 3.1 %collective-permute-start.4 = (bf16[8,8,1152]{2,1,0:T(8,128)(2,1)S(1)}, bf16[8,8,1152]{2,1,0:T(8,128)(2,1)S(1)}, u32[]{:S(2)}, u32[]{:S(2)}) collective-permute-start(bf16[8,8,1152]{2,1,0:T(8,128)(2,1)S(1)} %get-tuple-element.68), channel_id=1, source_target_pairs={{0,16},{16,0},{32,48},{48,32},{64,80},{80,64},{96,112},{112,96},{1... | collective-permute-start | bytes 442376 | tf_op jit(solution)/shard_map/ppermute | solution.py:556
  28.3 1.2 collective-permute-start.5
  29.5 8.7 %collective-permute-start.6 = (f32[8,8]{1,0:T(8,128)S(1)}, f32[8,8]{1,0:T(8,128)S(1)}, u32[]{:S(2)}, u32[]{:S(2)}) collective-permute-start(f32[8,8]{1,0:T(8,128)S(1)} %pair_sum.4.a), channel_id=1, source_target_pairs={{0,128},{16,144},{32,160},{48,176},{64,192},{80,208},{96,224},{112... | collective-permute-start | bytes 776 | tf_op jit(solution)/shard_map/ppermute | solution.py:564
  38.2 2.5 %collective-permute-start.7 = (f32[8,8]{1,0:T(8,128)S(1)}, f32[8,8]{1,0:T(8,128)S(1)}, u32[]{:S(2)}, u32[]{:S(2)}) collective-permute-start(f32[8,8]{1,0:T(8,128)S(1)} %pair_sum.5.a), channel_id=1, source_target_pairs={{0,32},{16,48},{32,0},{48,16},{64,96},{80,112},{96,64},{112,80},{1... | collective-permute-start | bytes 776 | tf_op jit(solution)/shard_map/ppermute | solution.py:560
  40.7 4.4 %collective-permute-start.8 = (f32[8,8]{1,0:T(8,128)S(1)}, f32[8,8]{1,0:T(8,128)S(1)}, u32[]{:S(2)}, u32[]{:S(2)}) collective-permute-start(f32[8,8]{1,0:T(8,128)S(1)} %pair_sum.6.a), channel_id=1, source_target_pairs={{0,64},{16,80},{32,96},{48,112},{64,0},{80,16},{96,32},{112,48},{1... | collective-permute-start | bytes 776 | tf_op jit(solution)/shard_map/ppermute | solution.py:560
  42.7 8.8 %collective-permute-start.9 = (bf16[2,1152,128]{2,1,0:T(8,128)(2,1)S(1)}, bf16[2,1152,128]{2,1,0:T(8,128)(2,1)S(1)}, u32[]{:S(2)}, u32[]{:S(2)}) collective-permute-start(bf16[2,1152,128]{2,1,0:T(8,128)(2,1)S(1)} %get-tuple-element.84), channel_id=1, source_target_pairs={{0,16},{16,0},{32,48},{48,32},{64,80},{80,64},{96,112},{112,96},{1... | collective-permute-start | bytes 1769480 | tf_op jit(solution)/shard_map/ppermute | solution.py:556
  48.3 4.7 %collective-permute-start.10 = (bf16[2,128,1152]{2,1,0:T(8,128)(2,1)S(1)}, bf16[2,128,1152]{2,1,0:T(8,128)(2,1)S(1)}, u32[]{:S(2)}, u32[]{:S(2)}) collective-permute-start(bf16[2,128,1152]{2,1,0:T(8,128)(2,1)S(1)} %get-tuple-element.86), channel_id=1, source_target_pairs={{0,16},{16,0},{32,48},{48,32},{64,80},{80,64},{96,112},{112,96},{1... | collective-permute-start | bytes 1769480 | tf_op jit(solution)/shard_map/ppermute | solution.py:556
  54.8 10.3 %collective-permute-start.15 = (bf16[144,1152]{1,0:T(8,128)(2,1)S(1)}, bf16[144,1152]{1,0:T(8,128)(2,1)S(1)}, u32[]{:S(2)}, u32[]{:S(2)}) collective-permute-start(bf16[144,1152]{1,0:T(8,128)(2,1)S(1)} %get-tuple-element.91), channel_id=1, source_target_pairs={{0,1},{1,2},{2,3},{3,0},{4,5},{5,6},{6,7},{7,4},{8,9},{9,10},{10,1... | collective-permute-start | bytes 995336 | tf_op jit(solution)/shard_map/ppermute | solution.py:572
  56.1 9.9 %collective-permute-start.16 = (bf16[144,1152]{1,0:T(8,128)(2,1)S(1)}, bf16[144,1152]{1,0:T(8,128)(2,1)S(1)}, u32[]{:S(2)}, u32[]{:S(2)}) collective-permute-start(bf16[144,1152]{1,0:T(8,128)(2,1)S(1)} %get-tuple-element.92), channel_id=1, source_target_pairs={{0,32},{16,48},{32,64},{48,80},{64,96},{80,112},{96,0},{112,16},{1... | collective-permute-start | bytes 995336 | tf_op jit(solution)/shard_map/ppermute | solution.py:568
  56.2 11.2 %collective-permute-start.17 = (bf16[144,1152]{1,0:T(8,128)(2,1)S(1)}, bf16[144,1152]{1,0:T(8,128)(2,1)S(1)}, u32[]{:S(2)}, u32[]{:S(2)}) collective-permute-start(bf16[144,1152]{1,0:T(8,128)(2,1)S(1)} %get-tuple-element.93), channel_id=1, source_target_pairs={{0,3},{1,0},{2,1},{3,2},{4,7},{5,4},{6,5},{7,6},{8,11},{9,8},{10,9... | collective-permute-start | bytes 995336 | tf_op jit(solution)/shard_map/ppermute | solution.py:572
  57.7 11.4 %collective-permute-start.18 = (bf16[144,1152]{1,0:T(8,128)(2,1)S(1)}, bf16[144,1152]{1,0:T(8,128)(2,1)S(1)}, u32[]{:S(2)}, u32[]{:S(2)}) collective-permute-start(bf16[144,1152]{1,0:T(8,128)(2,1)S(1)} %get-tuple-element.94), channel_id=1, source_target_pairs={{0,96},{16,112},{32,0},{48,16},{64,32},{80,48},{96,64},{112,80},{1... | collective-permute-start | bytes 995336 | tf_op jit(solution)/shard_map/ppermute | solution.py:568
  60.2 12.0 %collective-permute-start.11 = (bf16[144,1152]{1,0:T(8,128)(2,1)S(1)}, bf16[144,1152]{1,0:T(8,128)(2,1)S(1)}, u32[]{:S(2)}, u32[]{:S(2)}) collective-permute-start(bf16[144,1152]{1,0:T(8,128)(2,1)S(1)} %get-tuple-element.87), channel_id=1, source_target_pairs={{0,1},{1,2},{2,3},{3,0},{4,5},{5,6},{6,7},{7,4},{8,9},{9,10},{10,1... | collective-permute-start | bytes 995336 | tf_op jit(solution)/shard_map/ppermute | solution.py:572
  65.1 8.5 %collective-permute-start.12 = (bf16[144,1152]{1,0:T(8,128)(2,1)S(1)}, bf16[144,1152]{1,0:T(8,128)(2,1)S(1)}, u32[]{:S(2)}, u32[]{:S(2)}) collective-permute-start(bf16[144,1152]{1,0:T(8,128)(2,1)S(1)} %get-tuple-element.88), channel_id=1, source_target_pairs={{0,32},{16,48},{32,64},{48,80},{64,96},{80,112},{96,0},{112,16},{1... | collective-permute-start | bytes 995336 | tf_op jit(solution)/shard_map/ppermute | solution.py:568
  66.0 8.9 %collective-permute-start.13 = (bf16[144,1152]{1,0:T(8,128)(2,1)S(1)}, bf16[144,1152]{1,0:T(8,128)(2,1)S(1)}, u32[]{:S(2)}, u32[]{:S(2)}) collective-permute-start(bf16[144,1152]{1,0:T(8,128)(2,1)S(1)} %get-tuple-element.89), channel_id=1, source_target_pairs={{0,3},{1,0},{2,1},{3,2},{4,7},{5,4},{6,5},{7,6},{8,11},{9,8},{10,9... | collective-permute-start | bytes 995336 | tf_op jit(solution)/shard_map/ppermute | solution.py:572
  67.5 8.7 %collective-permute-start.14 = (bf16[144,1152]{1,0:T(8,128)(2,1)S(1)}, bf16[144,1152]{1,0:T(8,128)(2,1)S(1)}, u32[]{:S(2)}, u32[]{:S(2)}) collective-permute-start(bf16[144,1152]{1,0:T(8,128)(2,1)S(1)} %get-tuple-element.90), channel_id=1, source_target_pairs={{0,96},{16,112},{32,0},{48,16},{64,32},{80,48},{96,64},{112,80},{1... | collective-permute-start | bytes 995336 | tf_op jit(solution)/shard_map/ppermute | solution.py:568
  69.4 7.7 %collective-permute-start.19 = (bf16[144,1152]{1,0:T(8,128)(2,1)S(1)}, bf16[144,1152]{1,0:T(8,128)(2,1)S(1)}, u32[]{:S(2)}, u32[]{:S(2)}) collective-permute-start(bf16[144,1152]{1,0:T(8,128)(2,1)S(1)} %get-tuple-element.99), channel_id=1, source_target_pairs={{0,1},{1,2},{2,3},{3,0},{4,5},{5,6},{6,7},{7,4},{8,9},{9,10},{10,1... | collective-permute-start | bytes 995336 | tf_op jit(solution)/shard_map/ppermute | solution.py:572
  72.2 9.2 %collective-permute-start.20 = (bf16[144,1152]{1,0:T(8,128)(2,1)S(1)}, bf16[144,1152]{1,0:T(8,128)(2,1)S(1)}, u32[]{:S(2)}, u32[]{:S(2)}) collective-permute-start(bf16[144,1152]{1,0:T(8,128)(2,1)S(1)} %get-tuple-element.100), channel_id=1, source_target_pairs={{0,32},{16,48},{32,64},{48,80},{64,96},{80,112},{96,0},{112,16},{1... | collective-permute-start | bytes 995336 | tf_op jit(solution)/shard_map/ppermute | solution.py:568
  73.6 7.8 %collective-permute-start.21 = (bf16[144,1152]{1,0:T(8,128)(2,1)S(1)}, bf16[144,1152]{1,0:T(8,128)(2,1)S(1)}, u32[]{:S(2)}, u32[]{:S(2)}) collective-permute-start(bf16[144,1152]{1,0:T(8,128)(2,1)S(1)} %get-tuple-element.101), channel_id=1, source_target_pairs={{0,3},{1,0},{2,1},{3,2},{4,7},{5,4},{6,5},{7,6},{8,11},{9,8},{10,9... | collective-permute-start | bytes 995336 | tf_op jit(solution)/shard_map/ppermute | solution.py:572
  74.9 6.5 %collective-permute-start.22 = (bf16[144,1152]{1,0:T(8,128)(2,1)S(1)}, bf16[144,1152]{1,0:T(8,128)(2,1)S(1)}, u32[]{:S(2)}, u32[]{:S(2)}) collective-permute-start(bf16[144,1152]{1,0:T(8,128)(2,1)S(1)} %get-tuple-element.102), channel_id=1, source_target_pairs={{0,96},{16,112},{32,0},{48,16},{64,32},{80,48},{96,64},{112,80},{1... | collective-permute-start | bytes 995336 | tf_op jit(solution)/shard_map/ppermute | solution.py:568
  81.9 5.8 %collective-permute-start.23 = (bf16[72,1152]{1,0:T(8,128)(2,1)S(1)}, bf16[72,1152]{1,0:T(8,128)(2,1)S(1)}, u32[]{:S(2)}, u32[]{:S(2)}) collective-permute-start(bf16[72,1152]{1,0:T(8,128)(2,1)S(1)} %get-tuple-element.107), channel_id=1, source_target_pairs={{0,32},{16,48},{32,64},{48,80},{64,96},{80,112},{96,0},{112,16},{1... | collective-permute-start | bytes 497672 | tf_op jit(solution)/shard_map/ppermute | solution.py:568
  82.7 5.7 %collective-permute-start.24 = (bf16[72,1152]{1,0:T(8,128)(2,1)S(1)}, bf16[72,1152]{1,0:T(8,128)(2,1)S(1)}, u32[]{:S(2)}, u32[]{:S(2)}) collective-permute-start(bf16[72,1152]{1,0:T(8,128)(2,1)S(1)} %get-tuple-element.108), channel_id=1, source_target_pairs={{0,1},{1,2},{2,3},{3,0},{4,5},{5,6},{6,7},{7,4},{8,9},{9,10},{10,1... | collective-permute-start | bytes 497672 | tf_op jit(solution)/shard_map/ppermute | solution.py:572
  82.9 5.5 %collective-permute-start.25 = (bf16[72,1152]{1,0:T(8,128)(2,1)S(1)}, bf16[72,1152]{1,0:T(8,128)(2,1)S(1)}, u32[]{:S(2)}, u32[]{:S(2)}) collective-permute-start(bf16[72,1152]{1,0:T(8,128)(2,1)S(1)} %get-tuple-element.109), channel_id=1, source_target_pairs={{0,96},{16,112},{32,0},{48,16},{64,32},{80,48},{96,64},{112,80},{1... | collective-permute-start | bytes 497672 | tf_op jit(solution)/shard_map/ppermute | solution.py:568
  84.6 6.7 %collective-permute-start.26 = (bf16[72,1152]{1,0:T(8,128)(2,1)S(1)}, bf16[72,1152]{1,0:T(8,128)(2,1)S(1)}, u32[]{:S(2)}, u32[]{:S(2)}) collective-permute-start(bf16[72,1152]{1,0:T(8,128)(2,1)S(1)} %get-tuple-element.110), channel_id=1, source_target_pairs={{0,3},{1,0},{2,1},{3,2},{4,7},{5,4},{6,5},{7,6},{8,11},{9,8},{10,9... | collective-permute-start | bytes 497672 | tf_op jit(solution)/shard_map/ppermute | solution.py:572
  87.3 6.3 %collective-permute-start.27 = (bf16[72,1152]{1,0:T(8,128)(2,1)S(1)}, bf16[72,1152]{1,0:T(8,128)(2,1)S(1)}, u32[]{:S(2)}, u32[]{:S(2)}) collective-permute-start(bf16[72,1152]{1,0:T(8,128)(2,1)S(1)} %get-tuple-element.111), channel_id=1, source_target_pairs={{0,2},{1,3},{2,0},{3,1},{4,6},{5,7},{6,4},{7,5},{8,10},{9,11},{10,... | collective-permute-start | bytes 497672 | tf_op jit(solution)/shard_map/ppermute | solution.py:572
  87.7 6.6 %collective-permute-start.28 = (bf16[72,1152]{1,0:T(8,128)(2,1)S(1)}, bf16[72,1152]{1,0:T(8,128)(2,1)S(1)}, u32[]{:S(2)}, u32[]{:S(2)}) collective-permute-start(bf16[72,1152]{1,0:T(8,128)(2,1)S(1)} %get-tuple-element.112), channel_id=1, source_target_pairs={{0,64},{16,80},{32,96},{48,112},{64,0},{80,16},{96,32},{112,48},{1... | collective-permute-start | bytes 497672 | tf_op jit(solution)/shard_map/ppermute | solution.py:568
  94.5 6.9 %collective-permute-start.29 = (bf16[40,1152]{1,0:T(8,128)(2,1)S(1)}, bf16[40,1152]{1,0:T(8,128)(2,1)S(1)}, u32[]{:S(2)}, u32[]{:S(2)}) collective-permute-start(bf16[40,1152]{1,0:T(8,128)(2,1)S(1)} %get-tuple-element.114), channel_id=1, source_target_pairs={{0,4},{1,5},{2,6},{3,7},{4,8},{5,9},{6,10},{7,11},{8,12},{9,13},{1... | collective-permute-start | bytes 276488 | tf_op jit(solution)/shard_map/ppermute | solution.py:583
  96.3 5.6 %collective-permute-start.30 = (bf16[40,1152]{1,0:T(8,128)(2,1)S(1)}, bf16[40,1152]{1,0:T(8,128)(2,1)S(1)}, u32[]{:S(2)}, u32[]{:S(2)}) collective-permute-start(bf16[40,1152]{1,0:T(8,128)(2,1)S(1)} %get-tuple-element.115), channel_id=1, source_target_pairs={{0,8},{1,9},{2,10},{3,11},{4,12},{5,13},{6,14},{7,15},{8,128},{9,1... | collective-permute-start | bytes 276488 | tf_op jit(solution)/shard_map/ppermute | solution.py:583
  100.1 3.4 %collective-permute-start.31 = (bf16[40,1152]{1,0:T(8,128)(2,1)S(1)}, bf16[40,1152]{1,0:T(8,128)(2,1)S(1)}, u32[]{:S(2)}, u32[]{:S(2)}) collective-permute-start(bf16[40,1152]{1,0:T(8,128)(2,1)S(1)} %get-tuple-element.116), channel_id=1, source_target_pairs={{0,140},{1,141},{2,142},{3,143},{4,0},{5,1},{6,2},{7,3},{8,4},{9,5... | collective-permute-start | bytes 276488 | tf_op jit(solution)/shard_map/ppermute | solution.py:583
  103.5 7.7 %collective-permute-start.32 = (bf16[40,1152]{1,0:T(8,128)(2,1)S(1)}, bf16[40,1152]{1,0:T(8,128)(2,1)S(1)}, u32[]{:S(2)}, u32[]{:S(2)}) collective-permute-start(bf16[40,1152]{1,0:T(8,128)(2,1)S(1)} %plain_sum.2.refs_0_), channel_id=1, source_target_pairs={{0,128},{16,144},{32,160},{48,176},{64,192},{80,208},{96,224},{112... | collective-permute-start | bytes 276488 | tf_op jit(solution)/shard_map/ppermute | solution.py:564
  111.3 4.4 %collective-permute-start.35 = (bf16[40,1152]{1,0:T(8,128)(2,1)S(1)}, bf16[40,1152]{1,0:T(8,128)(2,1)S(1)}, u32[]{:S(2)}, u32[]{:S(2)}) collective-permute-start(bf16[40,1152]{1,0:T(8,128)(2,1)S(1)} %plain_sum.3.refs_0_), channel_id=1, source_target_pairs={{0,96},{16,112},{32,0},{48,16},{64,32},{80,48},{96,64},{112,80},{1... | collective-permute-start | bytes 276488 | tf_op jit(solution)/shard_map/ppermute | solution.py:568
  113.2 5.0 %collective-permute-start.34 = (bf16[40,1152]{1,0:T(8,128)(2,1)S(1)}, bf16[40,1152]{1,0:T(8,128)(2,1)S(1)}, u32[]{:S(2)}, u32[]{:S(2)}) collective-permute-start(bf16[40,1152]{1,0:T(8,128)(2,1)S(1)} %plain_sum.3.refs_0_), channel_id=1, source_target_pairs={{0,64},{16,80},{32,96},{48,112},{64,0},{80,16},{96,32},{112,48},{1... | collective-permute-start | bytes 276488 | tf_op jit(solution)/shard_map/ppermute | solution.py:568
  113.2 5.6 %collective-permute-start.33 = (bf16[40,1152]{1,0:T(8,128)(2,1)S(1)}, bf16[40,1152]{1,0:T(8,128)(2,1)S(1)}, u32[]{:S(2)}, u32[]{:S(2)}) collective-permute-start(bf16[40,1152]{1,0:T(8,128)(2,1)S(1)} %plain_sum.3.refs_0_), channel_id=1, source_target_pairs={{0,32},{16,48},{32,64},{48,80},{64,96},{80,112},{96,0},{112,16},{1... | collective-permute-start | bytes 276488 | tf_op jit(solution)/shard_map/ppermute | solution.py:568
  118.8 11.3 %collective-permute-start.36 = (bf16[4,40,1152]{2,1,0:T(8,128)(2,1)S(1)}, bf16[4,40,1152]{2,1,0:T(8,128)(2,1)S(1)}, u32[]{:S(2)}, u32[]{:S(2)}) collective-permute-start(bf16[4,40,1152]{2,1,0:T(8,128)(2,1)S(1)} %stack.1.mine), channel_id=1, source_target_pairs={{0,16},{16,0},{32,48},{48,32},{64,80},{80,64},{96,112},{112,96},{1... | collective-permute-start | bytes 1105928 | tf_op jit(solution)/shard_map/ppermute | solution.py:556
